TPU v7x, 32 devices: a whole 2x2x4 slice. The times are simulated.
32 devices in a mesh: fsdp: 4 (over y, x), context: 4 (over z), tensor: 2 (over core).
Axes of the slice: x: 2, y: 2, z: 4, core: 2. Of those that a mesh axis runs over, the one named last changes fastest.
Arguments:
- tokens: bfloat16 [4, 2560, 768], P('fsdp', 'context'), may hold values from -6 to 6
- attn_gain: bfloat16 [768], P('fsdp'), may hold values from 0.5 to 1.5
- w_qkv: bfloat16 [768, 3, 768], P('fsdp', None, 'tensor'), may hold values from -0.21875 to 0.21875
- w_out: bfloat16 [768, 768], P('tensor', 'fsdp'), may hold values from -0.875 to 0.875
- ffn_gain: bfloat16 [768], P('fsdp'), may hold values from 0.5 to 1.5
- w_gu: bfloat16 [768, 2, 2048], P('fsdp', None, 'tensor'), may hold values from -0.21875 to 0.21875
- w_dn: bfloat16 [2048, 768], P('tensor', 'fsdp'), may hold values from -0.125 to 0.125
- w_egu: bfloat16 [8, 768, 2, 2048], P('fsdp', None, None, 'tensor'), may hold values from -0.21875 to 0.21875
- w_edn: bfloat16 [8, 2048, 768], P('fsdp', 'tensor'), may hold values from -0.125 to 0.125
- adapters: bfloat16 [8, 233472], P('fsdp', ('context', 'tensor')), may hold values from -0.29882812 to 0.29882812
- adapter_ids: int32 [4], P('fsdp'), may hold values from 0 to 7
- parents: int32 [4, 13], P('fsdp'), may hold values from 0 to 4, as said below
- seg_lengths: int32 [4, 13], P('fsdp'), may hold values from 64 to 1024, as said below
- routes: int32 [4, 2560, 2], P('fsdp', 'context'), may hold values from 0 to 7, as said below
- route_weights: bfloat16 [4, 2560, 2], P('fsdp', 'context'), may hold values from 0.25 to 0.75
- cotangent: bfloat16 [4, 2560, 768], P('fsdp', 'context'), may hold values from -6 to 6
Outputs:
- block_out: float32 [4, 2560, 768], P('fsdp', 'context')
- input_grad: float32 [4, 2560, 768], P('fsdp', 'context')
- adapter_grads: float32 [8, 233472], P('fsdp', ('context', 'tensor'))
Inputs may be any that keep to these rules, and one draw needn't show every extreme that they name: Segment 0 is the root with parent 0; segments 1 to 4 have parent 0; segments 5 to 12 have parents among 1 to 4, two each. `seg_lengths`: segment 0 has 1024 tokens; every other segment has 64 to 192; a tree's lengths sum to 2560. `routes`: a token's two experts differ; among the rows that one device holds (640 rows of each of its 1 trees) no expert is named more than 320 times, and one expert is named exactly 320 times.
All inputs are finite; a program needn't handle non-finite values.
Results may differ from a plain program's by a relative error of at most 0.02.
The roundings to bfloat16 on the way count: a program that leaves them out, or rounds other values in their place, can miss the bound.
Values may be sent and summed in bfloat16 or wider, within the bound.
A program may use at most 320 MiB of HBM per device.

v0:
```python
import jax
import jax.numpy as jnp
from jax import lax
from jax.sharding import PartitionSpec as P

D = 768
HEADS = 12
HEAD_DIM = 64
FF = 2048
EXPERTS = 8
TOPK = 2
RANK = 16
ADAPTERS = 8
PARAMS = 233472


epsilon = 1e-06
adapter_scale = 2.0
rope_base = 10000.0
masked_score = -1e30
highest_precision = lax.Precision.HIGHEST


def unpack(flat_params):
    leading = flat_params.shape[:-1]
    block_shapes = [
        (D, 3 * RANK),
        (3, RANK, D),
        (D, RANK),
        (RANK, D),
        (D, 2 * RANK),
        (2, RANK, FF),
        (FF, RANK),
        (RANK, D),
    ]
    pieces = []
    offset = 0
    for block_shape in block_shapes:
        extent = 1
        for factor in block_shape:
            extent = extent * factor
        pieces.append(flat_params[..., offset : offset + extent].reshape(leading + block_shape))
        offset = offset + extent
    return pieces


def silu_of(values):
    return values * jax.nn.sigmoid(values)


def rms_scale(values):
    return lax.rsqrt(jnp.mean(values * values, axis=-1, keepdims=True) + epsilon)


def norm_back(values, scaling, gain_values, gradient):
    weighted = gradient * gain_values
    inner_mean = jnp.mean(values * weighted, axis=-1, keepdims=True)
    return scaling * weighted - values * (scaling * scaling * scaling) * inner_mean


def rotate(values, cosine, sinus):
    half_dim = values.shape[-1] // 2
    front_half = values[..., :half_dim]
    back_half = values[..., half_dim:]
    return jnp.concatenate(
        [front_half * cosine - back_half * sinus, back_half * cosine + front_half * sinus], axis=-1
    )


def unrotate(gradient, cosine, sinus):
    half_dim = gradient.shape[-1] // 2
    front_half = gradient[..., :half_dim]
    back_half = gradient[..., half_dim:]
    return jnp.concatenate(
        [front_half * cosine + back_half * sinus, back_half * cosine - front_half * sinus], axis=-1
    )


def angles(positions):
    half_dim = HEAD_DIM // 2
    frequency = rope_base ** (-(jnp.arange(half_dim, dtype=jnp.float32) * 2.0) / HEAD_DIM)
    turned = positions.astype(jnp.float32)[..., None] * frequency
    return (jnp.cos(turned)[..., None, :], jnp.sin(turned)[..., None, :])


def tree_layout(lengths, parent_ids):
    seg_count = lengths.shape[0]
    seg_ids = jnp.arange(seg_count, dtype=jnp.int32)
    parent_hot = (parent_ids[:, None] == seg_ids[None, :]).astype(jnp.int32)
    grand_hot = jnp.dot(parent_hot, parent_hot)
    same_seg = (seg_ids[:, None] == seg_ids[None, :]).astype(jnp.int32)
    ancestry = (same_seg + parent_hot + grand_hot > 0).astype(jnp.int32)
    starts = jnp.cumsum(lengths) - lengths
    offsets = jnp.sum((ancestry - same_seg) * lengths[None, :], axis=1)
    return (ancestry, starts, offsets)


def locate(row_ids, starts, offsets):
    segment = jnp.sum((row_ids[:, None] >= starts[None, :]).astype(jnp.int32), axis=1) - 1
    seg_hot = (segment[:, None] == jnp.arange(starts.shape[0], dtype=jnp.int32)[None, :]).astype(
        jnp.int32
    )
    positions = (
        row_ids
        - jnp.sum(seg_hot * starts[None, :], axis=1)
        + jnp.sum(seg_hot * offsets[None, :], axis=1)
    )
    return (seg_hot, positions)


def expert_forward(inputs, gate_weights, down_weights):
    pre = jnp.einsum("secd,edjf->secjf", inputs, gate_weights, preferred_element_type=jnp.float32)
    active = (silu_of(pre[..., 0, :]) * pre[..., 1, :]).astype(jnp.bfloat16)
    return jnp.einsum("secf,efd->secd", active, down_weights, preferred_element_type=jnp.float32)


def expert_backward(inputs, out_grads, gate_values, gate_weights, down_weights):
    pre = jnp.einsum("secd,edjf->secjf", inputs, gate_weights, preferred_element_type=jnp.float32)
    gate_pre = pre[..., 0, :]
    up_pre = pre[..., 1, :]
    grad_active = jnp.einsum(
        "secd,efd->secf", out_grads, down_weights, preferred_element_type=jnp.float32
    )
    grad_active = grad_active * gate_values.astype(jnp.float32)[..., None]
    sigmoid_gate = jax.nn.sigmoid(gate_pre)
    grad_gate = grad_active * up_pre * sigmoid_gate * (1.0 + gate_pre * (1.0 - sigmoid_gate))
    grad_up = grad_active * gate_pre * sigmoid_gate
    grad_pre = jnp.stack([grad_gate, grad_up], axis=-2).astype(jnp.bfloat16)
    return jnp.einsum(
        "secjf,edjf->secd", grad_pre, gate_weights, preferred_element_type=jnp.float32
    )


def shards(
    tokens,
    attn_gain,
    w_qkv,
    w_out,
    ffn_gain,
    w_gu,
    w_dn,
    w_egu,
    w_edn,
    adapters,
    adapter_ids,
    parents,
    seg_lengths,
    routes,
    route_weights,
    cotangent,
):
    tree_count = tokens.shape[0]
    row_count = tokens.shape[1]
    contexts = lax.axis_size("context")
    tensors = lax.axis_size("tensor")
    fsdp_size = lax.axis_size("fsdp")
    tree_len = row_count * contexts
    token_count = tree_count * row_count
    local_heads = HEADS // tensors
    local_width = local_heads * HEAD_DIM
    local_ff = FF // tensors
    part_index = lax.axis_index("tensor")
    row_start = lax.axis_index("context") * row_count
    width_start = part_index * local_width
    ff_start = part_index * local_ff
    head_shape = (tree_count, row_count, local_heads, HEAD_DIM)
    wide_shape = (tree_count, tree_len, local_heads, HEAD_DIM)
    adapter_cols = lax.all_gather(adapters, ("context", "tensor"), axis=1, tiled=True)
    qkv_weight, output_matrix, gu_weight, down_matrix, gain_one, gain_two, adapter_all = (
        lax.all_gather(w_qkv, "fsdp", axis=0, tiled=True),
        lax.all_gather(w_out, "fsdp", axis=1, tiled=True),
        lax.all_gather(w_gu, "fsdp", axis=0, tiled=True),
        lax.all_gather(w_dn, "fsdp", axis=1, tiled=True),
        lax.all_gather(attn_gain, "fsdp", axis=0, tiled=True),
        lax.all_gather(ffn_gain, "fsdp", axis=0, tiled=True),
        lax.all_gather(adapter_cols, "fsdp", axis=0, tiled=True),
    )
    id_hot = (adapter_ids[:, None] == jnp.arange(ADAPTERS, dtype=jnp.int32)[None, :]).astype(
        jnp.bfloat16
    )
    chosen = jnp.dot(id_hot, adapter_all, preferred_element_type=jnp.float32)
    (
        a_qkv,
        query_key_value_adapter_up,
        a_out,
        output_adapter_up,
        a_gu,
        gate_up_adapter_up,
        a_dn,
        down_adapter_up,
    ) = unpack(chosen)
    b_qkv_part = lax.dynamic_slice_in_dim(query_key_value_adapter_up, width_start, local_width, 3)
    a_out_part = lax.dynamic_slice_in_dim(a_out, width_start, local_width, 1)
    b_gu_part = lax.dynamic_slice_in_dim(gate_up_adapter_up, ff_start, local_ff, 3)
    down_adapter_slice = lax.dynamic_slice_in_dim(a_dn, ff_start, local_ff, 1)
    ancestry, starts, offsets = jax.vmap(tree_layout)(seg_lengths, parents)
    ancestry_f = ancestry.astype(jnp.float32)
    key_ids = jnp.arange(tree_len, dtype=jnp.int32)
    query_ids = row_start + jnp.arange(row_count, dtype=jnp.int32)
    key_hot, key_positions = jax.vmap(locate, in_axes=(None, 0, 0))(key_ids, starts, offsets)
    key_hot = key_hot.astype(jnp.float32)
    query_hot = lax.dynamic_slice_in_dim(key_hot, row_start, row_count, 1)
    positions = lax.dynamic_slice_in_dim(key_positions, row_start, row_count, 1)
    reach = (jnp.einsum("trs,tsu->tru", query_hot, ancestry_f) > 0.5).astype(jnp.float32)
    visible = (jnp.einsum("tru,tku->trk", reach, key_hot) > 0.5) & (
        key_ids[None, None, :] <= query_ids[None, :, None]
    )
    cosine, sinus = angles(positions)
    tokens_f = tokens.astype(jnp.float32)
    scale_one = rms_scale(tokens_f)
    normed_one = (tokens_f * scale_one * gain_one.astype(jnp.float32)).astype(jnp.bfloat16)
    query_key_value_rank = jnp.einsum(
        "trd,tdm->trm", normed_one, a_qkv.astype(jnp.bfloat16), preferred_element_type=jnp.float32
    )
    rank_split = query_key_value_rank.reshape(tree_count, row_count, 3, RANK)
    projected_rows = jnp.einsum(
        "trd,djc->trjc", normed_one, qkv_weight, preferred_element_type=jnp.float32
    )
    projected_rows = projected_rows + adapter_scale * jnp.einsum(
        "trjk,tjkc->trjc", rank_split, b_qkv_part, precision=highest_precision
    )
    queries = rotate(projected_rows[:, :, 0].reshape(head_shape), cosine, sinus).astype(
        jnp.bfloat16
    )
    key_rows = (
        rotate(projected_rows[:, :, 1].reshape(head_shape), cosine, sinus)
        .astype(jnp.bfloat16)
        .reshape(tree_count, row_count, local_width)
    )
    value_rows = projected_rows[:, :, 2].astype(jnp.bfloat16)
    key_all, value_all = (
        lax.all_gather(key_rows, "context", axis=1, tiled=True),
        lax.all_gather(value_rows, "context", axis=1, tiled=True),
    )
    key_heads = key_all.reshape(wide_shape)
    value_heads = value_all.reshape(wide_shape)

    def attend(inputs):
        query_rows, key_block, value_block, visible_rows = inputs
        scores = (
            jnp.einsum("rhd,khd->hrk", query_rows, key_block, preferred_element_type=jnp.float32)
            * 0.125
        )
        scores = jnp.where(visible_rows[None], scores, masked_score)
        row_max = jnp.max(scores, axis=-1, keepdims=True)
        weights = jnp.exp(scores - row_max)
        totals = jnp.sum(weights, axis=-1, keepdims=True)
        probabilities = (weights / totals).astype(jnp.bfloat16)
        mixed_block = jnp.einsum(
            "hrk,khd->rhd", probabilities, value_block, preferred_element_type=jnp.float32
        )
        return (mixed_block.astype(jnp.bfloat16), (row_max + jnp.log(totals))[..., 0])

    mixed_heads, log_totals = lax.map(attend, (queries, key_heads, value_heads, visible))
    mixed_row_values = mixed_heads.reshape(tree_count, row_count, local_width)
    output_rank_rows = jnp.einsum(
        "trc,tck->trk",
        mixed_row_values,
        a_out_part.astype(jnp.bfloat16),
        preferred_element_type=jnp.float32,
    )
    attention_slice = jnp.einsum(
        "trc,cd->trd", mixed_row_values, output_matrix, preferred_element_type=jnp.float32
    )
    attention_slice = attention_slice + adapter_scale * jnp.einsum(
        "trk,tkd->trd", output_rank_rows, output_adapter_up, precision=highest_precision
    )
    attn_total = lax.psum(attention_slice, "tensor")
    residual = tokens_f + attn_total
    scale_two = rms_scale(residual)
    normed_two = (residual * scale_two * gain_two.astype(jnp.float32)).astype(jnp.bfloat16)
    gate_up_rank_rows = jnp.einsum(
        "trd,tdm->trm", normed_two, a_gu.astype(jnp.bfloat16), preferred_element_type=jnp.float32
    ).reshape(tree_count, row_count, 2, RANK)
    gate_up_matrix = jnp.einsum(
        "trd,djf->trjf", normed_two, gu_weight, preferred_element_type=jnp.float32
    )
    gate_up_matrix = gate_up_matrix + adapter_scale * jnp.einsum(
        "trjk,tjkf->trjf", gate_up_rank_rows, b_gu_part, precision=highest_precision
    )
    gate_pre = gate_up_matrix[:, :, 0]
    up_pre = gate_up_matrix[:, :, 1]
    hidden_state = (silu_of(gate_pre) * up_pre).astype(jnp.bfloat16)
    down_rank_rows = jnp.einsum(
        "xbw,xwz->xbz",
        hidden_state,
        down_adapter_slice.astype(jnp.bfloat16),
        preferred_element_type=jnp.float32,
    )
    shared_slice = jnp.einsum(
        "wmg,gh->wmh", hidden_state, down_matrix, preferred_element_type=jnp.float32
    )
    shared_slice = shared_slice + adapter_scale * jnp.einsum(
        "trk,tkd->trd", down_rank_rows, down_adapter_up, precision=highest_precision
    )
    capacity = 4 * token_count // EXPERTS
    flat_routes = routes.reshape(token_count * TOPK)
    route_hot = (flat_routes[:, None] == jnp.arange(EXPERTS, dtype=jnp.int32)[None, :]).astype(
        jnp.int32
    )
    slot_place = jnp.sum((jnp.cumsum(route_hot, axis=0) - route_hot) * route_hot, axis=1)
    slot_index = flat_routes * capacity + slot_place
    slot_owner = (
        jnp.full((EXPERTS * capacity,), token_count, jnp.int32)
        .at[slot_index]
        .set(jnp.arange(token_count * TOPK, dtype=jnp.int32) // TOPK)
    )
    gate_grid = (
        jnp.zeros((EXPERTS * capacity,), jnp.bfloat16)
        .at[slot_index]
        .set(route_weights.reshape(token_count * TOPK))
        .reshape(EXPERTS, capacity)
    )
    padded_rows = jnp.concatenate(
        [normed_two.reshape(token_count, D), jnp.zeros((1, D), jnp.bfloat16)], axis=0
    )
    dispatched = padded_rows[slot_owner].reshape(EXPERTS, capacity, D)
    egu_all, edn_all = (
        lax.all_gather(w_egu, "fsdp", axis=0, tiled=True),
        lax.all_gather(w_edn, "fsdp", axis=0, tiled=True),
    )
    expert_out = expert_forward(dispatched[None], egu_all, edn_all)[0]
    picked = expert_out.reshape(EXPERTS * capacity, D)[slot_index].reshape(token_count, TOPK, D)
    moe_part = jnp.sum(
        picked * route_weights.astype(jnp.float32).reshape(token_count, TOPK, 1), axis=1
    )
    ffn_total = lax.psum(
        (shared_slice + moe_part.reshape(tree_count, row_count, D)).astype(jnp.bfloat16), "tensor"
    ).astype(jnp.float32)
    block_out = residual + ffn_total
    output_gradient = cotangent.astype(jnp.float32)
    grad_hidden = jnp.einsum(
        "boz,kz->bok", cotangent, down_matrix, preferred_element_type=jnp.float32
    )
    down_rank_gradient = adapter_scale * jnp.einsum(
        "trd,tkd->trk",
        cotangent,
        down_adapter_up.astype(jnp.bfloat16),
        preferred_element_type=jnp.float32,
    )
    grad_hidden = grad_hidden + jnp.einsum(
        "jax,jnx->jan", down_rank_gradient, down_adapter_slice, precision=highest_precision
    )
    sigmoid_gate = jax.nn.sigmoid(gate_pre)
    grad_gate = grad_hidden * up_pre * sigmoid_gate * (1.0 + gate_pre * (1.0 - sigmoid_gate))
    grad_up = grad_hidden * gate_pre * sigmoid_gate
    grad_gu = jnp.stack([grad_gate, grad_up], axis=2).astype(jnp.bfloat16)
    grad_normed_two = jnp.einsum(
        "trjf,djf->trd", grad_gu, gu_weight, preferred_element_type=jnp.float32
    )
    gate_up_rank_gradient = adapter_scale * jnp.einsum(
        "trjf,tjkf->trjk",
        grad_gu,
        b_gu_part.astype(jnp.bfloat16),
        preferred_element_type=jnp.float32,
    )
    rank_gu_flat = gate_up_rank_gradient.reshape(tree_count, row_count, 2 * RANK)
    grad_normed_two = grad_normed_two + jnp.einsum(
        "trm,tdm->trd", rank_gu_flat, a_gu, precision=highest_precision
    )
    padded_grads = jnp.concatenate(
        [cotangent.reshape(token_count, D), jnp.zeros((1, D), jnp.bfloat16)], axis=0
    )
    grad_slots = padded_grads[slot_owner].reshape(EXPERTS, capacity, D)
    expert_grad = expert_backward(
        dispatched[None], grad_slots[None], gate_grid[None], egu_all, edn_all
    )[0]
    moe_grad = jnp.sum(
        expert_grad.reshape(EXPERTS * capacity, D)[slot_index].reshape(token_count, TOPK, D), axis=1
    )
    grad_normed_two = grad_normed_two + moe_grad.reshape(tree_count, row_count, D)
    grad_normed_two = lax.psum(grad_normed_two, "tensor")
    grad_residual = output_gradient + norm_back(
        residual, scale_two, gain_two.astype(jnp.float32), grad_normed_two
    )
    grad_attn = grad_residual.astype(jnp.bfloat16)
    grad_mixed = jnp.einsum(
        "trd,cd->trc", grad_attn, output_matrix, preferred_element_type=jnp.float32
    )
    output_rank_gradient = adapter_scale * jnp.einsum(
        "trd,tkd->trk",
        grad_attn,
        output_adapter_up.astype(jnp.bfloat16),
        preferred_element_type=jnp.float32,
    )
    grad_mixed = grad_mixed + jnp.einsum(
        "trk,tck->trc", output_rank_gradient, a_out_part, precision=highest_precision
    )
    grad_mixed_heads = grad_mixed.astype(jnp.bfloat16).reshape(head_shape)

    def attend_back(inputs):
        query_rows, key_block, value_block, visible_rows, log_total, grad_rows = inputs
        scores = (
            jnp.einsum("rhd,khd->hrk", query_rows, key_block, preferred_element_type=jnp.float32)
            * 0.125
        )
        scores = jnp.where(visible_rows[None], scores, masked_score)
        probabilities = jnp.exp(scores - log_total[..., None])
        grad_values = jnp.einsum(
            "hrk,rhd->khd",
            probabilities.astype(jnp.bfloat16),
            grad_rows,
            preferred_element_type=jnp.float32,
        )
        grad_probs = jnp.einsum(
            "rhd,khd->hrk", grad_rows, value_block, preferred_element_type=jnp.float32
        )
        inner_sum = jnp.sum(probabilities * grad_probs, axis=-1, keepdims=True)
        grad_scores = (probabilities * (grad_probs - inner_sum)).astype(jnp.bfloat16)
        grad_query = (
            jnp.einsum("hrk,khd->rhd", grad_scores, key_block, preferred_element_type=jnp.float32)
            * 0.125
        )
        grad_keys = (
            jnp.einsum("hrk,rhd->khd", grad_scores, query_rows, preferred_element_type=jnp.float32)
            * 0.125
        )
        span = key_block.shape[0]
        return (
            grad_query,
            jnp.concatenate([grad_keys.reshape(span, -1), grad_values.reshape(span, -1)], axis=1),
        )

    grad_query_rot, grad_key_value = lax.map(
        attend_back, (queries, key_heads, value_heads, visible, log_totals, grad_mixed_heads)
    )
    own_grads = lax.psum_scatter(
        grad_key_value.astype(jnp.bfloat16), "context", scatter_dimension=1, tiled=True
    ).astype(jnp.float32)
    grad_query = unrotate(grad_query_rot, cosine, sinus).reshape(tree_count, row_count, local_width)
    grad_key = unrotate(own_grads[..., :local_width].reshape(head_shape), cosine, sinus).reshape(
        tree_count, row_count, local_width
    )
    grad_qkv = jnp.stack([grad_query, grad_key, own_grads[..., local_width:]], axis=2).astype(
        jnp.bfloat16
    )
    grad_normed_one = jnp.einsum(
        "trjc,djc->trd", grad_qkv, qkv_weight, preferred_element_type=jnp.float32
    )
    query_key_value_rank_gradient = adapter_scale * jnp.einsum(
        "trjc,tjkc->trjk",
        grad_qkv,
        b_qkv_part.astype(jnp.bfloat16),
        preferred_element_type=jnp.float32,
    )
    rank_qkv_flat = query_key_value_rank_gradient.reshape(tree_count, row_count, 3 * RANK)
    grad_normed_one = grad_normed_one + jnp.einsum(
        "trm,tdm->trd", rank_qkv_flat, a_qkv, precision=highest_precision
    )
    grad_normed_one = lax.psum(grad_normed_one.astype(jnp.bfloat16), "tensor").astype(jnp.float32)
    input_grad = grad_residual + norm_back(
        tokens_f, scale_one, gain_one.astype(jnp.float32), grad_normed_one
    )
    grad_qkv_f = grad_qkv.astype(jnp.float32)
    grad_gu_f = grad_gu.astype(jnp.float32)
    grad_a_qkv = jnp.einsum(
        "trd,trm->tdm", normed_one.astype(jnp.float32), rank_qkv_flat, precision=highest_precision
    )
    query_key_value_gradient_slice = adapter_scale * jnp.einsum(
        "trjk,trjc->tjkc", rank_split, grad_qkv_f, precision=highest_precision
    )
    grad_b_qkv = lax.dynamic_update_slice_in_dim(
        jnp.zeros((tree_count, 3, RANK, D), jnp.float32),
        query_key_value_gradient_slice,
        width_start,
        3,
    )
    grad_a_out_part = jnp.einsum(
        "trc,trk->tck",
        mixed_row_values.astype(jnp.float32),
        output_rank_gradient,
        precision=highest_precision,
    )
    grad_a_out = lax.dynamic_update_slice_in_dim(
        jnp.zeros((tree_count, D, RANK), jnp.float32), grad_a_out_part, width_start, 1
    )
    output_adapter_up_gradient = adapter_scale * jnp.einsum(
        "ags,agh->ash", output_rank_rows, grad_attn.astype(jnp.float32), precision=highest_precision
    )
    grad_a_gu = jnp.einsum(
        "trd,trm->tdm", normed_two.astype(jnp.float32), rank_gu_flat, precision=highest_precision
    )
    gate_up_adapter_gradient_slice = adapter_scale * jnp.einsum(
        "trjk,trjf->tjkf", gate_up_rank_rows, grad_gu_f, precision=highest_precision
    )
    grad_b_gu = lax.dynamic_update_slice_in_dim(
        jnp.zeros((tree_count, 2, RANK, FF), jnp.float32),
        gate_up_adapter_gradient_slice,
        ff_start,
        3,
    )
    grad_a_dn_part = jnp.einsum(
        "uya,uye->uae",
        hidden_state.astype(jnp.float32),
        down_rank_gradient,
        precision=highest_precision,
    )
    grad_a_dn = lax.dynamic_update_slice_in_dim(
        jnp.zeros((tree_count, FF, RANK), jnp.float32), grad_a_dn_part, ff_start, 1
    )
    down_adapter_up_gradient = adapter_scale * jnp.einsum(
        "ags,agh->ash", down_rank_rows, output_gradient, precision=highest_precision
    )
    grad_pieces = [
        grad_a_qkv,
        grad_b_qkv,
        grad_a_out,
        output_adapter_up_gradient,
        grad_a_gu,
        grad_b_gu,
        grad_a_dn,
        down_adapter_up_gradient,
    ]
    packed = jnp.concatenate([piece.reshape(tree_count, -1) for piece in grad_pieces], axis=1)
    by_adapter = jnp.dot(id_hot.astype(jnp.float32).T, packed, precision=highest_precision)
    owners_cols = contexts * tensors
    rows_own = ADAPTERS // fsdp_size
    cols_own = PARAMS // owners_cols
    arranged = by_adapter.reshape(fsdp_size, rows_own, owners_cols, cols_own).transpose(0, 2, 1, 3)
    arranged = arranged.reshape(fsdp_size * owners_cols * rows_own, cols_own)
    adapter_grads = lax.psum_scatter(
        arranged, ("fsdp", "context", "tensor"), scatter_dimension=0, tiled=True
    )
    return (block_out, input_grad, adapter_grads)


def solution(mesh):
    return jax.shard_map(
        shards,
        mesh=mesh,
        in_specs=(
            P("fsdp", "context", None),
            P("fsdp"),
            P("fsdp", None, "tensor"),
            P("tensor", "fsdp"),
            P("fsdp"),
            P("fsdp", None, "tensor"),
            P("tensor", "fsdp"),
            P("fsdp", None, None, "tensor"),
            P("fsdp", "tensor", None),
            P("fsdp", ("context", "tensor")),
            P("fsdp"),
            P("fsdp", None),
            P("fsdp", None),
            P("fsdp", "context", None),
            P("fsdp", "context", None),
            P("fsdp", "context", None),
        ),
        out_specs=(
            P("fsdp", "context", None),
            P("fsdp", "context", None),
            P("fsdp", ("context", "tensor")),
        ),
        check_vma=False,
    )
```

profile of v0, /device:TPU:0, one launch (start us, length us, event | category | flops | bytes accessed | tf_op | source)
XLA Modules:
  0.0 1168.4 jit_solution(4829525538750778763)
XLA Ops:
  8.0 19.0 %all_gather.38 = bf16[2,233472]{1,0:T(2,128)(2,1)} all-gather(bf16[2,29184]{1,0:T(2,128)(2,1)} %param.25), channel_id=1, replica_groups=mesh['fsdp'=4,'context'=4,'tensor'=2] {'context','tensor'}, dimensions={1}, use_global_device_ids=true | all-gather | bytes 1050624 | tf_op jit(solution)/shard_map/all_gather | solution.py:168
  30.6 10.7 all-reduce.5
  52.0 44.2 %all-gather.25.cloned.1.call-done = bf16[4,2,233472]{2,1,0:T(2,128)(2,1)} async-done(((bf16[1,2,233472]{2,1,0:T(2,128)(2,1)}), bf16[4,2,233472]{2,1,0:T(2,128)(2,1)}) %all-gather.25.cloned.1.call-update) | async-done | bytes 3735568 | tf_op jit(solution)/shard_map/all_gather | solution.py:176
  115.7 10.7 all_gather.42
  131.7 26.2 %all-gather.13.cloned.1.call-done = bf16[1,2560,384]{1,2,0:T(8,128)(2,1)} async-done(((bf16[1,640,384]{1,2,0:T(8,128)(2,1)}), bf16[1,2560,384]{1,2,0:T(8,128)(2,1)}) %all-gather.13.cloned.1.call-update) | async-done | bytes 1966096 | tf_op jit(solution)/shard_map/all_gather | solution.py:232
  157.9 17.9 %fusion.184 = (f32[6,640]{1,0:T(8,128)S(1)}, f32[6,640,2560]{2,1,0:T(8,128)}) fusion(bf16[2560,6,64]{0,2,1:T(8,128)(2,1)} %bitcast.440, bf16[640,6,32]{0,2,1:T(8,128)(2,1)} %get-tuple-element.75, bf16[640,6,32]{0,2,1:T(8,128)(2,1)S(1)} %copy-done.23, pred[640,2560]{1,0:T(8,128)(4,1)S(1)} %fusion.26), kind=kOutput, calls=%fused_computation.311 | convolution fusion | flops 1288761600 | bytes 43432960 | tf_op jit(solution)/shard_map/while/body/eval_jaxpr/rhd,khd->hrk/dot_general | solution.py:241
  175.8 16.2 %fusion = f32[6,640]{1,0:T(8,128)S(1)} fusion(f32[6,640,2560]{2,1,0:T(8,128)} %get-tuple-element.95, f32[6,640]{1,0:T(8,128)S(1)} %get-tuple-element.94), kind=kLoop, calls=%fused_computation.12 | loop fusion | flops 19656960 | bytes 39352320 | tf_op jit(solution)/shard_map/while/body/eval_jaxpr/reduce_sum | solution.py:247
  192.0 10.6 all-gather.23.cloned.1.call-done
  202.5 15.9 %fusion.66 = bf16[6,64,640]{2,1,0:T(8,128)(2,1)S(1)} fusion(bf16[2560,6,64]{0,2,1:T(8,128)(2,1)} %bitcast.453, f32[6,640,2560]{2,1,0:T(8,128)} %get-tuple-element.95, f32[6,640]{1,0:T(8,128)S(1)} %fusion, f32[6,640]{1,0:T(8,128)S(1)} %get-tuple-element.94), kind=kOutput, calls=%fused_computation.114 | convolution fusion | flops 1288028160 | bytes 41809920 | tf_op jit(solution)/shard_map/while/body/eval_jaxpr/hrk,khd->rhd/dot_general | solution.py:249
  242.9 12.6 %scatter_custom_fusion.1 = bf16[2560]{0:T(1024)(128)(2,1)S(1)} fusion(s32[1280]{0:T(1024)S(1)} %fusion.141, bf16[1280]{0:T(1024)(128)(2,1)S(1)} %reshape.1243, bf16[]{:T(256)} %constant.96.clone.1), kind=kCustom, calls=%fused_computation.263 | custom fusion | bytes 5122 | tf_op jit(solution)/shard_map/scatter | solution.py:311
  323.1 212.3 %all-gather.19.cloned.1.call-done = bf16[8,768,2,1024]{3,1,2,0:T(8,128)(2,1)} async-done(((bf16[2,768,2,1024]{3,1,2,0:T(8,128)(2,1)}), bf16[8,768,2,1024]{3,1,2,0:T(8,128)(2,1)}) %all-gather.19.cloned.1.call-update) | async-done | bytes 25165840 | tf_op jit(solution)/shard_map/all_gather | solution.py:319
  535.4 21.7 %convolution_bitcast_fusion = f32[1,8,320,2,1024]{4,2,3,1,0:T(8,128)} fusion(bf16[8,320,768,1]{2,1,3,0:T(8,128)(2,1)} %bitcast.436, bf16[8,768,2,1024]{3,1,2,0:T(8,128)(2,1)} %all-gather.19.cloned.1.call-done), kind=kOutput, calls=%fused_computation.45 | convolution fusion | flops 8053063680 | bytes 50069504 | tf_op jit(solution)/shard_map/secd,edjf->secjf/dot_general | solution.py:112
  557.1 102.8 %all-gather.21.cloned.1.call-done = bf16[8,1024,768]{2,1,0:T(8,128)(2,1)} async-done(((bf16[2,1024,768]{2,1,0:T(8,128)(2,1)}), bf16[8,1024,768]{2,1,0:T(8,128)(2,1)}) %all-gather.21.cloned.1.call-update) | async-done | bytes 12582928 | tf_op jit(solution)/shard_map/all_gather | solution.py:320
  659.9 24.1 %fusion.30 = (bf16[8,320,1,1024]{3,1,0,2:T(8,128)(2,1)}, bf16[8,320,1,1024]{3,1,0,2:T(8,128)(2,1)}) fusion(f32[1,8,320,2,1024]{4,2,3,1,0:T(8,128)} %convolution_bitcast_fusion, f32[8,320]{1,0:T(8,128)S(1)} %copy-done.71, bf16[8,320,768]{2,1,0:T(8,128)(2,1)} %bitcast.448, bf16[8,1024,768]{2,1,0:T(8,128)(2,1)} %all-gather.21.cloned.1.call-done), kind=kOutput, calls=%fused_computation.51 | convolution fusion | flops 4063232000 | bytes 47982592 | tf_op jit(solution)/shard_map/secd,efd->secf/dot_general | solution.py:121
  684.0 20.2 %fusion.2 = f32[8,320,768,1]{2,1,0,3:T(8,128)} fusion(bf16[8,768,2,1024]{3,1,2,0:T(8,128)(2,1)} %all-gather.19.cloned.1.call-done, bf16[8,320,1,1024]{3,1,0,2:T(8,128)(2,1)} %get-tuple-element.65, bf16[8,320,1,1024]{3,1,0,2:T(8,128)(2,1)} %get-tuple-element.64), kind=kOutput, calls=%fused_computation.14 | convolution fusion | flops 8058306560 | bytes 43515904 | tf_op jit(solution)/shard_map/secjf,edjf->secd/dot_general | solution.py:129
  745.5 10.3 all-reduce.14.cloned.1.call-done
  761.0 15.9 %fusion.32 = bf16[6,64,2560]{2,1,0:T(8,128)(2,1)S(1)} fusion(bf16[640,6,64]{0,2,1:T(8,128)(2,1)S(1)} %bitcast.443, f32[6,640,2560]{2,1,0:T(8,128)} %get-tuple-element.95, f32[6,640]{1,0:T(8,128)S(1)} %copy-done.26), kind=kOutput, calls=%fused_computation.54 | convolution fusion | flops 1278935040 | bytes 41794560 | tf_op jit(solution)/shard_map/while/body/eval_jaxpr/hrk,rhd->khd/dot_general | solution.py:399
  776.9 29.4 %multiply_reduce_fusion = (f32[6,640]{1,0:T(8,128)S(1)}, f32[6,640,2560]{2,1,0:T(8,128)}) fusion(f32[6,640,2560]{2,1,0:T(8,128)} %get-tuple-element.95, f32[6,640]{1,0:T(8,128)S(1)} %copy-done.26, bf16[640,6,64]{0,2,1:T(8,128)(2,1)S(1)} %bitcast.444, bf16[2560,6,64]{0,2,1:T(8,128)(2,1)} %bitcast.454), kind=kOutput, calls=%fused_computation.7 | convolution fusion | flops 1287778560 | bytes 81131520 | tf_op jit(solution)/shard_map/while/body/eval_jaxpr/rhd,khd->hrk/dot_general | solution.py:405
  808.6 32.1 %multiply_convert_fusion = bf16[6,640,2560]{2,1,0:T(8,128)(2,1)} fusion(f32[6,640,2560]{2,1,0:T(8,128)} %get-tuple-element.97, f32[6,640,2560]{2,1,0:T(8,128)} %get-tuple-element.95, f32[6,640]{1,0:T(8,128)S(1)} %get-tuple-element.96, f32[6,640]{1,0:T(8,128)S(1)} %copy-done.26), kind=kLoop, calls=%fused_computation.6 | loop fusion | flops 39321600 | bytes 98334720 | tf_op jit(solution)/shard_map/while/body/eval_jaxpr/convert_element_type | solution.py:409
  840.7 11.4 fusion.31
  877.5 15.3 %fusion.27 = f32[8,320,768]{2,1,0:T(8,128)} fusion(bf16[8,1024,768]{2,1,0:T(8,128)(2,1)} %all-gather.21.cloned.1.call-done, f32[1,8,320,2,1024]{4,2,3,1,0:T(8,128)} %convolution_bitcast_fusion), kind=kOutput, calls=%fused_computation.49 | convolution fusion | flops 4042260480 | bytes 41418752 | tf_op jit(solution)/shard_map/secf,efd->secd/dot_general | solution.py:114
  920.4 10.4 fusion.67
  966.7 9.3 reshape.1193
  989.4 170.3 %all-reduce.16.cloned.1.call-done = f32[64,29184]{1,0:T(8,128)} async-done(((f32[64,29184]{1,0:T(8,128)}), f32[64,29184]{1,0:T(8,128)}) %all-reduce.16.cloned.1.call-update) | async-done | bytes 7471120
  (362 shorter events, 282.0 us)
Async XLA Ops:
  7.2 38.6 %copy-start.4 = (bf16[1,640,768]{2,1,0:T(8,128)(2,1)S(1)}, bf16[1,640,768]{2,1,0:T(8,128)(2,1)}, u32[]{:S(2)}) copy-start(bf16[1,640,768]{2,1,0:T(8,128)(2,1)} %param.16) | copy-start | bytes 2949124
  7.2 39.9 %all-gather.11.cloned.1.call-start = ((), (), s32[]{:S(2)}) async-start(), calls=%async_computation.1 | async-start | bytes 2211840 | tf_op jit(solution)/shard_map/all_gather | solution.py:170
  7.9 88.3 %all-gather.25.cloned.1.call-start = ((), (), s32[]{:S(2)}) async-start(), calls=%async_computation.11 | async-start | bytes 4669440 | tf_op jit(solution)/shard_map/all_gather | solution.py:176
  27.0 130.9 %all-gather.13.cloned.1.call-start = ((), (), s32[]{:S(2)}) async-start(), calls=%async_computation.2 | async-start | bytes 2457600 | tf_op jit(solution)/shard_map/all_gather | solution.py:232
  41.3 65.4 %copy-start.62 = (f32[768]{0:T(1024)}, f32[768]{0:T(1024)S(1)}, u32[]{:S(2)}) copy-start(f32[768]{0:T(1024)S(1)} %convert_element_type.279) | copy-start | bytes 9220
  45.3 70.1 %copy-start.57 = (s32[2560]{0:T(1024)}, s32[2560]{0:T(1024)S(1)}, u32[]{:S(2)}) copy-start(s32[2560]{0:T(1024)S(1)} %broadcast_add_fusion) | copy-start | bytes 30724
  46.7 60.0 %copy-start.68 = (f32[640]{0:T(1024)}, f32[640]{0:T(1024)S(1)}, u32[]{:S(2)}) copy-start(f32[640]{0:T(1024)S(1)} %get-tuple-element.89) | copy-start | bytes 7684
  47.0 64.9 %copy-start.33 = (f32[640,32]{0,1:T(8,128)}, f32[640,32]{0,1:T(8,128)S(1)}, u32[]{:S(2)}) copy-start(f32[640,32]{0,1:T(8,128)S(1)} %get-tuple-element.86) | copy-start | bytes 245764
  47.1 64.9 %copy-start.35 = (f32[640,32]{0,1:T(8,128)}, f32[640,32]{0,1:T(8,128)S(1)}, u32[]{:S(2)}) copy-start(f32[640,32]{0,1:T(8,128)S(1)} %get-tuple-element.87) | copy-start | bytes 245764
  113.9 88.6 %all-gather.23.cloned.1.call-start = ((), (), s32[]{:S(2)}) async-start(), calls=%async_computation.10 | async-start | bytes 2457600 | tf_op jit(solution)/shard_map/all_gather | solution.py:233
  114.8 150.7 %all-gather.17.cloned.1.call-start = ((), (), s32[]{:S(2)}) async-start(), calls=%async_computation.5 | async-start | bytes 1966080 | tf_op jit(solution)/shard_map/all_gather | solution.py:173
  115.4 168.4 %all-reduce.12.cloned.1.call-start = ((), (), s32[]{:S(2)}) async-start(), calls=%async_computation.3 | async-start | bytes 3932160 | tf_op jit(solution)/shard_map/psum | solution.py:268
  126.4 31.5 %copy-start.23 = (bf16[640,6,32]{0,2,1:T(8,128)(2,1)S(1)}, bf16[640,6,32]{0,2,1:T(8,128)(2,1)}, u32[]{:S(2)}) copy-start(bf16[640,6,32]{0,2,1:T(8,128)(2,1)} %get-tuple-element.74) | copy-start | bytes 737284
  223.6 82.0 %all-gather.15.cloned.1.call-start = ((), (), s32[]{:S(2)}) async-start(), calls=%async_computation.4 | async-start | bytes 3932160 | tf_op jit(solution)/shard_map/all_gather | solution.py:172
  224.8 310.6 %all-gather.19.cloned.1.call-start = ((), (), s32[]{:S(2)}) async-start(), calls=%async_computation.6 | async-start | bytes 31457280 | tf_op jit(solution)/shard_map/all_gather | solution.py:319
  232.5 427.4 %all-gather.21.cloned.1.call-start = ((), (), s32[]{:S(2)}) async-start(), calls=%async_computation.7 | async-start | bytes 15728640 | tf_op jit(solution)/shard_map/all_gather | solution.py:320
  233.2 522.6 %all-reduce.14.cloned.1.call-start = ((), (), s32[]{:S(2)}) async-start(), calls=%async_computation.8 | async-start | bytes 3932160 | tf_op jit(solution)/shard_map/psum | solution.py:372
  319.5 237.6 %copy-start.48 = (f32[2,16,640]{2,1,0:T(8,128)}, f32[2,16,640]{2,1,0:T(8,128)S(1)}, u32[]{:S(2)}) copy-start(f32[2,16,640]{2,1,0:T(8,128)S(1)} %convolution_multiply_fusion.4) | copy-start | bytes 245764
  535.4 124.5 %copy-start.71 = (f32[8,320]{1,0:T(8,128)S(1)}, f32[8,320]{1,0:T(8,128)}, u32[]{:S(2)}) copy-start(f32[8,320]{1,0:T(8,128)} %reshape.1195) | copy-start | bytes 30724
  734.6 199.5 %reduce-scatter.2.cloned.1.call-start = ((), (), s32[]{:S(2)}) async-start(), calls=%async_computation.9 | async-start | bytes 4915200 | tf_op jit(solution)/shard_map/reduce_scatter | solution.py:427
  808.6 32.1 %copy-start.24 = (bf16[640,6,32]{0,2,1:T(8,128)(2,1)S(1)}, bf16[640,6,32]{0,2,1:T(8,128)(2,1)}, u32[]{:S(2)}) copy-start(bf16[640,6,32]{0,2,1:T(8,128)(2,1)} %get-tuple-element.74) | copy-start | bytes 737284
  808.6 32.1 %copy-start.25 = (bf16[640,6,32]{0,2,1:T(8,128)(2,1)S(1)}, bf16[640,6,32]{0,2,1:T(8,128)(2,1)}, u32[]{:S(2)}) copy-start(bf16[640,6,32]{0,2,1:T(8,128)(2,1)} %get-tuple-element.75) | copy-start | bytes 737284
  860.0 123.0 %all-reduce.18.cloned.1.call-start = ((), (), s32[]{:S(2)}) async-start(), calls=%async_computation.13 | async-start | bytes 3932160 | tf_op jit(solution)/shard_map/psum | solution.py:327
  961.5 198.3 %all-reduce.16.cloned.1.call-start = ((), (), s32[]{:S(2)}) async-start(), calls=%async_computation.12 | async-start | bytes 14942208
  (72 other events, 416.2 us)
Sparse Core Ops, SparseCore 0:
  9.9 35.5 all-gather.10
  47.3 48.8 all-gather.24
  114.0 43.8 all-gather.12
  159.9 42.6 all-gather.22
  204.2 29.7 all-gather.16
  236.8 21.0 all-reduce.11
  260.4 45.1 all-gather.14
  307.6 227.6 all-gather.18
  537.4 122.5 all-gather.20
  734.7 21.0 all-reduce.13
  860.2 73.8 reduce-scatter.1
  961.6 21.4 all-reduce.17
  989.9 169.8 all-reduce.15
where the time goes:
time: 1180 us; the launch traced here: 1170 us
  waiting for transfers between devices  596 us (51%)
  matrix products  268 us (23%)
  local copies, waits for them, and re-layouts  137 us (12%)
  other arithmetic  110 us (9%)
  blocking collectives  40.4 us (3%)
  between operations  16.8 us (1%)
    all_gather x1, waiting for transfers between devices, shards(): lax.all_gather(w_egu, 'fsdp', axis=0, tiled=True)  212 us
    unnamed x14, waiting for transfers between devices  172 us
    all_gather x1, waiting for transfers between devices, shards(): lax.all_gather(w_edn, 'fsdp', axis=0, tiled=True)  103 us
    all_gather x1, waiting for transfers between devices, shards(): lax.all_gather(adapter_cols, 'fsdp', axis=0, tiled=True)  44.2 us
    convert_element_type x1, other arithmetic, attend_back(): (probabilities * (grad_probs - inner_sum)).astype(jnp.bfloat16)  32.1 us
    dot_general x1, matrix products, attend_back(): jnp.einsum('rhd,khd->hrk', grad_rows, value_block, preferred_element_type...  29.4 us
    unnamed x188, local copies, waits for them, and re-layouts  27.3 us
    all_gather x1, waiting for transfers between devices, shards(): lax.all_gather(key_rows, 'context', axis=1, tiled=True)  26.2 us
  transfers between devices with their start and end apart: 13, of which 10 were waited for; matrix products, arithmetic and copies ran while one was open for 24% of the time, Pallas kernels for 0%

commit v1 on v0

--- a/solution.py
+++ b/solution.py
@@ -1,6 +1,10 @@
 import jax
 import jax.numpy as jnp
+import functools
+
 from jax import lax
+from jax.experimental import pallas as pl
+from jax.experimental.pallas import tpu as pltpu
 from jax.sharding import PartitionSpec as P
 
 D = 768
@@ -108,27 +112,169 @@
     return (seg_hot, positions)
 
 
-def expert_forward(inputs, gate_weights, down_weights):
-    pre = jnp.einsum("secd,edjf->secjf", inputs, gate_weights, preferred_element_type=jnp.float32)
-    active = (silu_of(pre[..., 0, :]) * pre[..., 1, :]).astype(jnp.bfloat16)
-    return jnp.einsum("secf,efd->secd", active, down_weights, preferred_element_type=jnp.float32)
-
-
-def expert_backward(inputs, out_grads, gate_values, gate_weights, down_weights):
-    pre = jnp.einsum("secd,edjf->secjf", inputs, gate_weights, preferred_element_type=jnp.float32)
-    gate_pre = pre[..., 0, :]
-    up_pre = pre[..., 1, :]
-    grad_active = jnp.einsum(
-        "secd,efd->secf", out_grads, down_weights, preferred_element_type=jnp.float32
-    )
-    grad_active = grad_active * gate_values.astype(jnp.float32)[..., None]
-    sigmoid_gate = jax.nn.sigmoid(gate_pre)
-    grad_gate = grad_active * up_pre * sigmoid_gate * (1.0 + gate_pre * (1.0 - sigmoid_gate))
-    grad_up = grad_active * gate_pre * sigmoid_gate
-    grad_pre = jnp.stack([grad_gate, grad_up], axis=-2).astype(jnp.bfloat16)
-    return jnp.einsum(
-        "secjf,edjf->secd", grad_pre, gate_weights, preferred_element_type=jnp.float32
-    )
+SLOT_TILE = 256
+TOKEN_TILE = 256
+
+
+def nt_dot(left, right):
+    return lax.dot_general(left, right, (((1,), (1,)), ((), ())), preferred_element_type=jnp.float32)
+
+
+def tn_dot(left, right):
+    return lax.dot_general(left, right, (((0,), (0,)), ((), ())), preferred_element_type=jnp.float32)
+
+
+def nn_dot(left, right):
+    return jnp.dot(left, right, preferred_element_type=jnp.float32)
+
+
+def moe_kernel(
+    spans,
+    place_row,
+    weight_row,
+    place_col,
+    weight_col,
+    rows_ref,
+    grads_ref,
+    egu_hbm,
+    edn_hbm,
+    out_ref,
+    back_ref,
+    egu_ref,
+    edn_ref,
+    out_sum,
+    back_sum,
+    taken,
+    taken_grad,
+    slot_weight,
+    sems,
+):
+    experts = egu_hbm.shape[0]
+    copies = []
+    for e in range(experts):
+        copies.append(
+            (
+                pltpu.make_async_copy(egu_hbm.at[e], egu_ref.at[e], sems.at[e, 0]),
+                pltpu.make_async_copy(edn_hbm.at[e], edn_ref.at[e], sems.at[e, 1]),
+            )
+        )
+        copies[e][0].start()
+        copies[e][1].start()
+    out_sum[...] = jnp.zeros_like(out_sum)
+    back_sum[...] = jnp.zeros_like(back_sum)
+    slot_rows = lax.broadcasted_iota(jnp.int32, (SLOT_TILE, TOKEN_TILE), 0)
+    slot_cols = lax.broadcasted_iota(jnp.int32, (TOKEN_TILE, SLOT_TILE), 1)
+    for e in range(experts):
+        copies[e][0].wait()
+        copies[e][1].wait()
+
+        def tile_step(i, carry, e=e):
+            low = spans[e, 1 + 2 * i]
+            high = spans[e, 2 + 2 * i]
+            first = i * SLOT_TILE
+            taken[...] = jnp.zeros_like(taken)
+            taken_grad[...] = jnp.zeros_like(taken_grad)
+            slot_weight[...] = jnp.zeros_like(slot_weight)
+
+            def fetch(b, c):
+                start = pl.multiple_of(b * TOKEN_TILE, TOKEN_TILE)
+                hit = place_row[e, :, pl.ds(start, TOKEN_TILE)] == slot_rows + first
+                pick = jnp.where(hit, 1.0, 0.0).astype(jnp.bfloat16)
+                taken[...] += nn_dot(pick, rows_ref[pl.ds(start, TOKEN_TILE), :])
+                taken_grad[...] += nn_dot(pick, grads_ref[pl.ds(start, TOKEN_TILE), :])
+                slot_weight[...] += jnp.sum(
+                    jnp.where(hit, weight_row[e, :, pl.ds(start, TOKEN_TILE)], 0.0),
+                    axis=1,
+                    keepdims=True,
+                )
+                return c
+
+            lax.fori_loop(low, high, fetch, 0)
+            inputs = taken[...].astype(jnp.bfloat16)
+            gate_pre = nn_dot(inputs, egu_ref[e, 0])
+            up_pre = nn_dot(inputs, egu_ref[e, 1])
+            sigmoid_gate = jax.nn.sigmoid(gate_pre)
+            silu = gate_pre * sigmoid_gate
+            active = (silu * up_pre).astype(jnp.bfloat16)
+            result = nn_dot(active, edn_ref[e]).astype(jnp.bfloat16)
+            grad_active = nt_dot(taken_grad[...].astype(jnp.bfloat16), edn_ref[e])
+            grad_active = grad_active * slot_weight[...]
+            grad_gate = (
+                grad_active * up_pre * sigmoid_gate * (1.0 + gate_pre * (1.0 - sigmoid_gate))
+            ).astype(jnp.bfloat16)
+            grad_up = (grad_active * silu).astype(jnp.bfloat16)
+            grad_rows = (
+                nt_dot(grad_gate, egu_ref[e, 0]) + nt_dot(grad_up, egu_ref[e, 1])
+            ).astype(jnp.bfloat16)
+
+            def give(b, c):
+                start = pl.multiple_of(b * TOKEN_TILE, TOKEN_TILE)
+                block = pl.ds(start, TOKEN_TILE)
+                hit = place_col[block, e : e + 1] == slot_cols + first
+                pick = jnp.where(hit, 1.0, 0.0).astype(jnp.bfloat16)
+                out_sum[block, :] += nn_dot(pick, result) * weight_col[block, e : e + 1]
+                back_sum[block, :] += nn_dot(pick, grad_rows)
+                return c
+
+            lax.fori_loop(low, high, give, 0)
+            return carry
+
+        lax.fori_loop(0, spans[e, 0], tile_step, 0)
+    out_ref[...] = out_sum[...].astype(jnp.bfloat16)
+    back_ref[...] = back_sum[...].astype(jnp.bfloat16)
+
+
+def moe_layout(routes, weights, first_expert, experts):
+    total = routes.shape[0]
+    blocks = total // TOKEN_TILE
+    ids = first_expert + jnp.arange(experts, dtype=jnp.int32)
+    hits = routes[None] == ids[:, None, None]
+    hit = jnp.any(hits, axis=-1)
+    weight = jnp.sum(jnp.where(hits, weights.astype(jnp.float32)[None], 0.0), axis=-1)
+    counted = hit.astype(jnp.int32)
+    upto = jnp.cumsum(counted, axis=1)
+    place = jnp.where(hit, upto - 1, -1)
+    ends = upto.reshape(experts, blocks, TOKEN_TILE)[:, :, -1]
+    begins = jnp.concatenate([jnp.zeros((experts, 1), jnp.int32), ends[:, :-1]], axis=1)
+    count = ends[:, -1]
+    tiles = total // SLOT_TILE
+    tile_start = jnp.arange(tiles, dtype=jnp.int32) * SLOT_TILE
+    low = jnp.sum((ends[:, None, :] <= tile_start[None, :, None]).astype(jnp.int32), axis=2)
+    tile_end = jnp.minimum(tile_start[None] + SLOT_TILE, count[:, None])
+    high = jnp.sum((begins[:, None, :] < tile_end[:, :, None]).astype(jnp.int32), axis=2)
+    spans = jnp.stack([low, high], axis=2).reshape(experts, 2 * tiles)
+    spans = jnp.concatenate([((count + SLOT_TILE - 1) // SLOT_TILE)[:, None], spans], axis=1)
+    return spans, place, weight
+
+
+def moe_call(spans, place, weight, rows, grads, egu, edn):
+    total, width = rows.shape
+    experts, _, _, units = egu.shape
+    vmem = pl.BlockSpec(memory_space=pltpu.VMEM)
+    hbm = pl.BlockSpec(memory_space=pl.ANY)
+    shape = jax.ShapeDtypeStruct((total, width), jnp.bfloat16)
+    return pl.pallas_call(
+        moe_kernel,
+        grid_spec=pltpu.PrefetchScalarGridSpec(
+            num_scalar_prefetch=1,
+            grid=(),
+            in_specs=[vmem] * 6 + [hbm] * 2,
+            out_specs=[vmem, vmem],
+            scratch_shapes=[
+                pltpu.VMEM(egu.shape, jnp.bfloat16),
+                pltpu.VMEM(edn.shape, jnp.bfloat16),
+                pltpu.VMEM((total, width), jnp.float32),
+                pltpu.VMEM((total, width), jnp.float32),
+                pltpu.VMEM((SLOT_TILE, width), jnp.float32),
+                pltpu.VMEM((SLOT_TILE, width), jnp.float32),
+                pltpu.VMEM((SLOT_TILE, 1), jnp.float32),
+                pltpu.SemaphoreType.DMA((experts, 2)),
+            ],
+        ),
+        out_shape=[shape, shape],
+        name="experts",
+        compiler_params=pltpu.CompilerParams(vmem_limit_bytes=60 << 20),
+    )(spans, place[:, None, :], weight[:, None, :], place.T, weight.T, rows, grads, egu, edn)
 
 
 def shards(
@@ -165,20 +311,22 @@
     ff_start = part_index * local_ff
     head_shape = (tree_count, row_count, local_heads, HEAD_DIM)
     wide_shape = (tree_count, tree_len, local_heads, HEAD_DIM)
-    adapter_cols = lax.all_gather(adapters, ("context", "tensor"), axis=1, tiled=True)
-    qkv_weight, output_matrix, gu_weight, down_matrix, gain_one, gain_two, adapter_all = (
+    qkv_weight, output_matrix, gu_weight, down_matrix, gain_one, gain_two, adapter_cols = (
         lax.all_gather(w_qkv, "fsdp", axis=0, tiled=True),
         lax.all_gather(w_out, "fsdp", axis=1, tiled=True),
         lax.all_gather(w_gu, "fsdp", axis=0, tiled=True),
         lax.all_gather(w_dn, "fsdp", axis=1, tiled=True),
         lax.all_gather(attn_gain, "fsdp", axis=0, tiled=True),
         lax.all_gather(ffn_gain, "fsdp", axis=0, tiled=True),
-        lax.all_gather(adapter_cols, "fsdp", axis=0, tiled=True),
+        lax.all_gather(adapters, "fsdp", axis=0, tiled=True),
     )
     id_hot = (adapter_ids[:, None] == jnp.arange(ADAPTERS, dtype=jnp.int32)[None, :]).astype(
         jnp.bfloat16
     )
-    chosen = jnp.dot(id_hot, adapter_all, preferred_element_type=jnp.float32)
+    own_cols = jnp.dot(id_hot, adapter_cols, preferred_element_type=jnp.float32)
+    chosen = lax.all_gather(
+        own_cols.astype(jnp.bfloat16), ("context", "tensor"), axis=1, tiled=True
+    ).astype(jnp.float32)
     (
         a_qkv,
         query_key_value_adapter_up,
@@ -293,36 +441,20 @@
     shared_slice = shared_slice + adapter_scale * jnp.einsum(
         "trk,tkd->trd", down_rank_rows, down_adapter_up, precision=highest_precision
     )
-    capacity = 4 * token_count // EXPERTS
-    flat_routes = routes.reshape(token_count * TOPK)
-    route_hot = (flat_routes[:, None] == jnp.arange(EXPERTS, dtype=jnp.int32)[None, :]).astype(
-        jnp.int32
-    )
-    slot_place = jnp.sum((jnp.cumsum(route_hot, axis=0) - route_hot) * route_hot, axis=1)
-    slot_index = flat_routes * capacity + slot_place
-    slot_owner = (
-        jnp.full((EXPERTS * capacity,), token_count, jnp.int32)
-        .at[slot_index]
-        .set(jnp.arange(token_count * TOPK, dtype=jnp.int32) // TOPK)
-    )
-    gate_grid = (
-        jnp.zeros((EXPERTS * capacity,), jnp.bfloat16)
-        .at[slot_index]
-        .set(route_weights.reshape(token_count * TOPK))
-        .reshape(EXPERTS, capacity)
-    )
-    padded_rows = jnp.concatenate(
-        [normed_two.reshape(token_count, D), jnp.zeros((1, D), jnp.bfloat16)], axis=0
-    )
-    dispatched = padded_rows[slot_owner].reshape(EXPERTS, capacity, D)
-    egu_all, edn_all = (
-        lax.all_gather(w_egu, "fsdp", axis=0, tiled=True),
-        lax.all_gather(w_edn, "fsdp", axis=0, tiled=True),
-    )
-    expert_out = expert_forward(dispatched[None], egu_all, edn_all)[0]
-    picked = expert_out.reshape(EXPERTS * capacity, D)[slot_index].reshape(token_count, TOPK, D)
-    moe_part = jnp.sum(
-        picked * route_weights.astype(jnp.float32).reshape(token_count, TOPK, 1), axis=1
+    routes_all = lax.all_gather(routes[0], "fsdp", axis=0, tiled=True)
+    route_weights_all = lax.all_gather(route_weights[0], "fsdp", axis=0, tiled=True)
+    cotangent_all = lax.all_gather(cotangent[0], "fsdp", axis=0, tiled=True)
+    normed_all = lax.all_gather(normed_two[0], "fsdp", axis=0, tiled=True)
+    own_experts = EXPERTS // fsdp_size
+    spans, place, weight = moe_layout(
+        routes_all, route_weights_all, lax.axis_index("fsdp") * own_experts, own_experts
+    )
+    moe_all, moe_back_all = moe_call(
+        spans, place, weight, normed_all, cotangent_all, w_egu.transpose(0, 2, 1, 3), w_edn
+    )
+    moe_part = lax.psum_scatter(moe_all, "fsdp", scatter_dimension=0, tiled=True).astype(jnp.float32)
+    moe_grad = lax.psum_scatter(moe_back_all, "fsdp", scatter_dimension=0, tiled=True).astype(
+        jnp.float32
     )
     ffn_total = lax.psum(
         (shared_slice + moe_part.reshape(tree_count, row_count, D)).astype(jnp.bfloat16), "tensor"
@@ -357,16 +489,6 @@
     rank_gu_flat = gate_up_rank_gradient.reshape(tree_count, row_count, 2 * RANK)
     grad_normed_two = grad_normed_two + jnp.einsum(
         "trm,tdm->trd", rank_gu_flat, a_gu, precision=highest_precision
-    )
-    padded_grads = jnp.concatenate(
-        [cotangent.reshape(token_count, D), jnp.zeros((1, D), jnp.bfloat16)], axis=0
-    )
-    grad_slots = padded_grads[slot_owner].reshape(EXPERTS, capacity, D)
-    expert_grad = expert_backward(
-        dispatched[None], grad_slots[None], gate_grid[None], egu_all, edn_all
-    )[0]
-    moe_grad = jnp.sum(
-        expert_grad.reshape(EXPERTS * capacity, D)[slot_index].reshape(token_count, TOPK, D), axis=1
     )
     grad_normed_two = grad_normed_two + moe_grad.reshape(tree_count, row_count, D)
     grad_normed_two = lax.psum(grad_normed_two, "tensor")
@@ -512,15 +634,15 @@
         down_adapter_up_gradient,
     ]
     packed = jnp.concatenate([piece.reshape(tree_count, -1) for piece in grad_pieces], axis=1)
-    by_adapter = jnp.dot(id_hot.astype(jnp.float32).T, packed, precision=highest_precision)
-    owners_cols = contexts * tensors
+    own_part = lax.psum_scatter(
+        packed[0], ("context", "tensor"), scatter_dimension=0, tiled=True
+    )
+    part_all = lax.all_gather(own_part[None], "fsdp", axis=0, tiled=True)
+    ids_all = lax.all_gather(adapter_ids, "fsdp", axis=0, tiled=True)
     rows_own = ADAPTERS // fsdp_size
-    cols_own = PARAMS // owners_cols
-    arranged = by_adapter.reshape(fsdp_size, rows_own, owners_cols, cols_own).transpose(0, 2, 1, 3)
-    arranged = arranged.reshape(fsdp_size * owners_cols * rows_own, cols_own)
-    adapter_grads = lax.psum_scatter(
-        arranged, ("fsdp", "context", "tensor"), scatter_dimension=0, tiled=True
-    )
+    own_ids = lax.axis_index("fsdp") * rows_own + jnp.arange(rows_own, dtype=jnp.int32)
+    own_hot = (own_ids[:, None] == ids_all[None, :]).astype(jnp.float32)
+    adapter_grads = jnp.sum(own_hot[:, :, None] * part_all[None], axis=1)
     return (block_out, input_grad, adapter_grads)
 
 

time: 1180 us -> 772 us (0.65)
  waiting for transfers between devices: 596 us -> 274 us
  matrix products: 268 us -> 174 us
  local copies, waits for them, and re-layouts: 137 us -> 76 us
  Pallas kernels: 0 us -> 49.4 us
  blocking collectives: 40.4 us -> 85.8 us
  other arithmetic: 110 us -> 85.3 us
    all_gather x3 -> x2, waiting for transfers between devices: 359 us -> 65.2 us  [the longest x1 52.4 us: shards(): normed_all = lax.all_gather(normed_two[0], 'fsdp', axis=0, tiled=True)]
    unnamed x14 -> x15, waiting for transfers between devices: 172 us -> 45 us
    dot_general x5 -> x1, matrix products: 84.5 us -> 0.43 us  [shards(): own_cols = jnp.dot(id_hot, adapter_cols, preferred_element_type=jnp.float32)]
    pallas_call x0 -> x1, Pallas kernels: none -> 49.4 us  [moe_call(): pl.pallas_call(moe_kernel, grid_spec=pltpu.PrefetchScalarGridSpec(num_sca...]
    reduce_scatter x0 -> x2, waiting for transfers between devices: none -> 37.7 us  [the longest x1 37.7 us: shards(): lax.psum_scatter(moe_back_all, 'fsdp', scatter_dimension=0, tiled=True)]
    all_gather x1 -> x5, blocking collectives: 19 us -> 56 us  [the longest x1 17.3 us: shards(): lax.all_gather(own_cols.astype(jnp.bfloat16), ('context', 'tensor'), axis...]
    gather x4 -> x0, local copies, waits for them, and re-layouts: 36.1 us -> none  [the longest x1 9.25 us: shards(): expert_out.reshape(EXPERTS * capacity, D)[slot_index]]
    reduce_scatter x1, waiting for transfers between devices: 3.16 us -> 25.4 us  [shards(): lax.psum_scatter(grad_key_value.astype(jnp.bfloat16), 'context', scatter_...]
  transfers between devices with their start and end apart: 13 -> 14, of which waited for: 10 -> 11; matrix products, arithmetic and copies ran while one was open for 24% -> 35% of each run, Pallas kernels for 0% -> 6%
where the time goes in v1:
time: 772 us; the launch traced here: 763 us
  waiting for transfers between devices  274 us (35%)
  matrix products  174 us (23%)
  blocking collectives  85.8 us (11%)
  other arithmetic  85.3 us (11%)
  local copies, waits for them, and re-layouts  76 us (10%)
  Pallas kernels  49.4 us (6%)
  between operations  17.2 us (2%)
    all_gather x1, waiting for transfers between devices, shards(): normed_all = lax.all_gather(normed_two[0], 'fsdp', axis=0, tiled=True)  52.4 us
    pallas_call x1, Pallas kernels, moe_call(): pl.pallas_call(moe_kernel, grid_spec=pltpu.PrefetchScalarGridSpec(num_sca...  49.4 us
    unnamed x15, waiting for transfers between devices  45 us
    reduce_scatter x1, waiting for transfers between devices, shards(): lax.psum_scatter(moe_back_all, 'fsdp', scatter_dimension=0, tiled=True)  37.7 us
    unnamed x174, local copies, waits for them, and re-layouts  32.1 us
    convert_element_type x1, other arithmetic, attend_back(): (probabilities * (grad_probs - inner_sum)).astype(jnp.bfloat16)  32.1 us
    dot_general x1, matrix products, attend_back(): jnp.einsum('rhd,khd->hrk', grad_rows, value_block, preferred_element_type...  29.9 us
    reduce_scatter x1, waiting for transfers between devices, shards(): lax.psum_scatter(grad_key_value.astype(jnp.bfloat16), 'context', scatter_...  25.4 us
  transfers between devices with their start and end apart: 14, of which 11 were waited for; matrix products, arithmetic and copies ran while one was open for 35% of the time, Pallas kernels for 6%

profile of v1, /device:TPU:0, one launch (start us, length us, event | category | flops | bytes accessed | tf_op | source)
XLA Modules:
  0.0 763.1 jit_solution(4474667207104287496)
XLA Ops:
  13.0 11.4 %all-reduce.5 = (bf16[768]{0:T(1024)(128)(2,1)S(1)}, bf16[768]{0:T(1024)(128)(2,1)S(1)}) all-reduce(bf16[768]{0:T(1024)(128)(2,1)S(1)} %dynamic-update-slice.1, bf16[768]{0:T(1024)(128)(2,1)S(1)} %dynamic-update-slice), channel_id=1, replica_groups=mesh['fsdp'=4,'context'=4,'tensor'=2] {'fsdp'}, use_global_device_ids=true, to_apply=%add.2 | all-reduce | flops 1536 | bytes 6144
  26.8 11.8 %all-gather.7 = bf16[4,2,29184]{2,1,0:T(2,128)(2,1)S(1)} all-gather(bf16[1,2,29184]{2,1,0:T(2,128)(2,1)} %bitcast.355), channel_id=1, replica_groups=mesh['fsdp'=4,'context'=4,'tensor'=2] {'fsdp'}, dimensions={0}, use_global_device_ids=true | all-gather | bytes 583680 | tf_op jit(solution)/shard_map/all_gather | solution.py:321
  39.3 17.3 %all-gather.8 = bf16[8,1,29184]{2,1,0:T(2,128)(2,1)S(1)} all-gather(bf16[1,1,29184]{2,1,0:T(2,128)(2,1)S(1)} %reshape.1163), channel_id=2, replica_groups=mesh['fsdp'=4,'context'=4,'tensor'=2] {'context','tensor'}, dimensions={0}, use_global_device_ids=true | all-gather | bytes 525312 | tf_op jit(solution)/shard_map/all_gather | solution.py:327
  71.3 11.0 %all_gather.54 = bf16[384,768]{0,1:T(8,128)(2,1)S(1)} all-gather(bf16[384,192]{0,1:T(8,128)(2,1)} %param.19), channel_id=1, replica_groups=mesh['fsdp'=4,'context'=4,'tensor'=2] {'fsdp'}, dimensions={1}, use_global_device_ids=true | all-gather | bytes 737280 | tf_op jit(solution)/shard_map/all_gather | solution.py:316
  86.5 25.1 %all-gather.20.cloned.1.call-done = bf16[1,2560,384]{1,2,0:T(8,128)(2,1)} async-done(((bf16[1,640,384]{1,2,0:T(8,128)(2,1)}), bf16[1,2560,384]{1,2,0:T(8,128)(2,1)}) %all-gather.20.cloned.1.call-update) | async-done | bytes 1966096 | tf_op jit(solution)/shard_map/all_gather | solution.py:380
  111.6 17.9 %fusion.148 = (f32[6,640]{1,0:T(8,128)S(1)}, f32[6,640,2560]{2,1,0:T(8,128)}) fusion(bf16[2560,6,64]{0,2,1:T(8,128)(2,1)} %bitcast.312, bf16[640,6,32]{0,2,1:T(8,128)(2,1)} %get-tuple-element.77, bf16[640,6,32]{0,2,1:T(8,128)(2,1)S(1)} %copy-done.18, pred[640,2560]{1,0:T(8,128)(4,1)S(1)} %fusion.6), kind=kOutput, calls=%fused_computation.271 | convolution fusion | flops 1288761600 | bytes 43432960 | tf_op jit(solution)/shard_map/while/body/eval_jaxpr/rhd,khd->hrk/dot_general | solution.py:389
  129.5 16.2 %fusion = f32[6,640]{1,0:T(8,128)S(1)} fusion(f32[6,640,2560]{2,1,0:T(8,128)} %get-tuple-element.99, f32[6,640]{1,0:T(8,128)S(1)} %get-tuple-element.98), kind=kLoop, calls=%fused_computation.6 | loop fusion | flops 19656960 | bytes 39352320 | tf_op jit(solution)/shard_map/while/body/eval_jaxpr/reduce_sum | solution.py:395
  145.7 10.7 %all-gather.26.cloned.1.call-done = bf16[1,2560,1,384]{1,3,2,0:T(8,128)(2,1)} async-done(((bf16[1,640,1,384]{1,3,2,0:T(8,128)(2,1)}), bf16[1,2560,1,384]{1,3,2,0:T(8,128)(2,1)}) %all-gather.26.cloned.1.call-update) | async-done | bytes 1966096 | tf_op jit(solution)/shard_map/all_gather | solution.py:381
  156.4 15.6 %fusion.42 = bf16[6,64,640]{2,1,0:T(8,128)(2,1)S(1)} fusion(bf16[2560,6,64]{0,2,1:T(8,128)(2,1)} %bitcast.333, f32[6,640,2560]{2,1,0:T(8,128)} %get-tuple-element.99, f32[6,640]{1,0:T(8,128)S(1)} %fusion, f32[6,640]{1,0:T(8,128)S(1)} %get-tuple-element.98), kind=kOutput, calls=%fused_computation.77 | convolution fusion | flops 1288028160 | bytes 41809920 | tf_op jit(solution)/shard_map/while/body/eval_jaxpr/hrk,khd->rhd/dot_general | solution.py:397
  175.9 19.3 %all-reduce.12.cloned.1.call-done = f32[1,640,768]{2,1,0:T(8,128)} async-done(((f32[1,640,768]{2,1,0:T(8,128)}), f32[1,640,768]{2,1,0:T(8,128)}) %all-reduce.12.cloned.1.call-update) | async-done | bytes 1966096 | tf_op jit(solution)/shard_map/psum | solution.py:416
  236.0 12.8 %all-gather.30.cloned.1.call-done = bf16[1,2560,768]{2,1,0:T(8,128)(2,1)} async-done(((bf16[1,640,768]{2,1,0:T(8,128)(2,1)}), bf16[1,2560,768]{2,1,0:T(8,128)(2,1)}) %all-gather.30.cloned.1.call-update) | async-done | bytes 3932176 | tf_op jit(solution)/shard_map/all_gather | solution.py:446
  248.8 52.4 %all-gather.28.cloned.1.call-done = bf16[1,2560,768]{2,1,0:T(8,128)(2,1)} async-done(((bf16[1,640,768]{2,1,0:T(8,128)(2,1)}), bf16[1,2560,768]{2,1,0:T(8,128)(2,1)}) %all-gather.28.cloned.1.call-update) | async-done | bytes 3932176 | tf_op jit(solution)/shard_map/all_gather | solution.py:447
  301.2 49.4 %experts.1 = (bf16[2560,768]{1,0:T(8,128)(2,1)}, bf16[2560,768]{1,0:T(8,128)(2,1)}) custom-call(s32[2,21]{1,0:T(2,128)} %pad_add_fusion.1.spans, s32[2,1,2560]{2,1,0:T(1,128)} %copy_select_fusion.place_row, f32[2,1,2560]{2,1,0:T(1,128)} %broadcast_in_dim.73.weight_row, s32[2560,2]{1,0:T(8,128)} %bitcast.323, f32[2560,2]{1,0:T(8,128)} %bitcast.324, ...), custom_call_target="tpu_custom_call" | custom-call | tf_op jit(solution)/shard_map/experts/pallas_call | solution.py:256
  366.0 14.3 %all-gather.22.cloned.1.call-done = bf16[768,2,1024]{2,0,1:T(8,128)(2,1)} async-done(((bf16[192,2,1024]{2,0,1:T(8,128)(2,1)}), bf16[768,2,1024]{2,0,1:T(8,128)(2,1)}) %all-gather.22.cloned.1.call-update) | async-done | bytes 3145744 | tf_op jit(solution)/shard_map/all_gather | solution.py:317
  396.4 37.7 %reduce-scatter.6.cloned.1.call-done = bf16[640,768]{1,0:T(8,128)(2,1)} async-done(((bf16[2560,768]{1,0:T(8,128)(2,1)}), bf16[640,768]{1,0:T(8,128)(2,1)}) %reduce-scatter.6.cloned.1.call-update) | async-done | bytes 983056 | tf_op jit(solution)/shard_map/reduce_scatter | solution.py:456
  439.3 20.1 %all-reduce.14.cloned.1.call-done = f32[1,640,768]{2,1,0:T(8,128)} async-done(((f32[1,640,768]{2,1,0:T(8,128)}), f32[1,640,768]{2,1,0:T(8,128)}) %all-reduce.14.cloned.1.call-update) | async-done | bytes 1966096 | tf_op jit(solution)/shard_map/psum | solution.py:494
  464.8 29.9 %multiply_reduce_fusion = (f32[6,640]{1,0:T(8,128)S(1)}, f32[6,640,2560]{2,1,0:T(8,128)}) fusion(f32[6,640,2560]{2,1,0:T(8,128)} %get-tuple-element.99, f32[6,640]{1,0:T(8,128)S(1)} %log_add_fusion, bf16[640,6,64]{0,2,1:T(8,128)(2,1)S(1)} %bitcast.321, bf16[2560,6,64]{0,2,1:T(8,128)(2,1)} %bitcast.334), kind=kOutput, calls=%fused_computation.1 | convolution fusion | flops 1287778560 | bytes 81131520 | tf_op jit(solution)/shard_map/while/body/eval_jaxpr/rhd,khd->hrk/dot_general | solution.py:527
  494.7 17.4 %fusion.8 = bf16[6,64,2560]{2,1,0:T(8,128)(2,1)} fusion(bf16[640,6,64]{0,2,1:T(8,128)(2,1)S(1)} %bitcast.322, f32[6,640,2560]{2,1,0:T(8,128)} %get-tuple-element.99, f32[6,640]{1,0:T(8,128)S(1)} %log_add_fusion), kind=kOutput, calls=%fused_computation.17 | convolution fusion | flops 1278935040 | bytes 41794560 | tf_op jit(solution)/shard_map/while/body/eval_jaxpr/hrk,rhd->khd/dot_general | solution.py:521
  516.2 32.1 %multiply_convert_fusion = bf16[6,640,2560]{2,1,0:T(8,128)(2,1)} fusion(f32[6,640,2560]{2,1,0:T(8,128)} %get-tuple-element.101, f32[6,640,2560]{2,1,0:T(8,128)} %get-tuple-element.99, f32[6,640]{1,0:T(8,128)S(1)} %get-tuple-element.100, f32[6,640]{1,0:T(8,128)S(1)} %log_add_fusion), kind=kLoop, calls=%fused_computation | loop fusion | flops 39321600 | bytes 98334720 | tf_op jit(solution)/shard_map/while/body/eval_jaxpr/convert_element_type | solution.py:531
  548.3 11.4 %fusion.7 = bf16[6,64,2560]{2,1,0:T(8,128)(2,1)} fusion(bf16[6,640,2560]{2,1,0:T(8,128)(2,1)} %multiply_convert_fusion, bf16[640,6,32]{0,2,1:T(8,128)(2,1)S(1)} %copy-done.20, bf16[640,6,32]{0,2,1:T(8,128)(2,1)S(1)} %copy-done.19), kind=kOutput, calls=%fused_computation.16 | convolution fusion | flops 1261240320 | bytes 22118400 | tf_op jit(solution)/shard_map/while/body/eval_jaxpr/hrk,rhd->khd/dot_general | solution.py:537
  605.2 11.5 %fusion.43 = f32[1,640,6,64]{1,3,2,0:T(8,128)} fusion(bf16[2560,6,64]{0,2,1:T(8,128)(2,1)} %bitcast.313, bf16[6,640,2560]{2,1,0:T(8,128)(2,1)} %multiply_convert_fusion), kind=kOutput, calls=%fused_computation.79 | convolution fusion | flops 1258536960 | bytes 22609920 | tf_op jit(solution)/shard_map/while/body/eval_jaxpr/hrk,khd->rhd/dot_general | solution.py:533
  616.7 25.4 %reduce-scatter.8.cloned.1.call-done = bf16[1,640,768]{2,1,0:T(8,128)(2,1)} async-done(((bf16[1,2560,768]{2,1,0:T(8,128)(2,1)}), bf16[1,640,768]{2,1,0:T(8,128)(2,1)}) %reduce-scatter.8.cloned.1.call-update) | async-done | bytes 983056 | tf_op jit(solution)/shard_map/reduce_scatter | solution.py:549
  683.4 42.9 %all-reduce.16.cloned.1.call-done = f32[233472]{0:T(1024)} async-done(((f32[233472]{0:T(1024)}), f32[233472]{0:T(1024)}) %all-reduce.16.cloned.1.call-update) | async-done | bytes 933904
  738.8 11.6 %all-reduce.18.cloned.1.call-done = (bf16[1,640,768]{2,1,0:T(8,128)(2,1)}, bf16[1,640,768]{2,1,0:T(8,128)(2,1)}) async-done(((bf16[1,640,768]{2,1,0:T(8,128)(2,1)}, bf16[1,640,768]{2,1,0:T(8,128)(2,1)}), (bf16[1,640,768]{2,1,0:T(8,128)(2,1)}, bf16[1,640,768]{2,1,0:T(8,128)(2,1)})) %all-reduce.18.cloned.1.call-update) | async-done | bytes 1966096 | tf_op jit(solution)/shard_map/psum | solution.py:459
  (352 shorter events, 220.6 us)
Async XLA Ops:
  7.2 52.5 %all-gather.18.cloned.1.call-start = ((), (), s32[]{:S(2)}) async-start(), calls=%async_computation.3 | async-start | bytes 2211840 | tf_op jit(solution)/shard_map/all_gather | solution.py:315
  7.9 103.7 %all-gather.20.cloned.1.call-start = ((), (), s32[]{:S(2)}) async-start(), calls=%async_computation.4 | async-start | bytes 2457600 | tf_op jit(solution)/shard_map/all_gather | solution.py:380
  24.5 35.3 %copy-start.57 = (f32[768]{0:T(1024)}, f32[768]{0:T(1024)S(1)}, u32[]{:S(2)}) copy-start(f32[768]{0:T(1024)S(1)} %convert_element_type.280) | copy-start | bytes 9220
  68.1 88.2 %all-gather.26.cloned.1.call-start = ((), (), s32[]{:S(2)}) async-start(), calls=%async_computation.12 | async-start | bytes 2457600 | tf_op jit(solution)/shard_map/all_gather | solution.py:381
  70.3 102.6 %copy-start.40 = (bf16[16,768]{1,0:T(8,128)(2,1)}, bf16[16,768]{1,0:T(8,128)(2,1)S(1)}, u32[]{:S(2)}) copy-start(bf16[16,768]{1,0:T(8,128)(2,1)S(1)} %reshape.1110) | copy-start | bytes 73732
  82.3 89.9 %copy-start.12 = (bf16[384,768]{0,1:T(8,128)(2,1)}, bf16[384,768]{0,1:T(8,128)(2,1)S(1)}, u32[]{:S(2)}) copy-start(bf16[384,768]{0,1:T(8,128)(2,1)S(1)} %all_gather.54) | copy-start | bytes 1769476
  82.5 29.1 %copy-start.18 = (bf16[640,6,32]{0,2,1:T(8,128)(2,1)S(1)}, bf16[640,6,32]{0,2,1:T(8,128)(2,1)}, u32[]{:S(2)}) copy-start(bf16[640,6,32]{0,2,1:T(8,128)(2,1)} %get-tuple-element.76) | copy-start | bytes 737284
  86.4 108.8 %all-reduce.12.cloned.1.call-start = ((), (), s32[]{:S(2)}) async-start(), calls=%async_computation.5 | async-start | bytes 3932160 | tf_op jit(solution)/shard_map/psum | solution.py:416
  175.2 73.6 %all-gather.30.cloned.1.call-start = ((), (), s32[]{:S(2)}) async-start(), calls=%async_computation.14 | async-start | bytes 4915200 | tf_op jit(solution)/shard_map/all_gather | solution.py:446
  175.8 125.4 %all-gather.28.cloned.1.call-start = ((), (), s32[]{:S(2)}) async-start(), calls=%async_computation.13 | async-start | bytes 4915200 | tf_op jit(solution)/shard_map/all_gather | solution.py:447
  198.6 162.4 %all-gather.24.cloned.1.call-start = ((), (), s32[]{:S(2)}) async-start(), calls=%async_computation.7 | async-start | bytes 1966080 | tf_op jit(solution)/shard_map/all_gather | solution.py:318
  199.4 180.9 %all-gather.22.cloned.1.call-start = ((), (), s32[]{:S(2)}) async-start(), calls=%async_computation.6 | async-start | bytes 3932160 | tf_op jit(solution)/shard_map/all_gather | solution.py:317
  201.7 232.5 %reduce-scatter.6.cloned.1.call-start = ((), (), s32[]{:S(2)}) async-start(), calls=%async_computation.9 | async-start | bytes 4915200 | tf_op jit(solution)/shard_map/reduce_scatter | solution.py:456
  350.7 108.7 %all-reduce.14.cloned.1.call-start = ((), (), s32[]{:S(2)}) async-start(), calls=%async_computation.10 | async-start | bytes 3932160 | tf_op jit(solution)/shard_map/psum | solution.py:494
  392.7 41.5 %copy-start.38 = (f32[2,16,640]{2,1,0:T(8,128)}, f32[2,16,640]{2,1,0:T(8,128)S(1)}, u32[]{:S(2)}) copy-start(f32[2,16,640]{2,1,0:T(8,128)S(1)} %convolution_multiply_fusion.4) | copy-start | bytes 245764
  438.3 160.9 %reduce-scatter.4.cloned.1.call-start = ((), (), s32[]{:S(2)}) async-start(), calls=%async_computation.8 | async-start | bytes 4915200 | tf_op jit(solution)/shard_map/reduce_scatter | solution.py:455
  439.2 202.9 %reduce-scatter.8.cloned.1.call-start = ((), (), s32[]{:S(2)}) async-start(), calls=%async_computation.11 | async-start | bytes 4915200 | tf_op jit(solution)/shard_map/reduce_scatter | solution.py:549
  516.2 32.1 %copy-start.19 = (bf16[640,6,32]{0,2,1:T(8,128)(2,1)S(1)}, bf16[640,6,32]{0,2,1:T(8,128)(2,1)}, u32[]{:S(2)}) copy-start(bf16[640,6,32]{0,2,1:T(8,128)(2,1)} %get-tuple-element.76) | copy-start | bytes 737284
  516.2 32.1 %copy-start.20 = (bf16[640,6,32]{0,2,1:T(8,128)(2,1)S(1)}, bf16[640,6,32]{0,2,1:T(8,128)(2,1)}, u32[]{:S(2)}) copy-start(bf16[640,6,32]{0,2,1:T(8,128)(2,1)} %get-tuple-element.77) | copy-start | bytes 737284
  568.1 158.2 %all-reduce.16.cloned.1.call-start = ((), (), s32[]{:S(2)}) async-start(), calls=%async_computation.15 | async-start | bytes 1867776
  616.7 30.3 %copy-start.26 = (f32[640,32]{0,1:T(8,128)S(1)}, f32[640,32]{0,1:T(8,128)}, u32[]{:S(2)}) copy-start(f32[640,32]{0,1:T(8,128)} %copy-done.25) | copy-start | bytes 245764
  616.7 30.3 %copy-start.28 = (f32[640,32]{0,1:T(8,128)S(1)}, f32[640,32]{0,1:T(8,128)}, u32[]{:S(2)}) copy-start(f32[640,32]{0,1:T(8,128)} %copy-done.27) | copy-start | bytes 245764
  668.5 81.9 %all-reduce.18.cloned.1.call-start = ((), (), s32[]{:S(2)}) async-start(), calls=%async_computation.16 | async-start | bytes 3932160 | tf_op jit(solution)/shard_map/psum | solution.py:459
  674.0 76.3 %copy-start.59 = (f32[768]{0:T(1024)S(1)}, f32[768]{0:T(1024)}, u32[]{:S(2)}) copy-start(f32[768]{0:T(1024)} %copy-done.57) | copy-start | bytes 9220
  (64 other events, 433.7 us)
Sparse Core Ops, SparseCore 0:
  9.8 36.3 all-gather.17
  68.2 43.2 all-gather.19
  113.7 42.6 all-gather.25
  175.3 19.8 all-reduce.11
  197.0 51.7 all-gather.29
  250.7 50.5 all-gather.27
  303.2 30.9 all-gather.23
  336.2 43.9 all-gather.21
  383.6 50.5 reduce-scatter.5
  438.4 20.9 all-reduce.13
  462.5 51.6 reduce-scatter.3
  568.2 73.8 reduce-scatter.7
  668.6 57.7 all-reduce.15
  729.3 21.0 all-reduce.17

commit v2 on v1

--- a/solution.py
+++ b/solution.py
@@ -275,6 +275,110 @@
         name="experts",
         compiler_params=pltpu.CompilerParams(vmem_limit_bytes=60 << 20),
     )(spans, place[:, None, :], weight[:, None, :], place.T, weight.T, rows, grads, egu, edn)
+
+
+MESH = pl.DeviceIdType.MESH
+
+
+def place_of():
+    return lax.axis_index("fsdp"), lax.axis_index("context"), lax.axis_index("tensor")
+
+
+def greet(devices):
+    barrier = pltpu.get_barrier_semaphore()
+    for device in devices:
+        pl.semaphore_signal(barrier, inc=1, device_id=device, device_id_type=MESH)
+    pl.semaphore_wait(barrier, len(devices))
+
+
+def send(source, target, send_sem, recv_sem, device):
+    return pltpu.make_async_remote_copy(
+        src_ref=source,
+        dst_ref=target,
+        send_sem=send_sem,
+        recv_sem=recv_sem,
+        device_id=device,
+        device_id_type=MESH,
+    )
+
+
+def small_kernel(
+    sizes,
+    ids_ref,
+    adapters_ref,
+    gains_ref,
+    table_ref,
+    chosen_ref,
+    gains_all,
+    table_all,
+    adapters_all,
+    send_sems,
+    recv_sems,
+):
+    fsdp, contexts, _ = sizes
+    f, c, t = place_of()
+    peers = [(lax.rem(f + k, fsdp), c, t) for k in range(1, fsdp)]
+    stacked = [(f, lax.rem(c + k, contexts), t) for k in range(1, contexts)]
+    sibling = (f, c, 1 - t)
+    greet(peers + stacked + [sibling])
+    first = []
+    for k, peer in enumerate(peers):
+        for j, (source, target) in enumerate(
+            ((adapters_ref, adapters_all), (gains_ref, gains_all), (table_ref, table_all))
+        ):
+            copy = send(source, target.at[f], send_sems.at[j, k], recv_sems.at[j, k], peer)
+            copy.start()
+            first.append(copy)
+    adapters_all[f] = adapters_ref[...]
+    gains_all[f] = gains_ref[...]
+    table_all[f] = table_ref[...]
+    for copy in first:
+        copy.wait()
+    wanted = ids_ref[0]
+    rows = RANK
+    own = ADAPTERS // fsdp
+    total = jnp.zeros((rows, adapters_ref.shape[1]), jnp.float32)
+    for a in range(ADAPTERS):
+        block = adapters_all[a // own, pl.ds((a % own) * rows, rows), :].astype(jnp.float32)
+        total = total + jnp.where(wanted == a, block, 0.0)
+    chosen_ref[t, c] = total.astype(jnp.bfloat16)
+    second = []
+    for k, other in enumerate(stacked):
+        copy = send(
+            chosen_ref.at[t, c], chosen_ref.at[t, c], send_sems.at[3, k], recv_sems.at[3, k], other
+        )
+        copy.start()
+        second.append(copy)
+    for copy in second:
+        copy.wait()
+    last = send(chosen_ref.at[t], chosen_ref.at[t], send_sems.at[4, 0], recv_sems.at[4, 0], sibling)
+    last.start()
+    last.wait()
+
+
+def small_call(sizes, ids, adapters, gains, table):
+    fsdp, contexts, tensors = sizes
+    slots = max(fsdp, contexts)
+    vmem = pl.BlockSpec(memory_space=pltpu.VMEM)
+    return pl.pallas_call(
+        functools.partial(small_kernel, sizes),
+        in_specs=[pl.BlockSpec(memory_space=pltpu.SMEM), vmem, vmem, vmem],
+        out_specs=[vmem] * 3,
+        out_shape=[
+            jax.ShapeDtypeStruct((tensors, contexts, RANK, adapters.shape[1]), jnp.bfloat16),
+            jax.ShapeDtypeStruct((fsdp,) + gains.shape, gains.dtype),
+            jax.ShapeDtypeStruct((fsdp,) + table.shape, table.dtype),
+        ],
+        scratch_shapes=[
+            pltpu.VMEM((fsdp,) + adapters.shape, adapters.dtype),
+            pltpu.SemaphoreType.DMA((5, slots)),
+            pltpu.SemaphoreType.DMA((5, slots)),
+        ],
+        name="small_gather",
+        compiler_params=pltpu.CompilerParams(
+            collective_id=1, has_side_effects=True, vmem_limit_bytes=60 << 20
+        ),
+    )(ids, adapters, gains, table)
 
 
 def shards(
@@ -311,22 +415,31 @@
     ff_start = part_index * local_ff
     head_shape = (tree_count, row_count, local_heads, HEAD_DIM)
     wide_shape = (tree_count, tree_len, local_heads, HEAD_DIM)
-    qkv_weight, output_matrix, gu_weight, down_matrix, gain_one, gain_two, adapter_cols = (
+    qkv_weight, output_matrix, gu_weight, down_matrix = (
         lax.all_gather(w_qkv, "fsdp", axis=0, tiled=True),
         lax.all_gather(w_out, "fsdp", axis=1, tiled=True),
         lax.all_gather(w_gu, "fsdp", axis=0, tiled=True),
         lax.all_gather(w_dn, "fsdp", axis=1, tiled=True),
-        lax.all_gather(attn_gain, "fsdp", axis=0, tiled=True),
-        lax.all_gather(ffn_gain, "fsdp", axis=0, tiled=True),
-        lax.all_gather(adapters, "fsdp", axis=0, tiled=True),
-    )
-    id_hot = (adapter_ids[:, None] == jnp.arange(ADAPTERS, dtype=jnp.int32)[None, :]).astype(
-        jnp.bfloat16
-    )
-    own_cols = jnp.dot(id_hot, adapter_cols, preferred_element_type=jnp.float32)
-    chosen = lax.all_gather(
-        own_cols.astype(jnp.bfloat16), ("context", "tensor"), axis=1, tiled=True
-    ).astype(jnp.float32)
+    )
+    sizes = (fsdp_size, contexts, tensors)
+    own_adapters = adapters.shape[0]
+    own_width = D // fsdp_size
+    gains = jnp.broadcast_to(jnp.concatenate([attn_gain, ffn_gain])[None], (16, 2 * own_width))
+    route_table = jnp.concatenate(
+        [
+            routes[0].astype(jnp.float32).T,
+            route_weights[0].astype(jnp.float32).T,
+            jnp.zeros((4, row_count), jnp.float32),
+        ]
+    )
+    chosen_parts, gains_all, table_all = small_call(
+        sizes, adapter_ids, adapters.reshape(own_adapters * RANK, -1), gains, route_table
+    )
+    chosen = chosen_parts.transpose(1, 0, 2, 3).reshape(1, PARAMS).astype(jnp.float32)
+    gain_one = gains_all[:, 0, :own_width].reshape(D)
+    gain_two = gains_all[:, 0, own_width:].reshape(D)
+    routes_all = table_all[:, 0:2].transpose(0, 2, 1).reshape(-1, TOPK).astype(jnp.int32)
+    route_weights_all = table_all[:, 2:4].transpose(0, 2, 1).reshape(-1, TOPK)
     (
         a_qkv,
         query_key_value_adapter_up,
@@ -441,8 +554,6 @@
     shared_slice = shared_slice + adapter_scale * jnp.einsum(
         "trk,tkd->trd", down_rank_rows, down_adapter_up, precision=highest_precision
     )
-    routes_all = lax.all_gather(routes[0], "fsdp", axis=0, tiled=True)
-    route_weights_all = lax.all_gather(route_weights[0], "fsdp", axis=0, tiled=True)
     cotangent_all = lax.all_gather(cotangent[0], "fsdp", axis=0, tiled=True)
     normed_all = lax.all_gather(normed_two[0], "fsdp", axis=0, tiled=True)
     own_experts = EXPERTS // fsdp_size

time: 772 us -> 766 us (level)
  blocking collectives: 85.8 us -> 27.4 us
  Pallas kernels: 49.4 us -> 72.6 us
  waiting for transfers between devices: 274 us -> 297 us
    all_gather x4 -> x0, blocking collectives: 46.2 us -> none  [the longest x1 17.3 us: shards(): lax.all_gather(own_cols.astype(jnp.bfloat16), ('context', 'tensor'), axis...]
    pallas_call x0 -> x1, Pallas kernels: none -> 27.2 us  [small_call(): pl.pallas_call(functools.partial(small_kernel, sizes), in_specs=[pl.Block...]
    all_gather x1, waiting for transfers between devices: 12.8 us -> 29.6 us  [shards(): cotangent_all = lax.all_gather(cotangent[0], 'fsdp', axis=0, tiled=True)]
    unnamed x2 -> x1, blocking collectives: 18.8 us -> 7.32 us
    unnamed x174 -> x168, local copies, waits for them, and re-layouts: 32.1 us -> 29.6 us
  transfers between devices with their start and end apart: 14 -> 14, of which waited for: 11 -> 12; matrix products, arithmetic and copies ran while one was open for 35% -> 36% of each run, Pallas kernels for 6% -> 10%
where the time goes in v2:
time: 766 us; the launch traced here: 756 us
  waiting for transfers between devices  297 us (39%)
  matrix products  173 us (23%)
  other arithmetic  89 us (12%)
  local copies, waits for them, and re-layouts  78 us (10%)
  Pallas kernels  72.6 us (9%)
  blocking collectives  27.4 us (4%)
  between operations  16.5 us (2%)
    all_gather x1, waiting for transfers between devices, shards(): normed_all = lax.all_gather(normed_two[0], 'fsdp', axis=0, tiled=True)  52.4 us
    pallas_call x1, Pallas kernels, moe_call(): pl.pallas_call(moe_kernel, grid_spec=pltpu.PrefetchScalarGridSpec(num_sca...  45.4 us
    unnamed x15, waiting for transfers between devices  44.3 us
    reduce_scatter x1, waiting for transfers between devices, shards(): lax.psum_scatter(moe_back_all, 'fsdp', scatter_dimension=0, tiled=True)  37.7 us
    convert_element_type x1, other arithmetic, attend_back(): (probabilities * (grad_probs - inner_sum)).astype(jnp.bfloat16)  32.1 us
    dot_general x1, matrix products, attend_back(): jnp.einsum('rhd,khd->hrk', grad_rows, value_block, preferred_element_type...  29.9 us
    all_gather x1, waiting for transfers between devices, shards(): cotangent_all = lax.all_gather(cotangent[0], 'fsdp', axis=0, tiled=True)  29.6 us
    unnamed x168, local copies, waits for them, and re-layouts  29.6 us
  transfers between devices with their start and end apart: 14, of which 12 were waited for; matrix products, arithmetic and copies ran while one was open for 36% of the time, Pallas kernels for 10%

profile of v2, /device:TPU:0, one launch (start us, length us, event | category | flops | bytes accessed | tf_op | source)
XLA Modules:
  0.0 755.9 jit_solution(14249621713571465239)
XLA Ops:
  17.1 27.2 %small_gather.1 = (bf16[2,4,16,1824]{3,2,1,0:T(8,128)(2,1)}, bf16[4,16,384]{2,1,0:T(8,128)(2,1)}, f32[4,8,640]{2,1,0:T(8,128)}) custom-call(s32[1]{0:T(128)S(6)} %copy.206.ids_ref, bf16[32,1824]{1,0:T(8,128)(2,1)} %reshape.1134.adapters_ref, bf16[16,384]{1,0:T(8,128)(2,1)} %broadcast_in_dim.75.gains_ref, f32[8,640]{1,0:T(8,128)} %maximum_maximum_fusion.table_ref), custom_call_target="tpu_custom_call" | custom-call | tf_op jit(solution)/shard_map/small_gather/pallas_call | solution.py:363
  63.4 10.2 %all_gather.33 = bf16[384,768]{0,1:T(8,128)(2,1)S(1)} all-gather(bf16[384,192]{0,1:T(8,128)(2,1)} %param.19), channel_id=1, replica_groups=mesh['fsdp'=4,'context'=4,'tensor'=2] {'fsdp'}, dimensions={1}, use_global_device_ids=true | all-gather | bytes 737280 | tf_op jit(solution)/shard_map/all_gather | solution.py:420
  78.1 26.2 %all-gather.15.cloned.1.call-done = bf16[1,2560,384]{1,2,0:T(8,128)(2,1)} async-done(((bf16[1,640,384]{1,2,0:T(8,128)(2,1)}), bf16[1,2560,384]{1,2,0:T(8,128)(2,1)}) %all-gather.15.cloned.1.call-update) | async-done | bytes 1966096 | tf_op jit(solution)/shard_map/all_gather | solution.py:493
  104.2 17.9 %fusion.145 = (f32[6,640]{1,0:T(8,128)S(1)}, f32[6,640,2560]{2,1,0:T(8,128)}) fusion(bf16[2560,6,64]{0,2,1:T(8,128)(2,1)} %bitcast.317, bf16[640,6,32]{0,2,1:T(8,128)(2,1)} %get-tuple-element.83, bf16[640,6,32]{0,2,1:T(8,128)(2,1)S(1)} %copy-done.18, pred[640,2560]{1,0:T(8,128)(4,1)S(1)} %fusion.6), kind=kOutput, calls=%fused_computation.273 | convolution fusion | flops 1288761600 | bytes 43432960 | tf_op jit(solution)/shard_map/while/body/eval_jaxpr/rhd,khd->hrk/dot_general | solution.py:502
  122.2 16.2 %fusion = f32[6,640]{1,0:T(8,128)S(1)} fusion(f32[6,640,2560]{2,1,0:T(8,128)} %get-tuple-element.107, f32[6,640]{1,0:T(8,128)S(1)} %get-tuple-element.106), kind=kLoop, calls=%fused_computation.6 | loop fusion | flops 19656960 | bytes 39352320 | tf_op jit(solution)/shard_map/while/body/eval_jaxpr/reduce_sum | solution.py:508
  138.3 10.7 %all-gather.21.cloned.1.call-done = bf16[1,2560,1,384]{1,3,2,0:T(8,128)(2,1)} async-done(((bf16[1,640,1,384]{1,3,2,0:T(8,128)(2,1)}), bf16[1,2560,1,384]{1,3,2,0:T(8,128)(2,1)}) %all-gather.21.cloned.1.call-update) | async-done | bytes 1966096 | tf_op jit(solution)/shard_map/all_gather | solution.py:494
  149.0 15.6 %fusion.42 = bf16[6,64,640]{2,1,0:T(8,128)(2,1)S(1)} fusion(bf16[2560,6,64]{0,2,1:T(8,128)(2,1)} %bitcast.332, f32[6,640,2560]{2,1,0:T(8,128)} %get-tuple-element.107, f32[6,640]{1,0:T(8,128)S(1)} %fusion, f32[6,640]{1,0:T(8,128)S(1)} %get-tuple-element.106), kind=kOutput, calls=%fused_computation.77 | convolution fusion | flops 1288028160 | bytes 41809920 | tf_op jit(solution)/shard_map/while/body/eval_jaxpr/hrk,khd->rhd/dot_general | solution.py:510
  168.6 19.3 %all-reduce.9.cloned.1.call-done = f32[1,640,768]{2,1,0:T(8,128)} async-done(((f32[1,640,768]{2,1,0:T(8,128)}), f32[1,640,768]{2,1,0:T(8,128)}) %all-reduce.9.cloned.1.call-update) | async-done | bytes 1966096 | tf_op jit(solution)/shard_map/psum | solution.py:529
  202.0 7.5 copy.187
  211.9 29.6 %all-gather.25.cloned.1.call-done = bf16[1,2560,768]{2,1,0:T(8,128)(2,1)} async-done(((bf16[1,640,768]{2,1,0:T(8,128)(2,1)}), bf16[1,2560,768]{2,1,0:T(8,128)(2,1)}) %all-gather.25.cloned.1.call-update) | async-done | bytes 3932176 | tf_op jit(solution)/shard_map/all_gather | solution.py:557
  241.5 52.4 %all-gather.23.cloned.1.call-done = bf16[1,2560,768]{2,1,0:T(8,128)(2,1)} async-done(((bf16[1,640,768]{2,1,0:T(8,128)(2,1)}), bf16[1,2560,768]{2,1,0:T(8,128)(2,1)}) %all-gather.23.cloned.1.call-update) | async-done | bytes 3932176 | tf_op jit(solution)/shard_map/all_gather | solution.py:558
  293.9 45.4 %experts.1 = (bf16[2560,768]{1,0:T(8,128)(2,1)}, bf16[2560,768]{1,0:T(8,128)(2,1)}) custom-call(s32[2,21]{1,0:T(2,128)} %pad_add_fusion.1.spans, s32[2,1,2560]{2,1,0:T(1,128)} %copy_select_fusion.place_row, f32[2,1,2560]{2,1,0:T(1,128)} %broadcast_in_dim.87.weight_row, s32[2560,2]{1,0:T(8,128)} %bitcast.322, f32[2560,2]{1,0:T(8,128)} %bitcast.323, ...), custom_call_target="tpu_custom_call" | custom-call | tf_op jit(solution)/shard_map/experts/pallas_call | solution.py:256
  354.6 18.4 %all-gather.17.cloned.1.call-done = bf16[768,2,1024]{2,0,1:T(8,128)(2,1)} async-done(((bf16[192,2,1024]{2,0,1:T(8,128)(2,1)}), bf16[768,2,1024]{2,0,1:T(8,128)(2,1)}) %all-gather.17.cloned.1.call-update) | async-done | bytes 3145744 | tf_op jit(solution)/shard_map/all_gather | solution.py:421
  389.2 37.7 %reduce-scatter.6.cloned.1.call-done = bf16[640,768]{1,0:T(8,128)(2,1)} async-done(((bf16[2560,768]{1,0:T(8,128)(2,1)}), bf16[640,768]{1,0:T(8,128)(2,1)}) %reduce-scatter.6.cloned.1.call-update) | async-done | bytes 983056 | tf_op jit(solution)/shard_map/reduce_scatter | solution.py:567
  432.0 20.1 %all-reduce.11.cloned.1.call-done = f32[1,640,768]{2,1,0:T(8,128)} async-done(((f32[1,640,768]{2,1,0:T(8,128)}), f32[1,640,768]{2,1,0:T(8,128)}) %all-reduce.11.cloned.1.call-update) | async-done | bytes 1966096 | tf_op jit(solution)/shard_map/psum | solution.py:605
  457.5 29.9 %multiply_reduce_fusion = (f32[6,640]{1,0:T(8,128)S(1)}, f32[6,640,2560]{2,1,0:T(8,128)}) fusion(f32[6,640,2560]{2,1,0:T(8,128)} %get-tuple-element.107, f32[6,640]{1,0:T(8,128)S(1)} %log_add_fusion, bf16[640,6,64]{0,2,1:T(8,128)(2,1)S(1)} %bitcast.320, bf16[2560,6,64]{0,2,1:T(8,128)(2,1)} %bitcast.333), kind=kOutput, calls=%fused_computation.1 | convolution fusion | flops 1287778560 | bytes 81131520 | tf_op jit(solution)/shard_map/while/body/eval_jaxpr/rhd,khd->hrk/dot_general | solution.py:638
  487.5 17.4 %fusion.8 = bf16[6,64,2560]{2,1,0:T(8,128)(2,1)} fusion(bf16[640,6,64]{0,2,1:T(8,128)(2,1)S(1)} %bitcast.321, f32[6,640,2560]{2,1,0:T(8,128)} %get-tuple-element.107, f32[6,640]{1,0:T(8,128)S(1)} %log_add_fusion), kind=kOutput, calls=%fused_computation.17 | convolution fusion | flops 1278935040 | bytes 41794560 | tf_op jit(solution)/shard_map/while/body/eval_jaxpr/hrk,rhd->khd/dot_general | solution.py:632
  509.0 32.1 %multiply_convert_fusion = bf16[6,640,2560]{2,1,0:T(8,128)(2,1)} fusion(f32[6,640,2560]{2,1,0:T(8,128)} %get-tuple-element.109, f32[6,640,2560]{2,1,0:T(8,128)} %get-tuple-element.107, f32[6,640]{1,0:T(8,128)S(1)} %get-tuple-element.108, f32[6,640]{1,0:T(8,128)S(1)} %log_add_fusion), kind=kLoop, calls=%fused_computation | loop fusion | flops 39321600 | bytes 98334720 | tf_op jit(solution)/shard_map/while/body/eval_jaxpr/convert_element_type | solution.py:642
  541.1 11.4 %fusion.7 = bf16[6,64,2560]{2,1,0:T(8,128)(2,1)} fusion(bf16[6,640,2560]{2,1,0:T(8,128)(2,1)} %multiply_convert_fusion, bf16[640,6,32]{0,2,1:T(8,128)(2,1)S(1)} %copy-done.20, bf16[640,6,32]{0,2,1:T(8,128)(2,1)S(1)} %copy-done.19), kind=kOutput, calls=%fused_computation.16 | convolution fusion | flops 1261240320 | bytes 22118400 | tf_op jit(solution)/shard_map/while/body/eval_jaxpr/hrk,rhd->khd/dot_general | solution.py:648
  598.0 11.5 %fusion.43 = f32[1,640,6,64]{1,3,2,0:T(8,128)} fusion(bf16[2560,6,64]{0,2,1:T(8,128)(2,1)} %bitcast.318, bf16[6,640,2560]{2,1,0:T(8,128)(2,1)} %multiply_convert_fusion), kind=kOutput, calls=%fused_computation.79 | convolution fusion | flops 1258536960 | bytes 22609920 | tf_op jit(solution)/shard_map/while/body/eval_jaxpr/hrk,khd->rhd/dot_general | solution.py:644
  609.5 25.4 %reduce-scatter.8.cloned.1.call-done = bf16[1,640,768]{2,1,0:T(8,128)(2,1)} async-done(((bf16[1,2560,768]{2,1,0:T(8,128)(2,1)}), bf16[1,640,768]{2,1,0:T(8,128)(2,1)}) %reduce-scatter.8.cloned.1.call-update) | async-done | bytes 983056 | tf_op jit(solution)/shard_map/reduce_scatter | solution.py:660
  676.8 42.2 %all-reduce.13.cloned.1.call-done = f32[233472]{0:T(1024)} async-done(((f32[233472]{0:T(1024)}), f32[233472]{0:T(1024)}) %all-reduce.13.cloned.1.call-update) | async-done | bytes 933904
  720.2 9.8 %all-gather.4 = f32[4,1,29184]{2,1,0:T(1,128)S(1)} all-gather(f32[1,1,29184]{2,1,0:T(1,128)S(1)} %reshape.1187), channel_id=5, replica_groups=mesh['fsdp'=4,'context'=4,'tensor'=2] {'fsdp'}, dimensions={0}, use_global_device_ids=true | all-gather | bytes 583680 | tf_op jit(solution)/shard_map/all_gather | solution.py:751
  731.5 11.6 %all-reduce.15.cloned.1.call-done = (bf16[1,640,768]{2,1,0:T(8,128)(2,1)}, bf16[1,640,768]{2,1,0:T(8,128)(2,1)}) async-done(((bf16[1,640,768]{2,1,0:T(8,128)(2,1)}, bf16[1,640,768]{2,1,0:T(8,128)(2,1)}), (bf16[1,640,768]{2,1,0:T(8,128)(2,1)}, bf16[1,640,768]{2,1,0:T(8,128)(2,1)})) %all-reduce.15.cloned.1.call-update) | async-done | bytes 1966096 | tf_op jit(solution)/shard_map/psum | solution.py:570
  (352 shorter events, 193.4 us)
Async XLA Ops:
  7.2 44.7 %all-gather.13.cloned.1.call-start = ((), (), s32[]{:S(2)}) async-start(), calls=%async_computation.3 | async-start | bytes 2211840 | tf_op jit(solution)/shard_map/all_gather | solution.py:419
  7.9 96.3 %all-gather.15.cloned.1.call-start = ((), (), s32[]{:S(2)}) async-start(), calls=%async_computation.4 | async-start | bytes 2457600 | tf_op jit(solution)/shard_map/all_gather | solution.py:493
  13.6 35.0 %copy-start.4 = (bf16[1,640,768]{2,1,0:T(8,128)(2,1)S(1)}, bf16[1,640,768]{2,1,0:T(8,128)(2,1)}, u32[]{:S(2)}) copy-start(bf16[1,640,768]{2,1,0:T(8,128)(2,1)} %param.16) | copy-start | bytes 2949124
  60.3 88.8 %all-gather.21.cloned.1.call-start = ((), (), s32[]{:S(2)}) async-start(), calls=%async_computation.12 | async-start | bytes 2457600 | tf_op jit(solution)/shard_map/all_gather | solution.py:494
  62.4 103.2 %copy-start.40 = (bf16[16,768]{1,0:T(8,128)(2,1)}, bf16[16,768]{1,0:T(8,128)(2,1)S(1)}, u32[]{:S(2)}) copy-start(bf16[16,768]{1,0:T(8,128)(2,1)S(1)} %reshape.1143) | copy-start | bytes 73732
  73.6 91.2 %copy-start.12 = (bf16[384,768]{0,1:T(8,128)(2,1)}, bf16[384,768]{0,1:T(8,128)(2,1)S(1)}, u32[]{:S(2)}) copy-start(bf16[384,768]{0,1:T(8,128)(2,1)S(1)} %all_gather.33) | copy-start | bytes 1769476
  73.9 30.4 %copy-start.18 = (bf16[640,6,32]{0,2,1:T(8,128)(2,1)S(1)}, bf16[640,6,32]{0,2,1:T(8,128)(2,1)}, u32[]{:S(2)}) copy-start(bf16[640,6,32]{0,2,1:T(8,128)(2,1)} %get-tuple-element.82) | copy-start | bytes 737284
  77.8 110.1 %all-reduce.9.cloned.1.call-start = ((), (), s32[]{:S(2)}) async-start(), calls=%async_computation.5 | async-start | bytes 3932160 | tf_op jit(solution)/shard_map/psum | solution.py:529
  167.9 73.7 %all-gather.25.cloned.1.call-start = ((), (), s32[]{:S(2)}) async-start(), calls=%async_computation.14 | async-start | bytes 4915200 | tf_op jit(solution)/shard_map/all_gather | solution.py:557
  168.5 125.5 %all-gather.23.cloned.1.call-start = ((), (), s32[]{:S(2)}) async-start(), calls=%async_computation.13 | async-start | bytes 4915200 | tf_op jit(solution)/shard_map/all_gather | solution.py:558
  191.3 158.4 %all-gather.19.cloned.1.call-start = ((), (), s32[]{:S(2)}) async-start(), calls=%async_computation.7 | async-start | bytes 1966080 | tf_op jit(solution)/shard_map/all_gather | solution.py:422
  192.0 181.0 %all-gather.17.cloned.1.call-start = ((), (), s32[]{:S(2)}) async-start(), calls=%async_computation.6 | async-start | bytes 3932160 | tf_op jit(solution)/shard_map/all_gather | solution.py:421
  194.3 232.6 %reduce-scatter.6.cloned.1.call-start = ((), (), s32[]{:S(2)}) async-start(), calls=%async_computation.9 | async-start | bytes 4915200 | tf_op jit(solution)/shard_map/reduce_scatter | solution.py:567
  339.4 112.8 %all-reduce.11.cloned.1.call-start = ((), (), s32[]{:S(2)}) async-start(), calls=%async_computation.10 | async-start | bytes 3932160 | tf_op jit(solution)/shard_map/psum | solution.py:605
  349.7 30.4 %copy-start.46 = (f32[16,640]{1,0:T(8,128)}, f32[16,640]{1,0:T(8,128)S(1)}, u32[]{:S(2)}) copy-start(f32[16,640]{1,0:T(8,128)S(1)} %convolution_multiply_fusion.9) | copy-start | bytes 122884
  385.4 41.5 %copy-start.38 = (f32[2,16,640]{2,1,0:T(8,128)}, f32[2,16,640]{2,1,0:T(8,128)S(1)}, u32[]{:S(2)}) copy-start(f32[2,16,640]{2,1,0:T(8,128)S(1)} %convolution_multiply_fusion.4) | copy-start | bytes 245764
  431.0 160.9 %reduce-scatter.4.cloned.1.call-start = ((), (), s32[]{:S(2)}) async-start(), calls=%async_computation.8 | async-start | bytes 4915200 | tf_op jit(solution)/shard_map/reduce_scatter | solution.py:566
  432.0 202.9 %reduce-scatter.8.cloned.1.call-start = ((), (), s32[]{:S(2)}) async-start(), calls=%async_computation.11 | async-start | bytes 4915200 | tf_op jit(solution)/shard_map/reduce_scatter | solution.py:660
  509.0 32.1 %copy-start.19 = (bf16[640,6,32]{0,2,1:T(8,128)(2,1)S(1)}, bf16[640,6,32]{0,2,1:T(8,128)(2,1)}, u32[]{:S(2)}) copy-start(bf16[640,6,32]{0,2,1:T(8,128)(2,1)} %get-tuple-element.82) | copy-start | bytes 737284
  509.0 32.1 %copy-start.20 = (bf16[640,6,32]{0,2,1:T(8,128)(2,1)S(1)}, bf16[640,6,32]{0,2,1:T(8,128)(2,1)}, u32[]{:S(2)}) copy-start(bf16[640,6,32]{0,2,1:T(8,128)(2,1)} %get-tuple-element.83) | copy-start | bytes 737284
  560.9 158.2 %all-reduce.13.cloned.1.call-start = ((), (), s32[]{:S(2)}) async-start(), calls=%async_computation.15 | async-start | bytes 1867776
  609.5 30.3 %copy-start.28 = (f32[640,32]{0,1:T(8,128)S(1)}, f32[640,32]{0,1:T(8,128)}, u32[]{:S(2)}) copy-start(f32[640,32]{0,1:T(8,128)} %copy-done.27) | copy-start | bytes 245764
  661.2 81.9 %all-reduce.15.cloned.1.call-start = ((), (), s32[]{:S(2)}) async-start(), calls=%async_computation.16 | async-start | bytes 3932160 | tf_op jit(solution)/shard_map/psum | solution.py:570
  666.8 76.3 %copy-start.59 = (f32[768]{0:T(1024)S(1)}, f32[768]{0:T(1024)}, u32[]{:S(2)}) copy-start(f32[768]{0:T(1024)} %copy-done.57) | copy-start | bytes 9220
  (64 other events, 418.0 us)
Sparse Core Ops, SparseCore 0:
  9.8 41.9 all-gather.12
  60.4 43.8 all-gather.14
  106.4 42.6 all-gather.20
  168.0 19.8 all-reduce.8
  189.7 51.7 all-gather.24
  243.4 50.5 all-gather.22
  295.9 30.9 all-gather.18
  328.9 44.0 all-gather.16
  376.4 50.4 reduce-scatter.5
  431.1 20.9 all-reduce.10
  455.2 51.6 reduce-scatter.3
  561.0 73.8 reduce-scatter.7
  661.3 57.6 all-reduce.12
  722.0 21.0 all-reduce.14

commit v3 on v2

--- a/solution.py
+++ b/solution.py
@@ -300,6 +300,1207 @@
         device_id=device,
         device_id_type=MESH,
     )
+
+
+def flip(index, bit):
+    return index + (1 - 2 * lax.rem(index // (1 << bit), 2)) * (1 << bit)
+
+
+def split_rows(count):
+    first = (count // 2 + 15) // 16 * 16
+    return ((0, first), (first, count - first))
+
+
+class Gather:
+    def __init__(self, bits, me, device_of, own, buf, stride, base, count, send_sems, recv_sems):
+        self.stages = [[] for _ in range(bits)]
+        self.arrived = [[] for _ in range(bits)]
+        number = 0
+        for half, (offset, size) in enumerate(split_rows(count)):
+            held = [me]
+            for stage in range(bits):
+                bit = (stage + half) % bits
+                for block in held:
+                    rows = self.rows(block * stride + base + offset, size)
+                    source = own.at[self.rows(base + offset, size)] if block is me else buf.at[rows]
+                    self.stages[stage].append(
+                        send(
+                            source,
+                            buf.at[rows],
+                            send_sems.at[number],
+                            recv_sems.at[number],
+                            device_of(flip(me, bit)),
+                        )
+                    )
+                    self.arrived[stage].append(
+                        self.rows(flip(block, bit) * stride + base + offset, size)
+                    )
+                    number = number + 1
+                held = held + [flip(block, bit) for block in held]
+
+    @staticmethod
+    def rows(start, size):
+        return pl.ds(pl.multiple_of(start, 16), size)
+
+    def start(self, stage):
+        for copy in self.stages[stage]:
+            copy.start()
+
+    def wait(self, stage):
+        for copy in self.stages[stage]:
+            copy.wait_recv()
+
+    def finish(self):
+        for stage in self.stages:
+            for copy in stage:
+                copy.wait_send()
+
+
+def turn(values, cosine, sinus):
+    lane = lax.broadcasted_iota(jnp.int32, values.shape, 1)
+    first = lax.rem(lane, HEAD_DIM) < HEAD_DIM // 2
+    swapped = jnp.where(
+        first,
+        pltpu.roll(values, 128 - HEAD_DIM // 2, 1),
+        pltpu.roll(values, HEAD_DIM // 2, 1),
+    )
+    return values * cosine + swapped * sinus
+
+
+def two_parts(values):
+    high = values.astype(jnp.bfloat16)
+    low = (values - high.astype(jnp.float32)).astype(jnp.bfloat16)
+    return jnp.concatenate([high, low], axis=1)
+
+
+def normed(values, gain):
+    scale = lax.rsqrt(jnp.mean(values * values, axis=-1, keepdims=True) + epsilon)
+    return (values * scale * gain).astype(jnp.bfloat16)
+
+
+def fill_bias(bias, hot_rows, reach_t, key_start, query_start):
+    seen = nn_dot(hot_rows, reach_t)
+    keys = key_start + lax.broadcasted_iota(jnp.int32, seen.shape, 0)
+    queries = query_start + lax.broadcasted_iota(jnp.int32, seen.shape, 1)
+    bias[...] = jnp.where((seen > 0.5) & (keys <= queries), 0.0, masked_score)
+
+
+def head_half(shape, axis, odd):
+    index = lax.broadcasted_iota(jnp.int32, shape, axis)
+    return (index >= HEAD_DIM) if odd else (index < HEAD_DIM)
+
+
+def forward_kernel(
+    sizes,
+    x_in,
+    g_in,
+    wq_in,
+    wo_in,
+    gu_in,
+    dn_in,
+    gains,
+    cosine,
+    sinus,
+    hot,
+    reach_t,
+    a_qkv,
+    b_qkv2,
+    a_o,
+    b_o2,
+    a_gu,
+    b_gu2,
+    a_gu_t2,
+    a_dn,
+    a_dn_t2,
+    b_dn2,
+    n1_all,
+    k_all,
+    v_all,
+    wq_all,
+    wo_all,
+    n2_all,
+    g_all,
+    q_t,
+    q_n,
+    mixed,
+    o_t,
+    lse,
+    resid,
+    shared_half,
+    dn2_half,
+    da_gu,
+    db_gu,
+    da_dn,
+    db_dn,
+    x_buf,
+    wq,
+    wo,
+    gu,
+    dn,
+    g_own,
+    n1_buf,
+    k_buf,
+    v_buf,
+    v_t,
+    peak,
+    total,
+    bias,
+    part_out,
+    part_in,
+    n2_own,
+    shared,
+    dn2,
+    shared_in,
+    dn2_in,
+    fs_send,
+    fs_recv,
+    z_send,
+    z_recv,
+    core_send,
+    core_recv,
+    local_sems,
+    chunk_sems,
+):
+    fsdp, contexts, _ = sizes
+    bits = fsdp.bit_length() - 1
+    f, c, t = place_of()
+    rows = x_in.shape[0]
+    half = rows // 2
+    heads = q_t.shape[0] // HEAD_DIM
+    width = q_t.shape[0]
+    units = dn_in.shape[1]
+    own_n = wq_in.shape[0]
+    sibling = (f, c, 1 - t)
+
+    def peer(index):
+        return (index, c, t)
+
+    greet(
+        [peer(flip(f, bit)) for bit in range(bits)]
+        + [sibling, (f, lax.rem(c + 1, contexts), t), (f, lax.rem(c + contexts - 1, contexts), t)]
+    )
+
+    def half_rows(chunk, part):
+        return pl.ds(pl.multiple_of(chunk * rows + part * half, 16), half)
+
+    def up(chunk, source):
+        return send(
+            source,
+            x_buf.at[half_rows(chunk, t)],
+            z_send.at[chunk],
+            z_recv.at[chunk],
+            (f, c + 1, t),
+        )
+
+    def across(chunk):
+        block = x_buf.at[half_rows(chunk, t)]
+        return send(block, block, core_send.at[chunk], core_recv.at[chunk], sibling)
+
+    @pl.when(c < contexts - 1)
+    def _():
+        up(c, x_in.at[half_rows(0, t)]).start()
+
+    gathers = []
+    for i, (own, buf) in enumerate(((wq_in, wq), (wo_in, wo), (gu_in, gu), (dn_in, dn))):
+        gathers.append(
+            Gather(bits, f, peer, own, buf, own_n, 0, own_n, fs_send.at[i], fs_recv.at[i])
+        )
+    g_gather = Gather(
+        bits, f, peer, g_in, g_all, rows, t * half, half, fs_send.at[4], fs_recv.at[4]
+    )
+    n2_gather = Gather(
+        bits, f, peer, n2_own, n2_all, rows, t * half, half, fs_send.at[5], fs_recv.at[5]
+    )
+    wq_gather, wo_gather, gu_gather, dn_gather = gathers
+    wq_gather.start(0)
+    locals_ = [pltpu.make_async_copy(x_in, x_buf.at[pl.ds(c * rows, rows)], local_sems.at[0])]
+    for i, (own, buf) in enumerate(((wq_in, wq), (wo_in, wo), (gu_in, gu), (dn_in, dn))):
+        locals_.append(
+            pltpu.make_async_copy(own, buf.at[pl.ds(f * own_n, own_n)], local_sems.at[1 + i])
+        )
+    locals_.append(pltpu.make_async_copy(g_in, g_own, local_sems.at[5]))
+    locals_.append(
+        pltpu.make_async_copy(g_in, g_all.at[pl.ds(f * rows, rows)], local_sems.at[6])
+    )
+    for copy in locals_:
+        copy.start()
+
+    o_t[...] = jnp.zeros_like(o_t)
+    peak[...] = jnp.full_like(peak, masked_score)
+    total[...] = jnp.zeros_like(total)
+    da_gu[...] = jnp.zeros_like(da_gu)
+    db_gu[...] = jnp.zeros_like(db_gu)
+    da_dn[...] = jnp.zeros_like(da_dn)
+    db_dn[...] = jnp.zeros_like(db_dn)
+    gain_one = gains[0:1, :]
+    gain_two = gains[1:2, :]
+
+    def receive(step):
+        chunk = c - step
+
+        @pl.when(step <= c)
+        def _():
+            up(chunk, x_buf.at[half_rows(chunk, t)]).wait_recv()
+
+            @pl.when(c < contexts - 1)
+            def _():
+                up(chunk, x_buf.at[half_rows(chunk, t)]).start()
+
+            across(chunk).start()
+
+    def chunk_rows(chunk):
+        return pl.ds(pl.multiple_of(chunk * rows, 16), rows)
+
+    def out_copies(chunk):
+        block = chunk_rows(chunk)
+        return [
+            pltpu.make_async_copy(n1_buf.at[block], n1_all.at[block], chunk_sems.at[0, chunk]),
+            pltpu.make_async_copy(k_buf.at[block], k_all.at[block], chunk_sems.at[1, chunk]),
+            pltpu.make_async_copy(v_buf.at[block], v_all.at[block], chunk_sems.at[2, chunk]),
+        ]
+
+    def project(chunk, own):
+        block = chunk_rows(chunk)
+        n1 = normed(x_buf[block, :].astype(jnp.float32), gain_one)
+        n1_buf[block, :] = n1
+        rank = two_parts(nn_dot(n1, a_qkv[...]))
+        cos_rows = cosine[block, :]
+        sin_rows = sinus[block, :]
+        for p in range(width // 128):
+            cols = slice(width + 128 * p, width + 128 * p + 128)
+            key = nn_dot(n1, wq[:, cols]) + nn_dot(rank, b_qkv2[:, cols])
+            k_buf[block, 128 * p : 128 * p + 128] = turn(key, cos_rows, sin_rows).astype(
+                jnp.bfloat16
+            )
+            cols = slice(2 * width + 128 * p, 2 * width + 128 * p + 128)
+            value = nn_dot(n1, wq[:, cols]) + nn_dot(rank, b_qkv2[:, cols])
+            v_buf[block, 128 * p : 128 * p + 128] = value.astype(jnp.bfloat16)
+            v_t[128 * p : 128 * p + 128, :] = value.T.astype(jnp.bfloat16)
+            if own:
+                cols = slice(128 * p, 128 * p + 128)
+                query = nn_dot(n1, wq[:, cols]) + nn_dot(rank, b_qkv2[:, cols])
+                query = turn(query, cos_rows, sin_rows) * 0.125
+                q_n[:, cols] = query.astype(jnp.bfloat16)
+                q_t[cols, :] = query.T.astype(jnp.bfloat16)
+        for copy in out_copies(chunk):
+            copy.start()
+
+    def attend(chunk):
+        block = chunk_rows(chunk)
+        fill_bias(bias, hot[block, :], reach_t[...], chunk * rows, c * rows)
+
+        def pair_step(p, carry):
+            lanes = pl.ds(pl.multiple_of(p * 128, 128), 128)
+            keys = k_buf[block, lanes]
+            query = q_t[lanes, :]
+            for odd in range(2):
+                h = 2 * p + odd
+                alone = jnp.where(
+                    head_half(query.shape, 0, odd), query, jnp.zeros_like(query)
+                )
+                scores = nn_dot(keys, alone) + bias[...]
+                before = peak[pl.ds(h, 1), :]
+                now = jnp.maximum(before, jnp.max(scores, axis=0, keepdims=True))
+                weights = jnp.exp(scores - now)
+                shrink = jnp.exp(before - now)
+                peak[pl.ds(h, 1), :] = now
+                total[pl.ds(h, 1), :] = total[pl.ds(h, 1), :] * shrink + jnp.sum(
+                    weights, axis=0, keepdims=True
+                )
+                head = pl.ds(pl.multiple_of(h * HEAD_DIM, HEAD_DIM), HEAD_DIM)
+                o_t[head, :] = o_t[head, :] * shrink + nn_dot(
+                    v_t[head, :], weights.astype(jnp.bfloat16)
+                )
+            return carry
+
+        lax.fori_loop(0, heads // 2, pair_step, 0)
+
+    receive(1)
+    wq_gather.wait(0)
+    for stage in range(1, bits):
+        wq_gather.start(stage)
+        if stage == 1:
+            wo_gather.start(0)
+        wq_gather.wait(stage)
+    wo_gather.wait(0)
+    for stage in range(1, bits):
+        wo_gather.start(stage)
+        if stage == 1:
+            gu_gather.start(0)
+        if stage < bits - 1:
+            wo_gather.wait(stage)
+    locals_[0].wait()
+    locals_[1].wait()
+    wq_out = pltpu.make_async_copy(wq, wq_all, local_sems.at[10])
+    wq_out.start()
+    project(c, True)
+    attend(c)
+
+    def between(step):
+        if step == 1:
+            gu_gather.wait(0)
+            for stage in range(1, bits):
+                gu_gather.start(stage)
+                if stage == 1:
+                    dn_gather.start(0)
+                if stage < bits - 1:
+                    gu_gather.wait(stage)
+        if step == 2:
+            dn_gather.wait(0)
+            for stage in range(1, bits):
+                dn_gather.start(stage)
+                if stage == 1:
+                    g_gather.start(0)
+                if stage < bits - 1:
+                    dn_gather.wait(stage)
+
+    def later(step):
+        chunk = c - step
+
+        @pl.when(step <= c)
+        def _():
+            across(chunk).wait_recv()
+            project(chunk, False)
+            attend(chunk)
+
+    for step in range(1, 3):
+        receive(step + 1)
+        between(step)
+        later(step)
+
+    def rest(step, carry):
+        receive(step + 1)
+        later(step)
+        return carry
+
+    lax.fori_loop(3, contexts, rest, 0)
+
+    for h in range(heads):
+        head = slice(h * HEAD_DIM, h * HEAD_DIM + HEAD_DIM)
+        o_t[head, :] = o_t[head, :] / total[h : h + 1, :]
+    lse[...] = peak[...] + jnp.log(total[...])
+    for p in range(width // 128):
+        mixed[:, 128 * p : 128 * p + 128] = o_t[128 * p : 128 * p + 128, :].T.astype(jnp.bfloat16)
+    wo_gather.wait(bits - 1)
+    locals_[2].wait()
+    wo_out = pltpu.make_async_copy(wo, wo_all, local_sems.at[11])
+    wo_out.start()
+
+    def local_rows(part):
+        return pl.ds(pl.multiple_of(part * half, 16), half)
+
+    mine = local_rows(t)
+    theirs = local_rows(1 - t)
+
+    def branch(block):
+        values = mixed[block, :]
+        rank = two_parts(nn_dot(values, a_o[...]))
+        return nt_dot(values, wo[...]) + nn_dot(rank, b_o2[...])
+
+    part_out[...] = branch(theirs)
+    number = contexts
+    part_copy = send(
+        part_out, part_in, core_send.at[number], core_recv.at[number], sibling
+    )
+    part_copy.start()
+    own_part = branch(mine) + x_in_rows(x_buf, c, rows, t, half)
+    part_copy.wait_recv()
+    resid_half = own_part + part_in[...]
+    resid[mine, :] = resid_half
+    n2_own[mine, :] = normed(resid_half, gain_two)
+    n2_gather.start(0)
+    n2_copy = send(
+        n2_own.at[mine], n2_own.at[mine], core_send.at[number + 1], core_recv.at[number + 1], sibling
+    )
+    n2_copy.start()
+    resid_copy = send(
+        resid.at[mine], resid.at[mine], core_send.at[number + 2], core_recv.at[number + 2], sibling
+    )
+    resid_copy.start()
+
+    def forwards(gather, buf, first):
+        copies = []
+        for stage in range(bits):
+            group = []
+            for block in gather.arrived[stage]:
+                index = first + len(copies)
+                copies.append(
+                    send(
+                        buf.at[block],
+                        buf.at[block],
+                        core_send.at[index],
+                        core_recv.at[index],
+                        sibling,
+                    )
+                )
+        return copies
+
+    per_stage = [len(stage) for stage in g_gather.arrived]
+    g_forward = forwards(g_gather, g_all, number + 5)
+    n2_forward = forwards(n2_gather, n2_all, number + 5 + sum(per_stage))
+
+    def pass_on(copies, stage):
+        start = sum(per_stage[:stage])
+        for copy in copies[start : start + per_stage[stage]]:
+            copy.start()
+
+    locals_[5].wait()
+    gu_gather.wait(bits - 1)
+    locals_[3].wait()
+    dn_gather.wait(bits - 1)
+    locals_[4].wait()
+
+    def shared_tile(block):
+        inputs = n2_own[block, :]
+        grads = g_own[block, :]
+        rank = nn_dot(inputs, a_gu[...])
+        rank2 = two_parts(rank)
+        gate = nn_dot(inputs, gu[:, :units]) + nn_dot(rank2, b_gu2[:, :units])
+        up_pre = nn_dot(inputs, gu[:, units:]) + nn_dot(rank2, b_gu2[:, units:])
+        sigmoid_gate = jax.nn.sigmoid(gate)
+        silu = gate * sigmoid_gate
+        hidden = (silu * up_pre).astype(jnp.bfloat16)
+        down_rank = nn_dot(hidden, a_dn[...])
+        shared[block, :] = nt_dot(hidden, dn[...]) + nn_dot(two_parts(down_rank), b_dn2[...])
+        down_back = nt_dot(grads, b_dn2[0:RANK, :])
+        grad_hidden = nn_dot(grads, dn[...]) + nn_dot(two_parts(down_back), a_dn_t2[...])
+        grad_gate = (
+            grad_hidden * up_pre * sigmoid_gate * (1.0 + gate * (1.0 - sigmoid_gate))
+        ).astype(jnp.bfloat16)
+        grad_up = (grad_hidden * silu).astype(jnp.bfloat16)
+        rank_back = nt_dot(grad_gate, b_gu2[0 : 2 * RANK, :units]) + nt_dot(
+            grad_up, b_gu2[0 : 2 * RANK, units:]
+        )
+        dn2[block, :] = (
+            nt_dot(grad_gate, gu[:, :units])
+            + nt_dot(grad_up, gu[:, units:])
+            + nn_dot(two_parts(rank_back), a_gu_t2[...])
+        )
+        rank_low = rank.astype(jnp.bfloat16)
+        da_gu[...] += tn_dot(rank_back.astype(jnp.bfloat16), inputs)
+        db_gu[0:RANK, :] += 2.0 * tn_dot(rank_low, grad_gate)[0:RANK]
+        db_gu[RANK:, :] += 2.0 * tn_dot(rank_low, grad_up)[RANK:]
+        da_dn[...] += tn_dot(down_back.astype(jnp.bfloat16), hidden)
+        db_dn[...] += 2.0 * tn_dot(down_rank.astype(jnp.bfloat16), grads)
+
+    n2_gather.wait(0)
+    for stage in range(1, bits):
+        n2_gather.start(stage)
+        pass_on(n2_forward, stage - 1)
+        if stage < bits - 1:
+            n2_gather.wait(stage)
+    n2_copy.wait_recv()
+    shared_tile(theirs)
+    pair_copies = [
+        send(
+            source.at[theirs], target, core_send.at[number + 3 + i], core_recv.at[number + 3 + i], sibling
+        )
+        for i, (source, target) in enumerate(((dn2, dn2_in), (shared, shared_in)))
+    ]
+    for copy in pair_copies:
+        copy.start()
+    g_gather.wait(0)
+    for stage in range(1, bits):
+        g_gather.start(stage)
+        pass_on(g_forward, stage - 1)
+        if stage < bits - 1:
+            g_gather.wait(stage)
+    n2_out = pltpu.make_async_copy(n2_own, n2_all.at[pl.ds(f * rows, rows)], local_sems.at[12])
+    n2_out.start()
+    shared_tile(mine)
+    for copy in pair_copies:
+        copy.wait()
+    dn2_half[...] = dn2[mine, :] + dn2_in[...]
+    shared_half[...] = shared[mine, :] + shared_in[...]
+    n2_gather.wait(bits - 1)
+    pass_on(n2_forward, bits - 1)
+    g_gather.wait(bits - 1)
+    pass_on(g_forward, bits - 1)
+    for copy in n2_forward + g_forward:
+        copy.wait()
+    resid_copy.wait()
+    n2_copy.wait_send()
+    part_copy.wait_send()
+    for gather in gathers + [g_gather, n2_gather]:
+        gather.finish()
+    n2_out.wait()
+    wq_out.wait()
+    wo_out.wait()
+    locals_[6].wait()
+
+    @pl.when(c < contexts - 1)
+    def _():
+        up(c, x_in.at[half_rows(0, t)]).wait_send()
+
+    def drain(step, carry):
+        chunk = c - step
+
+        @pl.when(c < contexts - 1)
+        def _():
+            up(chunk, x_buf.at[half_rows(chunk, t)]).wait_send()
+
+        across(chunk).wait_send()
+        return carry
+
+    lax.fori_loop(1, c + 1, drain, 0)
+
+    def drain_out(step, carry):
+        for copy in out_copies(c - step):
+            copy.wait()
+        return carry
+
+    lax.fori_loop(0, c + 1, drain_out, 0)
+
+
+def x_in_rows(x_buf, chunk, rows, part, half):
+    block = pl.ds(pl.multiple_of(chunk * rows + part * half, 16), half)
+    return x_buf[block, :].astype(jnp.float32)
+
+
+def forward_call(sizes, sharded, local):
+    fsdp, contexts, _ = sizes
+    x, g, wq, wo, gu, dn = sharded
+    rows = x.shape[0]
+    tree = rows * contexts
+    width = wo.shape[1]
+    units = dn.shape[1]
+    bf, f32 = jnp.bfloat16, jnp.float32
+    vmem = pl.BlockSpec(memory_space=pltpu.VMEM)
+    hbm = pl.BlockSpec(memory_space=pl.ANY)
+
+    def shape(kind, *dims):
+        return jax.ShapeDtypeStruct(dims, kind)
+
+    moves = 2 * (fsdp - 1)
+    hops = contexts + 5 + 2 * moves
+    return pl.pallas_call(
+        functools.partial(forward_kernel, sizes),
+        in_specs=[hbm] * 6 + [vmem] * len(local),
+        out_specs=[hbm] * 7 + [vmem] * 12,
+        out_shape=[
+            shape(bf, tree, D),
+            shape(bf, tree, width),
+            shape(bf, tree, width),
+            shape(bf, D, 3 * width),
+            shape(bf, D, width),
+            shape(bf, fsdp * rows, D),
+            shape(bf, fsdp * rows, D),
+            shape(bf, width, rows),
+            shape(bf, rows, width),
+            shape(bf, rows, width),
+            shape(f32, width, rows),
+            shape(f32, 8, rows),
+            shape(f32, rows, D),
+            shape(f32, rows // 2, D),
+            shape(f32, rows // 2, D),
+            shape(f32, 2 * RANK, D),
+            shape(f32, 2 * RANK, units),
+            shape(f32, RANK, units),
+            shape(f32, RANK, D),
+        ],
+        scratch_shapes=[
+            pltpu.VMEM((tree, D), bf),
+            pltpu.VMEM((D, 3 * width), bf),
+            pltpu.VMEM((D, width), bf),
+            pltpu.VMEM((D, 2 * units), bf),
+            pltpu.VMEM((D, units), bf),
+            pltpu.VMEM((rows, D), bf),
+            pltpu.VMEM((tree, D), bf),
+            pltpu.VMEM((tree, width), bf),
+            pltpu.VMEM((tree, width), bf),
+            pltpu.VMEM((width, rows), bf),
+            pltpu.VMEM((8, rows), f32),
+            pltpu.VMEM((8, rows), f32),
+            pltpu.VMEM((rows, rows), f32),
+            pltpu.VMEM((rows // 2, D), f32),
+            pltpu.VMEM((rows // 2, D), f32),
+            pltpu.VMEM((rows, D), bf),
+            pltpu.VMEM((rows, D), f32),
+            pltpu.VMEM((rows, D), f32),
+            pltpu.VMEM((rows // 2, D), f32),
+            pltpu.VMEM((rows // 2, D), f32),
+            pltpu.SemaphoreType.DMA((6, moves)),
+            pltpu.SemaphoreType.DMA((6, moves)),
+            pltpu.SemaphoreType.DMA((contexts,)),
+            pltpu.SemaphoreType.DMA((contexts,)),
+            pltpu.SemaphoreType.DMA((hops,)),
+            pltpu.SemaphoreType.DMA((hops,)),
+            pltpu.SemaphoreType.DMA((13,)),
+            pltpu.SemaphoreType.DMA((3, contexts)),
+        ],
+        name="forward",
+        compiler_params=pltpu.CompilerParams(
+            collective_id=2, has_side_effects=True, vmem_limit_bytes=62 << 20
+        ),
+    )(*sharded, *local)
+
+
+def flips(index, mask, bits):
+    for bit in range(bits):
+        if mask >> bit & 1:
+            index = flip(index, bit)
+    return index
+
+
+class Scatter:
+    def __init__(self, bits, me, device_of, work, inbox, count, send_sems, recv_sems):
+        self.bits, self.work, self.inbox = bits, work, inbox
+        self.copies = [[] for _ in range(bits)]
+        self.adds = [[] for _ in range(bits)]
+        number = 0
+        for half, (offset, size) in enumerate(split_rows(count)):
+            alive = list(range(1 << bits))
+            slot = 0
+            for stage in range(bits):
+                bit = (stage + half) % bits
+                for mask in alive:
+                    if mask >> bit & 1:
+                        source = Gather.rows(flips(me, mask, bits) * count + offset, size)
+                        target = pl.ds(slot * count + offset, size)
+                        kept = Gather.rows(flips(me, mask ^ (1 << bit), bits) * count + offset, size)
+                        self.copies[stage].append(
+                            send(
+                                work.at[source],
+                                inbox.at[target],
+                                send_sems.at[number],
+                                recv_sems.at[number],
+                                device_of(flip(me, bit)),
+                            )
+                        )
+                        self.adds[stage].append((kept, target, pl.ds(offset, size)))
+                        number = number + 1
+                        slot = slot + 1
+                alive = [mask for mask in alive if not mask >> bit & 1]
+
+    def start(self, stage):
+        for copy in self.copies[stage]:
+            copy.start()
+
+    def add(self, stage):
+        for copy in self.copies[stage]:
+            copy.wait_recv()
+        for kept, target, _ in self.adds[stage]:
+            total = self.work[kept, :].astype(jnp.float32) + self.inbox[target, :].astype(
+                jnp.float32
+            )
+            self.work[kept, :] = total.astype(jnp.bfloat16)
+
+    def last(self, out, own):
+        for copy in self.copies[self.bits - 1]:
+            copy.wait_recv()
+        for kept, target, rows in self.adds[self.bits - 1]:
+            total = self.work[kept, :].astype(jnp.float32) + self.inbox[target, :].astype(
+                jnp.float32
+            )
+            out[rows, :] = (total + own[rows, :]).astype(jnp.bfloat16)
+
+    def finish(self):
+        for stage in self.copies:
+            for copy in stage:
+                copy.wait_send()
+
+
+def backward_kernel(
+    sizes,
+    moe_out,
+    moe_back,
+    n1_hbm,
+    k_hbm,
+    v_hbm,
+    wq_hbm,
+    wo_hbm,
+    cos_hbm,
+    sin_hbm,
+    x_in,
+    g_in,
+    gains,
+    hot,
+    reach_t,
+    resid,
+    shared_half,
+    dn2_half,
+    q_t,
+    q_n,
+    mixed,
+    o_t,
+    lse,
+    a_qkv,
+    b_qkv2,
+    a_qkv_t2,
+    a_o,
+    a_o_t2,
+    b_o2,
+    block_out,
+    input_grad,
+    da_qkv,
+    db_qkv,
+    da_o,
+    db_o,
+    cosine,
+    sinus,
+    n1_buf,
+    k_buf,
+    v_buf,
+    wq,
+    wo,
+    work_back,
+    pair_back,
+    inbox_back,
+    work_out,
+    pair_out,
+    inbox_out,
+    total_half,
+    total_full,
+    ffn_half,
+    ffn_full,
+    dy,
+    do_n,
+    do_t,
+    delta,
+    k_t,
+    dq_t,
+    grad_kv,
+    bias,
+    part,
+    part_out,
+    part_in,
+    z_in,
+    z_out,
+    dn1_full,
+    fs_send,
+    fs_recv,
+    z_send,
+    z_recv,
+    core_send,
+    core_recv,
+    pair_send,
+    pair_recv,
+    local_sems,
+    chunk_sems,
+):
+    fsdp, contexts, _ = sizes
+    bits = fsdp.bit_length() - 1
+    f, c, t = place_of()
+    rows = x_in.shape[0]
+    half = rows // 2
+    width = q_t.shape[0]
+    heads = width // HEAD_DIM
+    sibling = (f, c, 1 - t)
+    f32, bf = jnp.float32, jnp.bfloat16
+
+    def peer(index):
+        return (index, c, t)
+
+    def local_rows(part_index):
+        return pl.ds(pl.multiple_of(part_index * half, 16), half)
+
+    mine = local_rows(t)
+    theirs = local_rows(1 - t)
+
+    def block_rows(block, part_index):
+        return pl.ds(pl.multiple_of(block * rows + part_index * half, 16), half)
+
+    def work_rows(block):
+        return pl.ds(pl.multiple_of(block * half, 16), half)
+
+    masks = list(range(fsdp - 1, -1, -1))
+
+    def exchange(source, work, inbox, which):
+        own, sent = [], []
+        for mask in masks:
+            block = flips(f, mask, bits)
+            own.append(
+                pltpu.make_async_copy(
+                    source.at[block_rows(block, t)],
+                    work.at[work_rows(block)],
+                    local_sems.at[which, mask],
+                )
+            )
+            sent.append(
+                send(
+                    source.at[block_rows(block, 1 - t)],
+                    inbox.at[work_rows(block)],
+                    core_send.at[which, mask],
+                    core_recv.at[which, mask],
+                    sibling,
+                )
+            )
+        return own, sent
+
+    back_own, back_sent = exchange(moe_back, work_back, pair_back, 0)
+    out_own, out_sent = exchange(moe_out, work_out, pair_out, 1)
+    for copy in back_own:
+        copy.start()
+    wo_copy = pltpu.make_async_copy(wo_hbm, wo, local_sems.at[2, 0])
+    wq_copy = pltpu.make_async_copy(wq_hbm, wq, local_sems.at[2, 1])
+    wo_copy.start()
+    greet(
+        [peer(flip(f, bit)) for bit in range(bits)]
+        + [sibling, (f, lax.rem(c + 1, contexts), t), (f, lax.rem(c + contexts - 1, contexts), t)]
+    )
+    for copy in back_sent:
+        copy.start()
+    for copy in out_own:
+        copy.start()
+    wq_copy.start()
+
+    def chunk_rows(chunk):
+        return pl.ds(pl.multiple_of(chunk * rows, 16), rows)
+
+    def loads(chunk):
+        block = chunk_rows(chunk)
+        return [
+            pltpu.make_async_copy(k_hbm.at[block], k_buf.at[block], chunk_sems.at[1, chunk]),
+            pltpu.make_async_copy(v_hbm.at[block], v_buf.at[block], chunk_sems.at[2, chunk]),
+        ]
+
+    def n1_load(chunk):
+        return pltpu.make_async_copy(
+            n1_hbm.at[chunk_rows(chunk)], n1_buf, chunk_sems.at[0, chunk]
+        )
+
+    def table_loads(chunk):
+        block = chunk_rows(chunk)
+        return [
+            pltpu.make_async_copy(cos_hbm.at[block], cosine, chunk_sems.at[3, chunk]),
+            pltpu.make_async_copy(sin_hbm.at[block], sinus, chunk_sems.at[4, chunk]),
+        ]
+
+    def start_loads(chunk, carry):
+        for copy in loads(chunk):
+            copy.start()
+        return carry
+
+    lax.fori_loop(0, c + 1, start_loads, 0)
+
+    back = Scatter(
+        bits, f, peer, work_back, inbox_back, half, fs_send.at[0], fs_recv.at[0]
+    )
+    out = Scatter(bits, f, peer, work_out, inbox_out, half, fs_send.at[1], fs_recv.at[1])
+
+    def pair_sum(own, sent, work, inbox):
+        for i, mask in enumerate(masks):
+            block = work_rows(flips(f, mask, bits))
+            own[i].wait()
+            sent[i].wait_recv()
+            work[block, :] = (
+                work[block, :].astype(f32) + inbox[block, :].astype(f32)
+            ).astype(bf)
+
+    pair_sum(back_own, back_sent, work_back, pair_back)
+    back.start(0)
+    for copy in out_sent:
+        copy.start()
+    for stage in range(1, bits):
+        back.add(stage - 1)
+        back.start(stage)
+    dq_t[...] = jnp.zeros_like(dq_t)
+    da_qkv[...] = jnp.zeros_like(da_qkv)
+    db_qkv[...] = jnp.zeros_like(db_qkv)
+    pair_sum(out_own, out_sent, work_out, pair_out)
+    back.last(total_half, dn2_half)
+    out.start(0)
+    total_full[mine, :] = total_half[...]
+    full_copy = send(
+        total_half, total_full.at[mine], core_send.at[2, 0], core_recv.at[2, 0], sibling
+    )
+    full_copy.start()
+    gain_one = gains[0:1, :]
+    gain_two = gains[1:2, :]
+    wo_copy.wait()
+    full_copy.wait_recv()
+
+    def attn_tile(i, carry):
+        block = local_rows(i)
+        values = resid[block, :]
+        gradient = g_in[block, :].astype(f32) + norm_back(
+            values, rms_scale(values), gain_two, total_full[block, :].astype(f32)
+        )
+        dy[block, :] = gradient
+        low_grad = gradient.astype(bf)
+        rank_back = nt_dot(low_grad, b_o2[0:RANK, :])
+        do_n[block, :] = (
+            nn_dot(low_grad, wo[...]) + nn_dot(two_parts(rank_back), a_o_t2[...])
+        ).astype(bf)
+        values_o = mixed[block, :]
+        rank = nn_dot(values_o, a_o[...])
+        first = tn_dot(rank_back.astype(bf), values_o)
+        second = 2.0 * tn_dot(rank.astype(bf), low_grad)
+
+        @pl.when(i == 0)
+        def _():
+            da_o[...] = first
+            db_o[...] = second
+
+        @pl.when(i > 0)
+        def _():
+            da_o[...] += first
+            db_o[...] += second
+
+        return carry
+
+    lax.fori_loop(0, 2, attn_tile, 0)
+    for p in range(width // 128):
+        lanes = slice(128 * p, 128 * p + 128)
+        turned = do_n[:, lanes].astype(f32).T
+        do_t[lanes, :] = turned.astype(bf)
+        product = turned * o_t[lanes, :]
+        for odd in range(2):
+            delta[2 * p + odd : 2 * p + odd + 1, :] = jnp.sum(
+                product[HEAD_DIM * odd : HEAD_DIM * odd + HEAD_DIM, :], axis=0, keepdims=True
+            )
+    wq_copy.wait()
+
+    def attend_back(chunk):
+        block = chunk_rows(chunk)
+        n1_load(chunk).start()
+        for copy in table_loads(chunk):
+            copy.start()
+        for copy in loads(chunk) + table_loads(chunk):
+            copy.wait()
+        fill_bias(bias, hot[block, :], reach_t[...], chunk * rows, c * rows)
+        cos_rows = cosine[...]
+        sin_rows = -sinus[...]
+        for p in range(width // 128):
+            lanes = slice(128 * p, 128 * p + 128)
+            k_t[lanes, :] = k_buf[block, lanes].astype(f32).T.astype(bf)
+
+        def pair_step(p, carry):
+            lanes = pl.ds(pl.multiple_of(p * 128, 128), 128)
+            keys = k_buf[block, lanes]
+            values = v_buf[block, lanes]
+            query_t = q_t[lanes, :]
+            grad_t = do_t[lanes, :]
+            query = q_n[:, lanes]
+            grad = do_n[:, lanes]
+            grad_keys = jnp.zeros((rows, 128), f32)
+            grad_values = jnp.zeros((rows, 128), f32)
+            for odd in range(2):
+                h = 2 * p + odd
+                upper = head_half(query_t.shape, 0, odd)
+                side = head_half(query.shape, 1, odd)
+                none_t = jnp.zeros_like(query_t)
+                none = jnp.zeros_like(query)
+                scores = nn_dot(keys, jnp.where(upper, query_t, none_t)) + bias[...]
+                weights = jnp.exp(scores - lse[pl.ds(h, 1), :])
+                grad_weights = nn_dot(values, jnp.where(upper, grad_t, none_t))
+                grad_scores = (weights * (grad_weights - delta[pl.ds(h, 1), :])).astype(bf)
+                grad_values += nn_dot(weights.astype(bf), jnp.where(side, grad, none))
+                grad_keys += nn_dot(grad_scores, jnp.where(side, query, none))
+                head = pl.ds(pl.multiple_of(h * HEAD_DIM, HEAD_DIM), HEAD_DIM)
+                dq_t[head, :] += nn_dot(k_t[head, :], grad_scores)
+            grad_kv[:, lanes] = turn(grad_keys, cos_rows, sin_rows).astype(bf)
+            grad_kv[:, pl.ds(pl.multiple_of(width + p * 128, 128), 128)] = grad_values.astype(bf)
+            return carry
+
+        lax.fori_loop(0, heads // 2, pair_step, 0)
+
+    def project_back(chunk, own):
+        block = chunk_rows(chunk)
+        grads = grad_kv[...]
+        result = nt_dot(grads, wq[:, width:])
+        rank_back = nt_dot(grads, b_qkv2[0 : 3 * RANK, width:])
+        n1_load(chunk).wait()
+        n1 = n1_buf[...]
+        rank = nn_dot(n1, a_qkv[...]).astype(bf)
+        both = 2.0 * tn_dot(rank, grads)
+        db_qkv[RANK : 2 * RANK, :] += both[RANK : 2 * RANK, :width]
+        db_qkv[2 * RANK :, :] += both[2 * RANK :, width:]
+        if own:
+            pieces = []
+            for p in range(width // 128):
+                lanes = slice(128 * p, 128 * p + 128)
+                grad_query = (dq_t[lanes, :] * 0.125).T
+                pieces.append(
+                    turn(grad_query, cosine[...], -sinus[...]).astype(bf)
+                )
+            grad_query = jnp.concatenate(pieces, axis=1)
+            result += nt_dot(grad_query, wq[:, :width])
+            rank_back += nt_dot(grad_query, b_qkv2[0 : 3 * RANK, :width])
+            db_qkv[0:RANK, :] += 2.0 * tn_dot(rank, grad_query)[0:RANK, :]
+        result += nn_dot(two_parts(rank_back), a_qkv_t2[...])
+        da_qkv[...] += tn_dot(rank_back.astype(bf), n1)
+        part[...] = result.astype(bf)
+        part_out[work_rows(chunk), :] = part[theirs, :]
+        z_out[work_rows(chunk), :] = part[mine, :]
+
+    def pair_copy(chunk):
+        return send(
+            part_out.at[work_rows(chunk)],
+            part_in.at[work_rows(chunk)],
+            pair_send.at[chunk],
+            pair_recv.at[chunk],
+            sibling,
+        )
+
+    def down(chunk):
+        block = work_rows(chunk)
+        return send(
+            z_out.at[block], z_in.at[block], z_send.at[chunk], z_recv.at[chunk], (f, c - 1, t)
+        )
+
+    def chain(chunk):
+        block = work_rows(chunk)
+        pair_copy(chunk).wait_recv()
+        summed = z_out[block, :].astype(f32) + part_in[block, :].astype(f32)
+        z_out[block, :] = summed.astype(bf)
+
+        @pl.when(c < contexts - 1)
+        def _():
+            down(chunk).wait_recv()
+            z_out[block, :] = (summed + z_in[block, :].astype(f32)).astype(bf)
+
+    def pass_down(chunk):
+        chain(chunk)
+        down(chunk).start()
+
+    def step(chunk, carry):
+        attend_back(chunk)
+        project_back(chunk, False)
+        pair_copy(chunk).start()
+
+        @pl.when(c == contexts - 1)
+        def _():
+            pass_down(chunk)
+
+        @pl.when((c < contexts - 1) & (chunk >= 1))
+        def _():
+            pass_down(chunk - 1)
+
+        return carry
+
+    lax.fori_loop(0, c, step, 0)
+    attend_back(c)
+    project_back(c, True)
+    pair_copy(c).start()
+
+    @pl.when((c < contexts - 1) & (c >= 1))
+    def _():
+        pass_down(c - 1)
+
+    for stage in range(1, bits):
+        out.add(stage - 1)
+        out.start(stage)
+    out.last(ffn_half, shared_half)
+    ffn_full[mine, :] = ffn_half[...]
+    ffn_copy = send(ffn_half, ffn_full.at[mine], core_send.at[2, 1], core_recv.at[2, 1], sibling)
+    ffn_copy.start()
+    chain(c)
+    dn1_full[mine, :] = z_out[work_rows(c), :]
+    dn1_copy = send(
+        z_out.at[work_rows(c)],
+        dn1_full.at[mine],
+        core_send.at[2, 2],
+        core_recv.at[2, 2],
+        sibling,
+    )
+    dn1_copy.start()
+    ffn_copy.wait_recv()
+    block_out[...] = resid[...] + ffn_full[...].astype(f32)
+    dn1_copy.wait_recv()
+
+    def final_tile(i, carry):
+        block = local_rows(i)
+        values = x_in[block, :].astype(f32)
+        input_grad[block, :] = dy[block, :] + norm_back(
+            values, rms_scale(values), gain_one, dn1_full[block, :].astype(f32)
+        )
+        return carry
+
+    lax.fori_loop(0, 2, final_tile, 0)
+    for copy in back_sent + out_sent + [full_copy, ffn_copy, dn1_copy]:
+        copy.wait_send()
+    back.finish()
+    out.finish()
+
+    def drain(chunk, carry):
+        pair_copy(chunk).wait_send()
+
+        @pl.when(chunk < c)
+        def _():
+            down(chunk).wait_send()
+
+        return carry
+
+    lax.fori_loop(0, c + 1, drain, 0)
+
+
+def backward_call(sizes, remote, local):
+    fsdp, contexts, _ = sizes
+    rows = local[0].shape[0]
+    half = rows // 2
+    tree = rows * contexts
+    width = remote[6].shape[1]
+    bf, f32 = jnp.bfloat16, jnp.float32
+    vmem = pl.BlockSpec(memory_space=pltpu.VMEM)
+    hbm = pl.BlockSpec(memory_space=pl.ANY)
+
+    def shape(kind, *dims):
+        return jax.ShapeDtypeStruct(dims, kind)
+
+    moves = 2 * (fsdp - 1)
+    slots = max(fsdp, 4)
+    dma = pltpu.SemaphoreType.DMA
+    return pl.pallas_call(
+        functools.partial(backward_kernel, sizes),
+        in_specs=[hbm] * len(remote) + [vmem] * len(local),
+        out_specs=[vmem] * 6,
+        out_shape=[
+            shape(f32, rows, D),
+            shape(f32, rows, D),
+            shape(f32, 3 * RANK, D),
+            shape(f32, 3 * RANK, width),
+            shape(f32, RANK, width),
+            shape(f32, RANK, D),
+        ],
+        scratch_shapes=[
+            pltpu.VMEM((rows, 128), f32),
+            pltpu.VMEM((rows, 128), f32),
+            pltpu.VMEM((rows, D), bf),
+            pltpu.VMEM((tree, width), bf),
+            pltpu.VMEM((tree, width), bf),
+            pltpu.VMEM((D, 3 * width), bf),
+            pltpu.VMEM((D, width), bf),
+            pltpu.VMEM((fsdp * half, D), bf),
+            pltpu.VMEM((fsdp * half, D), bf),
+            pltpu.VMEM(((fsdp - 1) * half, D), bf),
+            pltpu.VMEM((fsdp * half, D), bf),
+            pltpu.VMEM((fsdp * half, D), bf),
+            pltpu.VMEM(((fsdp - 1) * half, D), bf),
+            pltpu.VMEM((half, D), bf),
+            pltpu.VMEM((rows, D), bf),
+            pltpu.VMEM((half, D), bf),
+            pltpu.VMEM((rows, D), bf),
+            pltpu.VMEM((rows, D), f32),
+            pltpu.VMEM((rows, width), bf),
+            pltpu.VMEM((width, rows), bf),
+            pltpu.VMEM((8, rows), f32),
+            pltpu.VMEM((width, rows), bf),
+            pltpu.VMEM((width, rows), f32),
+            pltpu.VMEM((rows, 2 * width), bf),
+            pltpu.VMEM((rows, rows), f32),
+            pltpu.VMEM((rows, D), bf),
+            pltpu.VMEM((contexts * half, D), bf),
+            pltpu.VMEM((contexts * half, D), bf),
+            pltpu.VMEM((contexts * half, D), bf),
+            pltpu.VMEM((contexts * half, D), bf),
+            pltpu.VMEM((rows, D), bf),
+            dma((2, moves)),
+            dma((2, moves)),
+            dma((contexts,)),
+            dma((contexts,)),
+            dma((3, slots)),
+            dma((3, slots)),
+            dma((contexts,)),
+            dma((contexts,)),
+            dma((3, slots)),
+            dma((5, contexts)),
+        ],
+        name="backward",
+        compiler_params=pltpu.CompilerParams(
+            collective_id=3, has_side_effects=True, vmem_limit_bytes=62 << 20
+        ),
+    )(*remote, *local)
 
 
 def small_kernel(
@@ -415,12 +1616,6 @@
     ff_start = part_index * local_ff
     head_shape = (tree_count, row_count, local_heads, HEAD_DIM)
     wide_shape = (tree_count, tree_len, local_heads, HEAD_DIM)
-    qkv_weight, output_matrix, gu_weight, down_matrix = (
-        lax.all_gather(w_qkv, "fsdp", axis=0, tiled=True),
-        lax.all_gather(w_out, "fsdp", axis=1, tiled=True),
-        lax.all_gather(w_gu, "fsdp", axis=0, tiled=True),
-        lax.all_gather(w_dn, "fsdp", axis=1, tiled=True),
-    )
     sizes = (fsdp_size, contexts, tensors)
     own_adapters = adapters.shape[0]
     own_width = D // fsdp_size
@@ -461,101 +1656,80 @@
     key_hot, key_positions = jax.vmap(locate, in_axes=(None, 0, 0))(key_ids, starts, offsets)
     key_hot = key_hot.astype(jnp.float32)
     query_hot = lax.dynamic_slice_in_dim(key_hot, row_start, row_count, 1)
-    positions = lax.dynamic_slice_in_dim(key_positions, row_start, row_count, 1)
     reach = (jnp.einsum("trs,tsu->tru", query_hot, ancestry_f) > 0.5).astype(jnp.float32)
     visible = (jnp.einsum("tru,tku->trk", reach, key_hot) > 0.5) & (
         key_ids[None, None, :] <= query_ids[None, :, None]
     )
-    cosine, sinus = angles(positions)
-    tokens_f = tokens.astype(jnp.float32)
-    scale_one = rms_scale(tokens_f)
-    normed_one = (tokens_f * scale_one * gain_one.astype(jnp.float32)).astype(jnp.bfloat16)
-    query_key_value_rank = jnp.einsum(
-        "trd,tdm->trm", normed_one, a_qkv.astype(jnp.bfloat16), preferred_element_type=jnp.float32
-    )
-    rank_split = query_key_value_rank.reshape(tree_count, row_count, 3, RANK)
-    projected_rows = jnp.einsum(
-        "trd,djc->trjc", normed_one, qkv_weight, preferred_element_type=jnp.float32
-    )
-    projected_rows = projected_rows + adapter_scale * jnp.einsum(
-        "trjk,tjkc->trjc", rank_split, b_qkv_part, precision=highest_precision
-    )
-    queries = rotate(projected_rows[:, :, 0].reshape(head_shape), cosine, sinus).astype(
-        jnp.bfloat16
-    )
-    key_rows = (
-        rotate(projected_rows[:, :, 1].reshape(head_shape), cosine, sinus)
-        .astype(jnp.bfloat16)
-        .reshape(tree_count, row_count, local_width)
-    )
-    value_rows = projected_rows[:, :, 2].astype(jnp.bfloat16)
-    key_all, value_all = (
-        lax.all_gather(key_rows, "context", axis=1, tiled=True),
-        lax.all_gather(value_rows, "context", axis=1, tiled=True),
-    )
-    key_heads = key_all.reshape(wide_shape)
-    value_heads = value_all.reshape(wide_shape)
-
-    def attend(inputs):
-        query_rows, key_block, value_block, visible_rows = inputs
-        scores = (
-            jnp.einsum("rhd,khd->hrk", query_rows, key_block, preferred_element_type=jnp.float32)
-            * 0.125
-        )
-        scores = jnp.where(visible_rows[None], scores, masked_score)
-        row_max = jnp.max(scores, axis=-1, keepdims=True)
-        weights = jnp.exp(scores - row_max)
-        totals = jnp.sum(weights, axis=-1, keepdims=True)
-        probabilities = (weights / totals).astype(jnp.bfloat16)
-        mixed_block = jnp.einsum(
-            "hrk,khd->rhd", probabilities, value_block, preferred_element_type=jnp.float32
-        )
-        return (mixed_block.astype(jnp.bfloat16), (row_max + jnp.log(totals))[..., 0])
-
-    mixed_heads, log_totals = lax.map(attend, (queries, key_heads, value_heads, visible))
-    mixed_row_values = mixed_heads.reshape(tree_count, row_count, local_width)
-    output_rank_rows = jnp.einsum(
-        "trc,tck->trk",
-        mixed_row_values,
-        a_out_part.astype(jnp.bfloat16),
-        preferred_element_type=jnp.float32,
-    )
-    attention_slice = jnp.einsum(
-        "trc,cd->trd", mixed_row_values, output_matrix, preferred_element_type=jnp.float32
-    )
-    attention_slice = attention_slice + adapter_scale * jnp.einsum(
-        "trk,tkd->trd", output_rank_rows, output_adapter_up, precision=highest_precision
-    )
-    attn_total = lax.psum(attention_slice, "tensor")
-    residual = tokens_f + attn_total
-    scale_two = rms_scale(residual)
-    normed_two = (residual * scale_two * gain_two.astype(jnp.float32)).astype(jnp.bfloat16)
-    gate_up_rank_rows = jnp.einsum(
-        "trd,tdm->trm", normed_two, a_gu.astype(jnp.bfloat16), preferred_element_type=jnp.float32
-    ).reshape(tree_count, row_count, 2, RANK)
-    gate_up_matrix = jnp.einsum(
-        "trd,djf->trjf", normed_two, gu_weight, preferred_element_type=jnp.float32
-    )
-    gate_up_matrix = gate_up_matrix + adapter_scale * jnp.einsum(
-        "trjk,tjkf->trjf", gate_up_rank_rows, b_gu_part, precision=highest_precision
-    )
-    gate_pre = gate_up_matrix[:, :, 0]
-    up_pre = gate_up_matrix[:, :, 1]
-    hidden_state = (silu_of(gate_pre) * up_pre).astype(jnp.bfloat16)
-    down_rank_rows = jnp.einsum(
-        "xbw,xwz->xbz",
-        hidden_state,
-        down_adapter_slice.astype(jnp.bfloat16),
-        preferred_element_type=jnp.float32,
-    )
-    shared_slice = jnp.einsum(
-        "wmg,gh->wmh", hidden_state, down_matrix, preferred_element_type=jnp.float32
-    )
-    shared_slice = shared_slice + adapter_scale * jnp.einsum(
-        "trk,tkd->trd", down_rank_rows, down_adapter_up, precision=highest_precision
-    )
-    cotangent_all = lax.all_gather(cotangent[0], "fsdp", axis=0, tiled=True)
-    normed_all = lax.all_gather(normed_two[0], "fsdp", axis=0, tiled=True)
+    cos_all, sin_all = angles(key_positions)
+    cosine = lax.dynamic_slice_in_dim(cos_all, row_start, row_count, 1)
+    sinus = lax.dynamic_slice_in_dim(sin_all, row_start, row_count, 1)
+    cos_one = cos_all[0, :, 0, :]
+    sin_one = sin_all[0, :, 0, :]
+    cos_table = jnp.concatenate([cos_one] * 4, axis=1)
+    sin_table = jnp.concatenate([-sin_one, sin_one, -sin_one, sin_one], axis=1)
+    pad = 16 - key_hot.shape[2]
+    hot_table = jnp.pad(key_hot[0], ((0, 0), (0, pad))).astype(jnp.bfloat16)
+    reach_t = jnp.pad(reach[0], ((0, 0), (0, pad))).T.astype(jnp.bfloat16)
+
+    def low(values):
+        return values.astype(jnp.bfloat16)
+
+    def blocks(up_rows):
+        count, rank, cols = up_rows.shape
+        out = jnp.zeros((count, rank, count, cols), jnp.float32)
+        for j in range(count):
+            out = out.at[j, :, j].set(up_rows[j])
+        return out.reshape(count * rank, count * cols)
+
+    def twice(values):
+        return low(jnp.concatenate([values, values], axis=0))
+
+    local = (
+        jnp.pad(jnp.stack([gain_one, gain_two]).astype(jnp.float32), ((0, 6), (0, 0))),
+        cos_table,
+        sin_table,
+        hot_table,
+        reach_t,
+        low(a_qkv[0]),
+        twice(2.0 * blocks(b_qkv_part[0])),
+        low(a_out_part[0]),
+        twice(2.0 * output_adapter_up[0]),
+        low(a_gu[0]),
+        twice(2.0 * blocks(b_gu_part[0])),
+        twice(a_gu[0].T),
+        low(down_adapter_slice[0]),
+        twice(down_adapter_slice[0].T),
+        twice(2.0 * down_adapter_up[0]),
+    )
+    sharded = (
+        tokens[0],
+        cotangent[0],
+        w_qkv.reshape(own_width, 3 * local_width),
+        w_out.T,
+        w_gu.reshape(own_width, 2 * local_ff),
+        w_dn.T,
+    )
+    (
+        n1_all,
+        k_all,
+        v_all,
+        wq_all,
+        wo_all,
+        normed_all,
+        cotangent_all,
+        q_t,
+        q_n,
+        mixed_own,
+        o_t,
+        lse,
+        resid,
+        shared_half,
+        dn2_half,
+        da_gu_t,
+        db_gu_own,
+        da_dn_t,
+        db_dn_own,
+    ) = forward_call(sizes, sharded, local)
     own_experts = EXPERTS // fsdp_size
     spans, place, weight = moe_layout(
         routes_all, route_weights_all, lax.axis_index("fsdp") * own_experts, own_experts
@@ -563,177 +1737,39 @@
     moe_all, moe_back_all = moe_call(
         spans, place, weight, normed_all, cotangent_all, w_egu.transpose(0, 2, 1, 3), w_edn
     )
-    moe_part = lax.psum_scatter(moe_all, "fsdp", scatter_dimension=0, tiled=True).astype(jnp.float32)
-    moe_grad = lax.psum_scatter(moe_back_all, "fsdp", scatter_dimension=0, tiled=True).astype(
-        jnp.float32
-    )
-    ffn_total = lax.psum(
-        (shared_slice + moe_part.reshape(tree_count, row_count, D)).astype(jnp.bfloat16), "tensor"
-    ).astype(jnp.float32)
-    block_out = residual + ffn_total
-    output_gradient = cotangent.astype(jnp.float32)
-    grad_hidden = jnp.einsum(
-        "boz,kz->bok", cotangent, down_matrix, preferred_element_type=jnp.float32
-    )
-    down_rank_gradient = adapter_scale * jnp.einsum(
-        "trd,tkd->trk",
-        cotangent,
-        down_adapter_up.astype(jnp.bfloat16),
-        preferred_element_type=jnp.float32,
-    )
-    grad_hidden = grad_hidden + jnp.einsum(
-        "jax,jnx->jan", down_rank_gradient, down_adapter_slice, precision=highest_precision
-    )
-    sigmoid_gate = jax.nn.sigmoid(gate_pre)
-    grad_gate = grad_hidden * up_pre * sigmoid_gate * (1.0 + gate_pre * (1.0 - sigmoid_gate))
-    grad_up = grad_hidden * gate_pre * sigmoid_gate
-    grad_gu = jnp.stack([grad_gate, grad_up], axis=2).astype(jnp.bfloat16)
-    grad_normed_two = jnp.einsum(
-        "trjf,djf->trd", grad_gu, gu_weight, preferred_element_type=jnp.float32
-    )
-    gate_up_rank_gradient = adapter_scale * jnp.einsum(
-        "trjf,tjkf->trjk",
-        grad_gu,
-        b_gu_part.astype(jnp.bfloat16),
-        preferred_element_type=jnp.float32,
-    )
-    rank_gu_flat = gate_up_rank_gradient.reshape(tree_count, row_count, 2 * RANK)
-    grad_normed_two = grad_normed_two + jnp.einsum(
-        "trm,tdm->trd", rank_gu_flat, a_gu, precision=highest_precision
-    )
-    grad_normed_two = grad_normed_two + moe_grad.reshape(tree_count, row_count, D)
-    grad_normed_two = lax.psum(grad_normed_two, "tensor")
-    grad_residual = output_gradient + norm_back(
-        residual, scale_two, gain_two.astype(jnp.float32), grad_normed_two
-    )
-    grad_attn = grad_residual.astype(jnp.bfloat16)
-    grad_mixed = jnp.einsum(
-        "trd,cd->trc", grad_attn, output_matrix, preferred_element_type=jnp.float32
-    )
-    output_rank_gradient = adapter_scale * jnp.einsum(
-        "trd,tkd->trk",
-        grad_attn,
-        output_adapter_up.astype(jnp.bfloat16),
-        preferred_element_type=jnp.float32,
-    )
-    grad_mixed = grad_mixed + jnp.einsum(
-        "trk,tck->trc", output_rank_gradient, a_out_part, precision=highest_precision
-    )
-    grad_mixed_heads = grad_mixed.astype(jnp.bfloat16).reshape(head_shape)
-
-    def attend_back(inputs):
-        query_rows, key_block, value_block, visible_rows, log_total, grad_rows = inputs
-        scores = (
-            jnp.einsum("rhd,khd->hrk", query_rows, key_block, preferred_element_type=jnp.float32)
-            * 0.125
-        )
-        scores = jnp.where(visible_rows[None], scores, masked_score)
-        probabilities = jnp.exp(scores - log_total[..., None])
-        grad_values = jnp.einsum(
-            "hrk,rhd->khd",
-            probabilities.astype(jnp.bfloat16),
-            grad_rows,
-            preferred_element_type=jnp.float32,
-        )
-        grad_probs = jnp.einsum(
-            "rhd,khd->hrk", grad_rows, value_block, preferred_element_type=jnp.float32
-        )
-        inner_sum = jnp.sum(probabilities * grad_probs, axis=-1, keepdims=True)
-        grad_scores = (probabilities * (grad_probs - inner_sum)).astype(jnp.bfloat16)
-        grad_query = (
-            jnp.einsum("hrk,khd->rhd", grad_scores, key_block, preferred_element_type=jnp.float32)
-            * 0.125
-        )
-        grad_keys = (
-            jnp.einsum("hrk,rhd->khd", grad_scores, query_rows, preferred_element_type=jnp.float32)
-            * 0.125
-        )
-        span = key_block.shape[0]
-        return (
-            grad_query,
-            jnp.concatenate([grad_keys.reshape(span, -1), grad_values.reshape(span, -1)], axis=1),
-        )
-
-    grad_query_rot, grad_key_value = lax.map(
-        attend_back, (queries, key_heads, value_heads, visible, log_totals, grad_mixed_heads)
-    )
-    own_grads = lax.psum_scatter(
-        grad_key_value.astype(jnp.bfloat16), "context", scatter_dimension=1, tiled=True
-    ).astype(jnp.float32)
-    grad_query = unrotate(grad_query_rot, cosine, sinus).reshape(tree_count, row_count, local_width)
-    grad_key = unrotate(own_grads[..., :local_width].reshape(head_shape), cosine, sinus).reshape(
-        tree_count, row_count, local_width
-    )
-    grad_qkv = jnp.stack([grad_query, grad_key, own_grads[..., local_width:]], axis=2).astype(
-        jnp.bfloat16
-    )
-    grad_normed_one = jnp.einsum(
-        "trjc,djc->trd", grad_qkv, qkv_weight, preferred_element_type=jnp.float32
-    )
-    query_key_value_rank_gradient = adapter_scale * jnp.einsum(
-        "trjc,tjkc->trjk",
-        grad_qkv,
-        b_qkv_part.astype(jnp.bfloat16),
-        preferred_element_type=jnp.float32,
-    )
-    rank_qkv_flat = query_key_value_rank_gradient.reshape(tree_count, row_count, 3 * RANK)
-    grad_normed_one = grad_normed_one + jnp.einsum(
-        "trm,tdm->trd", rank_qkv_flat, a_qkv, precision=highest_precision
-    )
-    grad_normed_one = lax.psum(grad_normed_one.astype(jnp.bfloat16), "tensor").astype(jnp.float32)
-    input_grad = grad_residual + norm_back(
-        tokens_f, scale_one, gain_one.astype(jnp.float32), grad_normed_one
-    )
-    grad_qkv_f = grad_qkv.astype(jnp.float32)
-    grad_gu_f = grad_gu.astype(jnp.float32)
-    grad_a_qkv = jnp.einsum(
-        "trd,trm->tdm", normed_one.astype(jnp.float32), rank_qkv_flat, precision=highest_precision
-    )
-    query_key_value_gradient_slice = adapter_scale * jnp.einsum(
-        "trjk,trjc->tjkc", rank_split, grad_qkv_f, precision=highest_precision
-    )
+    remote = (moe_all, moe_back_all, n1_all, k_all, v_all, wq_all, wo_all, local[1], local[2])
+    block_out, input_grad, da_qkv_t, db_qkv_own, da_o_t, db_o_own = backward_call(
+        sizes,
+        remote,
+        (tokens[0], cotangent[0])
+        + (local[0], local[3], local[4])
+        + (resid, shared_half, dn2_half, q_t, q_n, mixed_own, o_t, lse)
+        + (local[5], local[6], twice(a_qkv[0].T), local[7], twice(a_out_part[0].T), local[8]),
+    )
+    block_out = block_out[None]
+    input_grad = input_grad[None]
+    grad_a_qkv = da_qkv_t.T[None]
     grad_b_qkv = lax.dynamic_update_slice_in_dim(
         jnp.zeros((tree_count, 3, RANK, D), jnp.float32),
-        query_key_value_gradient_slice,
+        db_qkv_own.reshape(1, 3, RANK, local_width),
         width_start,
         3,
     )
-    grad_a_out_part = jnp.einsum(
-        "trc,trk->tck",
-        mixed_row_values.astype(jnp.float32),
-        output_rank_gradient,
-        precision=highest_precision,
-    )
     grad_a_out = lax.dynamic_update_slice_in_dim(
-        jnp.zeros((tree_count, D, RANK), jnp.float32), grad_a_out_part, width_start, 1
-    )
-    output_adapter_up_gradient = adapter_scale * jnp.einsum(
-        "ags,agh->ash", output_rank_rows, grad_attn.astype(jnp.float32), precision=highest_precision
-    )
-    grad_a_gu = jnp.einsum(
-        "trd,trm->tdm", normed_two.astype(jnp.float32), rank_gu_flat, precision=highest_precision
-    )
-    gate_up_adapter_gradient_slice = adapter_scale * jnp.einsum(
-        "trjk,trjf->tjkf", gate_up_rank_rows, grad_gu_f, precision=highest_precision
-    )
+        jnp.zeros((tree_count, D, RANK), jnp.float32), da_o_t.T[None], width_start, 1
+    )
+    output_adapter_up_gradient = db_o_own[None]
+    grad_a_gu = da_gu_t.T[None]
     grad_b_gu = lax.dynamic_update_slice_in_dim(
         jnp.zeros((tree_count, 2, RANK, FF), jnp.float32),
-        gate_up_adapter_gradient_slice,
+        db_gu_own.reshape(1, 2, RANK, local_ff),
         ff_start,
         3,
     )
-    grad_a_dn_part = jnp.einsum(
-        "uya,uye->uae",
-        hidden_state.astype(jnp.float32),
-        down_rank_gradient,
-        precision=highest_precision,
-    )
     grad_a_dn = lax.dynamic_update_slice_in_dim(
-        jnp.zeros((tree_count, FF, RANK), jnp.float32), grad_a_dn_part, ff_start, 1
-    )
-    down_adapter_up_gradient = adapter_scale * jnp.einsum(
-        "ags,agh->ash", down_rank_rows, output_gradient, precision=highest_precision
-    )
+        jnp.zeros((tree_count, FF, RANK), jnp.float32), da_dn_t.T[None], ff_start, 1
+    )
+    down_adapter_up_gradient = db_dn_own[None]
     grad_pieces = [
         grad_a_qkv,
         grad_b_qkv,

time: 766 us -> 471 us (0.61)
  waiting for transfers between devices: 297 us -> 61.4 us
  Pallas kernels: 72.6 us -> 299 us
  matrix products: 173 us -> 0.4 us
  other arithmetic: 89 us -> 30.7 us
  local copies, waits for them, and re-layouts: 78 us -> 42.9 us
  blocking collectives: 27.4 us -> 15.7 us
    pallas_call x0 -> x2, Pallas kernels: none -> 232 us  [the longest x1 118 us: forward_call(): pl.pallas_call(functools.partial(forward_kernel, sizes), in_specs=[hbm] *...]
    dot_general x39 -> x1, matrix products: 172 us -> 0.13 us  [shards(): jnp.einsum('trs,tsu->tru', query_hot, ancestry_f) > 0.5]
    all_gather x7 -> x0, waiting for transfers between devices: 139 us -> none  [the longest x1 52.4 us: shards(): normed_all = lax.all_gather(normed_two[0], 'fsdp', axis=0, tiled=True)]
    reduce_scatter x3 -> x0, waiting for transfers between devices: 63.1 us -> none  [the longest x1 37.7 us: shards(): lax.psum_scatter(moe_back_all, 'fsdp', scatter_dimension=0, tiled=True)]
    psum x3 -> x0, waiting for transfers between devices: 51 us -> none  [the longest x1 20.1 us: shards(): grad_normed_two = lax.psum(grad_normed_two, 'tensor')]
    convert_element_type x4 -> x1, other arithmetic: 37.6 us -> 0.61 us  [shards(): reach_t = jnp.pad(reach[0], ((0, 0), (0, pad))).T.astype(jnp.bfloat16)]
    reduce_sum x5 -> x0, other arithmetic: 22.3 us -> none  [the longest x1 16.2 us: attend(): totals = jnp.sum(weights, axis=-1, keepdims=True)]
    unnamed x15 -> x2, waiting for transfers between devices: 44.3 us -> 61.4 us
  transfers between devices with their start and end apart: 14 -> 1, of which waited for: 12 -> 1; matrix products, arithmetic and copies ran while one was open for 36% -> 0% of each run, Pallas kernels for 10% -> 0%
where the time goes in v3:
time: 471 us; the launch traced here: 467 us
  Pallas kernels  299 us (63%)
  waiting for transfers between devices  61.4 us (13%)
  local copies, waits for them, and re-layouts  42.9 us (9%)
  other arithmetic  30.7 us (7%)
  between operations  16.7 us (4%)
  blocking collectives  15.7 us (3%)
    pallas_call x1, Pallas kernels, forward_call(): pl.pallas_call(functools.partial(forward_kernel, sizes), in_specs=[hbm] *...  118 us
    pallas_call x1, Pallas kernels, backward_call(): pl.pallas_call(functools.partial(backward_kernel, sizes), in_specs=[hbm]...  114 us
    unnamed x2, waiting for transfers between devices  61.4 us
    pallas_call x1, Pallas kernels, moe_call(): pl.pallas_call(moe_kernel, grid_spec=pltpu.PrefetchScalarGridSpec(num_sca...  45.3 us
    pallas_call x1, Pallas kernels, small_call(): pl.pallas_call(functools.partial(small_kernel, sizes), in_specs=[pl.Block...  21.8 us
    unnamed x102, local copies, waits for them, and re-layouts  19.1 us
    all_gather x1, blocking collectives, shards(): part_all = lax.all_gather(own_part[None], 'fsdp', axis=0, tiled=True)  9.81 us
  transfers between devices with their start and end apart: 1, of which 1 were waited for; matrix products, arithmetic and copies ran while one was open for 0% of the time, Pallas kernels for 0%

profile of v3, /device:TPU:0, one launch (start us, length us, event | category | flops | bytes accessed | tf_op | source)
XLA Modules:
  0.0 466.9 jit_solution(6207349206040287375)
XLA Ops:
  7.9 1.8 reshape.771.adapters_ref
  13.1 21.8 %small_gather.1 = (bf16[2,4,16,1824]{3,2,1,0:T(8,128)(2,1)}, bf16[4,16,384]{2,1,0:T(8,128)(2,1)}, f32[4,8,640]{2,1,0:T(8,128)}) custom-call(s32[1]{0:T(128)S(6)} %copy.236.ids_ref, bf16[32,1824]{1,0:T(8,128)(2,1)} %reshape.771.adapters_ref, bf16[16,384]{1,0:T(8,128)(2,1)} %broadcast_in_dim.40.gains_ref, f32[8,640]{1,0:T(8,128)} %maximum_maximum_fusion.table_ref), custom_call_target="tpu_custom_call" | custom-call | tf_op jit(solution)/shard_map/small_gather/pallas_call | solution.py:1564
  34.9 1.1 convert_bitcast_fusion
  36.1 1.4 reshape.793
  40.6 1.0 fusion.3
  44.0 1.2 convert_convert_fusion
  49.9 1.5 copy.173
  64.1 2.3 copy.200
  66.3 1.8 copy.199
  69.8 7.5 %copy.214 = bf16[2,768,2,1024]{3,1,2,0:T(8,128)(2,1)} copy(bf16[2,768,2,1024]{3,2,1,0:T(2,128)(2,1)} %param.33) | data formatting | bytes 12582912 | tf_op args[7]
  78.7 4.6 fusion.2
  85.5 1.2 bitcast_select_fusion
  87.4 3.6 pad_maximum_fusion
  90.9 118.1 %forward.1 = (bf16[2560,768]{1,0:T(8,128)(2,1)}, bf16[2560,384]{1,0:T(8,128)(2,1)}, bf16[2560,384]{1,0:T(8,128)(2,1)}, bf16[768,1152]{1,0:T(8,128)(2,1)}, bf16[7...) custom-call(bf16[640,768]{1,0:T(8,128)(2,1)} %bitcast.122, ...), custom_call_target="tpu_custom_call" | custom-call | tf_op jit(solution)/shard_map/forward/pallas_call | solution.py:876
  209.0 45.3 %experts.1 = (bf16[2560,768]{1,0:T(8,128)(2,1)}, bf16[2560,768]{1,0:T(8,128)(2,1)}) custom-call(s32[2,21]{1,0:T(2,128)} %pad_add_fusion.1.spans, s32[2,1,2560]{2,1,0:T(1,128)} %copy_select_fusion.place_row, f32[2,1,2560]{2,1,0:T(1,128)} %broadcast_in_dim.45.weight_row, s32[2560,2]{1,0:T(8,128)} %bitcast.120, f32[2560,2]{1,0:T(8,128)} %bitcast.121, ...), custom_call_target="tpu_custom_call" | custom-call | tf_op jit(solution)/shard_map/experts/pallas_call | solution.py:256
  254.3 114.0 %backward.1 = (f32[640,768]{1,0:T(8,128)}, f32[640,768]{1,0:T(8,128)}, f32[48,768]{1,0:T(8,128)}, f32[48,384]{1,0:T(8,128)}, f32[16,384]{1,0:T(8,128)}, /*index=5*/f32[16,768]{1,0:T(8,128)}) custom-call(bf16[2560,768]{1,0:T(8,128)(2,1)} %get-tuple-element.98.moe_out, bf16[2560,768]{1,0:T(8,128)(2,1)} %get-tuple-element.99.moe_back, ...), custom_call_target="tpu_custom_call" | custom-call | tf_op jit(solution)/shard_map/backward/pallas_call | solution.py:1444
  368.3 1.1 copy.190
  375.1 5.9 %all-reduce.6 = s32[4]{0:T(128)S(1)} all-reduce(s32[4]{0:T(128)S(1)} %dynamic-update-slice.15), channel_id=1, replica_groups=mesh['fsdp'=4,'context'=4,'tensor'=2] {'fsdp'}, use_global_device_ids=true, to_apply=%add.6 | all-reduce | flops 4 | bytes 32
  382.3 61.4 %all-reduce.10.cloned.1.call-done = f32[233472]{0:T(1024)} async-done(((f32[233472]{0:T(1024)}), f32[233472]{0:T(1024)}) %all-reduce.10.cloned.1.call-update) | async-done | bytes 933904
  443.7 1.0 dynamic-slice.35
  444.8 9.8 %all-gather.1 = f32[4,1,29184]{2,1,0:T(1,128)S(1)} all-gather(f32[1,1,29184]{2,1,0:T(1,128)S(1)} %reshape.811), channel_id=2, replica_groups=mesh['fsdp'=4,'context'=4,'tensor'=2] {'fsdp'}, dimensions={0}, use_global_device_ids=true | all-gather | bytes 583680 | tf_op jit(solution)/shard_map/all_gather | solution.py:1787
  454.7 1.4 multiply_reduce_fusion
  456.1 1.3 copy.237
  458.4 1.3 copy.238
  (209 shorter events, 39.1 us)
Async XLA Ops:
  7.2 436.5 %all-reduce.10.cloned.1.call-start = ((), (), s32[]{:S(2)}) async-start(), calls=%async_computation | async-start | bytes 1867776
  36.1 6.4 %copy-start.32 = (s32[1,13]{1,0:T(1,128)S(1)}, s32[1,13]{1,0:T(1,128)}, u32[]{:S(2)}) copy-start(s32[1,13]{1,0:T(1,128)} %param.38) | copy-start | bytes 160
  37.5 9.0 %copy-start = (f32[1,233472]{1,0:T(1,128)}, f32[1,233472]{1,0:T(1,128)S(1)}, u32[]{:S(2)}) copy-start(f32[1,233472]{1,0:T(1,128)S(1)} %reshape.793) | copy-start | bytes 2801668
  37.5 8.8 %copy-start.26 = (f32[4,8,640]{2,1,0:T(8,128)S(1)}, f32[4,8,640]{2,1,0:T(8,128)}, u32[]{:S(2)}) copy-start(f32[4,8,640]{2,1,0:T(8,128)} %get-tuple-element.93) | copy-start | bytes 245764
  48.7 3.3 slice-start
  52.6 3.1 copy-start.16
  52.7 4.5 copy-start.5
  52.7 4.1 copy-start.9
  55.9 5.3 %copy-start.8 = (bf16[36864]{0:T(1024)(128)(2,1)S(1)}, bf16[36864]{0:T(1024)(128)(2,1)}, u32[]{:S(2)}) copy-start(bf16[36864]{0:T(1024)(128)(2,1)} %fusion.3) | copy-start | bytes 221188
  55.9 5.4 %copy-start.10 = (bf16[24576]{0:T(1024)(128)(2,1)S(1)}, bf16[24576]{0:T(1024)(128)(2,1)}, u32[]{:S(2)}) copy-start(bf16[24576]{0:T(1024)(128)(2,1)} %fusion.5) | copy-start | bytes 147460
  57.2 5.2 %copy-start.14 = (bf16[12288]{0:T(1024)(128)(2,1)S(1)}, bf16[12288]{0:T(1024)(128)(2,1)}, u32[]{:S(2)}) copy-start(bf16[12288]{0:T(1024)(128)(2,1)} %get-tuple-element.123) | copy-start | bytes 73732
  59.6 6.7 %copy-start.7 = (bf16[32,768]{1,0:T(8,128)(2,1)}, bf16[32,768]{1,0:T(8,128)(2,1)S(1)}, u32[]{:S(2)}) copy-start(bf16[32,768]{1,0:T(8,128)(2,1)S(1)} %constant_dynamic-update-slice_fusion.2.b_o2) | copy-start | bytes 147460
  61.4 16.5 %copy-start.1 = (bf16[768,48]{1,0:T(8,128)(2,1)}, bf16[768,48]{1,0:T(8,128)(2,1)S(1)}, u32[]{:S(2)}) copy-start(bf16[768,48]{1,0:T(8,128)(2,1)S(1)} %reshape.798.a_qkv) | copy-start | bytes 221188
  61.5 6.6 %copy-start.4 = (bf16[768,32]{1,0:T(8,128)(2,1)}, bf16[768,32]{1,0:T(8,128)(2,1)S(1)}, u32[]{:S(2)}) copy-start(bf16[768,32]{1,0:T(8,128)(2,1)S(1)} %reshape.800.a_gu) | copy-start | bytes 147460
  62.3 5.8 %copy-start.15 = (s32[2,20,128]{2,1,0:T(8,128)S(1)}, s32[2,20,128]{2,1,0:T(8,128)}, u32[]{:S(2)}) copy-start(s32[2,20,128]{2,1,0:T(8,128)} %get-tuple-element.130) | copy-start | bytes 61444
  62.4 6.2 %copy-start.31 = (s32[10]{0:T(128)S(1)}, s32[10]{0:T(128)}, u32[]{:S(2)}) copy-start(s32[10]{0:T(128)} %broadcast_add_fusion.3) | copy-start | bytes 124
  63.0 6.1 %copy-start.30 = (s32[10]{0:T(128)S(1)}, s32[10]{0:T(128)}, u32[]{:S(2)}) copy-start(s32[10]{0:T(128)} %iota_multiply_fusion) | copy-start | bytes 124
  69.7 7.5 %copy-start.13 = (bf16[1,384,16]{1,2,0:T(8,128)(2,1)S(1)}, bf16[1,384,16]{1,2,0:T(8,128)(2,1)}, u32[]{:S(2)}) copy-start(bf16[1,384,16]{1,2,0:T(8,128)(2,1)} %copy-done.12) | copy-start | bytes 36868
  69.7 8.9 %copy-start.23 = (s32[2560]{0:T(1024)S(1)}, s32[2560]{0:T(1024)}, u32[]{:S(2)}) copy-start(s32[2560]{0:T(1024)} %get-tuple-element.127) | copy-start | bytes 30724
  69.7 8.9 %copy-start.24 = (s32[2560]{0:T(1024)S(1)}, s32[2560]{0:T(1024)}, u32[]{:S(2)}) copy-start(s32[2560]{0:T(1024)} %get-tuple-element.128) | copy-start | bytes 30724
  69.8 8.9 %copy-start.29 = (f32[32]{0:T(128)S(1)}, f32[32]{0:T(128)}, u32[]{:S(2)}) copy-start(f32[32]{0:T(128)} %multiply_power_fusion) | copy-start | bytes 388
  372.5 8.4 %copy-start.35 = (u32[32]{0:T(128)S(1)}, u32[32]{0:T(128)}, u32[]{:S(2)}) copy-start(u32[32]{0:T(128)} %constant.253) | copy-start | bytes 388
  382.3 73.8 %copy-start.3 = (f32[640,768]{1,0:T(8,128)S(1)}, f32[640,768]{1,0:T(8,128)}, u32[]{:S(2)}) copy-start(f32[640,768]{1,0:T(8,128)} %get-tuple-element.113) | copy-start | bytes 5898244
  456.1 2.3 copy-start.2
  (16 other events, 20.0 us)
Sparse Core Ops, SparseCore 0:
  373.8 69.7 all-reduce.9

commit v4 on v3

--- a/solution.py
+++ b/solution.py
@@ -315,6 +315,7 @@
     def __init__(self, bits, me, device_of, own, buf, stride, base, count, send_sems, recv_sems):
         self.stages = [[] for _ in range(bits)]
         self.arrived = [[] for _ in range(bits)]
+        self.passed = [[] for _ in range(bits)]
         number = 0
         for half, (offset, size) in enumerate(split_rows(count)):
             held = [me]
@@ -323,6 +324,7 @@
                 for block in held:
                     rows = self.rows(block * stride + base + offset, size)
                     source = own.at[self.rows(base + offset, size)] if block is me else buf.at[rows]
+                    self.passed[stage].append(block is not me)
                     self.stages[stage].append(
                         send(
                             source,
@@ -343,8 +345,15 @@
         return pl.ds(pl.multiple_of(start, 16), size)
 
     def start(self, stage):
-        for copy in self.stages[stage]:
-            copy.start()
+        if stage == 0:
+            for copies, passed in zip(self.stages, self.passed):
+                for copy, later in zip(copies, passed):
+                    if not later:
+                        copy.start()
+        else:
+            for copy, later in zip(self.stages[stage], self.passed[stage]):
+                if later:
+                    copy.start()
 
     def wait(self, stage):
         for copy in self.stages[stage]:
@@ -615,20 +624,19 @@
 
         lax.fori_loop(0, heads // 2, pair_step, 0)
 
+    def advance(gather, following):
+        gather.wait(0)
+        for stage in range(1, bits):
+            gather.start(stage)
+            if stage < bits - 1:
+                gather.wait(stage)
+        if following is not None:
+            following.start(0)
+
+    advance(wq_gather, wo_gather)
     receive(1)
-    wq_gather.wait(0)
-    for stage in range(1, bits):
-        wq_gather.start(stage)
-        if stage == 1:
-            wo_gather.start(0)
-        wq_gather.wait(stage)
-    wo_gather.wait(0)
-    for stage in range(1, bits):
-        wo_gather.start(stage)
-        if stage == 1:
-            gu_gather.start(0)
-        if stage < bits - 1:
-            wo_gather.wait(stage)
+    advance(wo_gather, gu_gather)
+    wq_gather.wait(bits - 1)
     locals_[0].wait()
     locals_[1].wait()
     wq_out = pltpu.make_async_copy(wq, wq_all, local_sems.at[10])
@@ -638,21 +646,9 @@
 
     def between(step):
         if step == 1:
-            gu_gather.wait(0)
-            for stage in range(1, bits):
-                gu_gather.start(stage)
-                if stage == 1:
-                    dn_gather.start(0)
-                if stage < bits - 1:
-                    gu_gather.wait(stage)
+            advance(gu_gather, dn_gather)
         if step == 2:
-            dn_gather.wait(0)
-            for stage in range(1, bits):
-                dn_gather.start(stage)
-                if stage == 1:
-                    g_gather.start(0)
-                if stage < bits - 1:
-                    dn_gather.wait(stage)
+            advance(dn_gather, g_gather)
 
     def later(step):
         chunk = c - step
@@ -1503,6 +1499,83 @@
     )(*remote, *local)
 
 
+def reduce_kernel(
+    sizes, packed, table_all, out, inbox, z_out, z_in, total, f_in, send_sems, recv_sems
+):
+    fsdp, contexts, _ = sizes
+    f, c, t = place_of()
+    f32, bf = jnp.float32, jnp.bfloat16
+    peers = [(lax.rem(f + k, fsdp), c, t) for k in range(1, fsdp)]
+    stacked = [(f, lax.rem(c + k, contexts), t) for k in range(1, contexts)]
+    sibling = (f, c, 1 - t)
+    greet(peers + stacked + [sibling])
+    order = [lax.rem(c + k, contexts) for k in range(1, contexts)] + [c]
+    pair = []
+    for k, block in enumerate(order):
+        copy = send(
+            packed.at[block, 1 - t], inbox.at[block], send_sems.at[0, k], recv_sems.at[0, k], sibling
+        )
+        copy.start()
+        pair.append(copy)
+    across = []
+    for k, other in enumerate(stacked):
+        pair[k].wait_recv()
+        z_out[k] = (packed[order[k], t] + inbox[order[k]]).astype(bf)
+        copy = send(z_out.at[k], z_in.at[k], send_sems.at[1, k], recv_sems.at[1, k], other)
+        copy.start()
+        across.append(copy)
+    pair[-1].wait_recv()
+    result = packed[c, t] + inbox[c]
+    for k, copy in enumerate(across):
+        copy.wait_recv()
+        result = result + z_in[k].astype(f32)
+    total[...] = result.astype(bf)
+    ends = []
+    for k, peer in enumerate(peers):
+        copy = send(total, f_in.at[k], send_sems.at[2, k], recv_sems.at[2, k], peer)
+        copy.start()
+        ends.append(copy)
+    own = ADAPTERS // fsdp
+    wanted = [(f * own + a).astype(f32) for a in range(own)]
+    sums = [jnp.where(table_all[f, 4:5, 0:1] == w, total[...].astype(f32), 0.0) for w in wanted]
+    for k, copy in enumerate(ends):
+        copy.wait_recv()
+        tree = table_all[lax.rem(f - k - 1 + fsdp, fsdp), 4:5, 0:1]
+        block = f_in[k].astype(f32)
+        sums = [s + jnp.where(tree == w, block, 0.0) for s, w in zip(sums, wanted)]
+    for a in range(own):
+        out[a] = sums[a]
+    for copy in pair + across + ends:
+        copy.wait_send()
+
+
+def reduce_call(sizes, packed, table_all):
+    fsdp, contexts, _ = sizes
+    block = packed.shape[2:]
+    vmem = pl.BlockSpec(memory_space=pltpu.VMEM)
+    bf, f32 = jnp.bfloat16, jnp.float32
+    slots = max(fsdp, contexts)
+    return pl.pallas_call(
+        functools.partial(reduce_kernel, sizes),
+        in_specs=[vmem, vmem],
+        out_specs=vmem,
+        out_shape=jax.ShapeDtypeStruct((ADAPTERS // fsdp,) + block, f32),
+        scratch_shapes=[
+            pltpu.VMEM((contexts,) + block, f32),
+            pltpu.VMEM((contexts - 1,) + block, bf),
+            pltpu.VMEM((contexts - 1,) + block, bf),
+            pltpu.VMEM(block, bf),
+            pltpu.VMEM((fsdp - 1,) + block, bf),
+            pltpu.SemaphoreType.DMA((3, slots)),
+            pltpu.SemaphoreType.DMA((3, slots)),
+        ],
+        name="adapter_sums",
+        compiler_params=pltpu.CompilerParams(
+            collective_id=4, has_side_effects=True, vmem_limit_bytes=60 << 20
+        ),
+    )(packed, table_all)
+
+
 def small_kernel(
     sizes,
     ids_ref,
@@ -1624,7 +1697,8 @@
         [
             routes[0].astype(jnp.float32).T,
             route_weights[0].astype(jnp.float32).T,
-            jnp.zeros((4, row_count), jnp.float32),
+            jnp.broadcast_to(adapter_ids.astype(jnp.float32)[:, None], (1, row_count)),
+            jnp.zeros((3, row_count), jnp.float32),
         ]
     )
     chosen_parts, gains_all, table_all = small_call(
@@ -1781,15 +1855,9 @@
         down_adapter_up_gradient,
     ]
     packed = jnp.concatenate([piece.reshape(tree_count, -1) for piece in grad_pieces], axis=1)
-    own_part = lax.psum_scatter(
-        packed[0], ("context", "tensor"), scatter_dimension=0, tiled=True
-    )
-    part_all = lax.all_gather(own_part[None], "fsdp", axis=0, tiled=True)
-    ids_all = lax.all_gather(adapter_ids, "fsdp", axis=0, tiled=True)
-    rows_own = ADAPTERS // fsdp_size
-    own_ids = lax.axis_index("fsdp") * rows_own + jnp.arange(rows_own, dtype=jnp.int32)
-    own_hot = (own_ids[:, None] == ids_all[None, :]).astype(jnp.float32)
-    adapter_grads = jnp.sum(own_hot[:, :, None] * part_all[None], axis=1)
+    adapter_grads = reduce_call(
+        sizes, packed[0].reshape(contexts, tensors, RANK, -1), table_all
+    ).reshape(own_adapters, -1)
     return (block_out, input_grad, adapter_grads)
 
 

time: 471 us -> 390 us (0.83)
  waiting for transfers between devices: 61.4 us -> 0 us
  other arithmetic: 30.7 us -> 46.9 us
  blocking collectives: 15.7 us -> 0 us
  between operations: 16.7 us -> 2.26 us
  local copies, waits for them, and re-layouts: 42.9 us -> 37.4 us
    unnamed x2 -> x0, waiting for transfers between devices: 61.4 us -> none
    pallas_call x0 -> x1, Pallas kernels: none -> 30.2 us  [reduce_call(): pl.pallas_call(functools.partial(reduce_kernel, sizes), in_specs=[vmem, v...]
    pallas_call x1, Pallas kernels: 114 us -> 98.5 us  [backward_call(): pl.pallas_call(functools.partial(backward_kernel, sizes), in_specs=[hbm]...]
    pallas_call x1, Pallas kernels: 118 us -> 104 us  [forward_call(): pl.pallas_call(functools.partial(forward_kernel, sizes), in_specs=[hbm] *...]
    another operation x6, other arithmetic: 3.02 us -> 16.5 us
    all_gather x1 -> x0, blocking collectives: 9.81 us -> none  [shards(): part_all = lax.all_gather(own_part[None], 'fsdp', axis=0, tiled=True)]
    concatenate x0 -> x1, other arithmetic: none -> 8.38 us  [shards(): jnp.concatenate([piece.reshape(tree_count, -1) for piece in grad_pieces],...]
    unnamed x1 -> x0, blocking collectives: 5.89 us -> none
  transfers between devices with their start and end apart: 1 -> 0, of which waited for: 1 -> 0; matrix products, arithmetic and copies ran while one was open for 0% -> 0% of each run, Pallas kernels for 0% -> 0%
where the time goes in v4:
time: 390 us; the launch traced here: 387 us
  Pallas kernels  300 us (77%)
  other arithmetic  46.9 us (12%)
  local copies, waits for them, and re-layouts  37.4 us (10%)
    pallas_call x1, Pallas kernels, forward_call(): pl.pallas_call(functools.partial(forward_kernel, sizes), in_specs=[hbm] *...  104 us
    pallas_call x1, Pallas kernels, backward_call(): pl.pallas_call(functools.partial(backward_kernel, sizes), in_specs=[hbm]...  98.5 us
    pallas_call x1, Pallas kernels, moe_call(): pl.pallas_call(moe_kernel, grid_spec=pltpu.PrefetchScalarGridSpec(num_sca...  45.6 us
    pallas_call x1, Pallas kernels, reduce_call(): pl.pallas_call(functools.partial(reduce_kernel, sizes), in_specs=[vmem, v...  30.2 us
    pallas_call x1, Pallas kernels, small_call(): pl.pallas_call(functools.partial(small_kernel, sizes), in_specs=[pl.Block...  21.8 us
    another operation x6, other arithmetic  16.5 us
    unnamed x57, local copies, waits for them, and re-layouts  13.6 us
    concatenate x1, other arithmetic, shards(): jnp.concatenate([piece.reshape(tree_count, -1) for piece in grad_pieces],...  8.38 us

profile of v4, /device:TPU:0, one launch (start us, length us, event | category | flops | bytes accessed | tf_op | source)
XLA Modules:
  0.0 387.0 jit_solution(7281926127317249234)
XLA Ops:
  3.5 1.8 reshape.745.adapters_ref
  6.6 21.8 %small_gather.1 = (bf16[2,4,16,1824]{3,2,1,0:T(8,128)(2,1)}, bf16[4,16,384]{2,1,0:T(8,128)(2,1)}, f32[4,8,640]{2,1,0:T(8,128)}) custom-call(s32[1]{0:T(128)S(6)} %copy.207.ids_ref, bf16[32,1824]{1,0:T(8,128)(2,1)} %reshape.745.adapters_ref, bf16[16,384]{1,0:T(8,128)(2,1)} %broadcast_in_dim.41.gains_ref, f32[8,640]{1,0:T(8,128)} %maximum_maximum_fusion.table_ref), custom_call_target="tpu_custom_call" | custom-call | tf_op jit(solution)/shard_map/small_gather/pallas_call | solution.py:1637
  28.4 1.1 convert_bitcast_fusion
  29.5 1.4 reshape.768
  34.6 4.6 %fusion.2 = (f32[2560,32]{1,0:T(8,128)S(1)}, f32[2560,32]{1,0:T(8,128)S(1)}, f32[2560,32]{1,0:T(8,128)S(1)}) fusion(f32[32]{0:T(128)S(1)} %multiply_power_fusion, f32[2560]{0:T(1024)S(1)} %add_convert_fusion), kind=kLoop, calls=%fused_computation.14 | loop fusion | flops 163840 | bytes 993408 | tf_op jit(solution)/shard_map/neg | solution.py:1743
  39.3 3.6 pad_maximum_fusion
  50.8 0.9 slice_reduce_fusion.5
  52.4 15.3 %convert_convert_fusion = bf16[2560,13]{1,0:T(8,128)(2,1)S(1)} fusion(s32[2560]{0:T(1024)S(1)} %broadcast_add_fusion.2), kind=kLoop, calls=%fused_computation.6 | loop fusion | flops 133120 | bytes 76800 | tf_op jit(solution)/shard_map/convert.25
  67.7 1.0 pad.43.hot
  68.7 1.1 copy.175
  70.5 104.0 %forward.1 = (bf16[2560,768]{1,0:T(8,128)(2,1)}, bf16[2560,384]{1,0:T(8,128)(2,1)}, bf16[2560,384]{1,0:T(8,128)(2,1)}, bf16[768,1152]{1,0:T(8,128)(2,1)}, bf16[7...) custom-call(bf16[640,768]{1,0:T(8,128)(2,1)} %bitcast.117, ...), custom_call_target="tpu_custom_call" | custom-call | tf_op jit(solution)/shard_map/forward/pallas_call | solution.py:872
  179.1 1.2 bitcast_select_fusion
  181.1 1.5 copy.149
  183.2 7.5 %copy.188 = bf16[2,768,2,1024]{3,1,2,0:T(8,128)(2,1)} copy(bf16[2,768,2,1024]{3,2,1,0:T(2,128)(2,1)} %param.33) | data formatting | bytes 12582912 | tf_op args[7]
  190.6 45.6 %experts.1 = (bf16[2560,768]{1,0:T(8,128)(2,1)}, bf16[2560,768]{1,0:T(8,128)(2,1)}) custom-call(s32[2,21]{1,0:T(2,128)} %pad_add_fusion.1.spans, s32[2,1,2560]{2,1,0:T(1,128)} %copy_select_fusion.place_row, f32[2,1,2560]{2,1,0:T(1,128)} %broadcast_in_dim.49.weight_row, s32[2560,2]{1,0:T(8,128)} %bitcast.115, f32[2560,2]{1,0:T(8,128)} %bitcast.116, ...), custom_call_target="tpu_custom_call" | custom-call | tf_op jit(solution)/shard_map/experts/pallas_call | solution.py:256
  237.7 98.5 %backward.1 = (f32[640,768]{1,0:T(8,128)}, f32[640,768]{1,0:T(8,128)}, f32[48,768]{1,0:T(8,128)}, f32[48,384]{1,0:T(8,128)}, f32[16,384]{1,0:T(8,128)}, /*index=5*/f32[16,768]{1,0:T(8,128)}) custom-call(bf16[2560,768]{1,0:T(8,128)(2,1)} %get-tuple-element.98.moe_out, bf16[2560,768]{1,0:T(8,128)(2,1)} %get-tuple-element.99.moe_back, ...), custom_call_target="tpu_custom_call" | custom-call | tf_op jit(solution)/shard_map/backward/pallas_call | solution.py:1440
  336.2 1.1 copy.166
  341.1 8.4 %reduce.44 = f32[233472]{0:T(1024)S(1)} reduce(f32[1,233472]{1,0:T(1,128)S(1)} %constant_dynamic-update-slice_fusion.4, f32[]{:T(128)} %broadcast.497), dimensions={0}, to_apply=%constant_dynamic-update-slice_fusion.4.reduce_sub_computation | reduce | bytes 1867780 | tf_op jit(solution)/shard_map/concatenate | solution.py:1857
  349.5 1.6 reshape_squeeze.3.packed
  351.1 30.2 %adapter_sums.1 = f32[2,16,1824]{2,1,0:T(8,128)} custom-call(f32[4,2,16,1824]{3,2,1,0:T(8,128)} %reshape_squeeze.3.packed, f32[4,8,640]{2,1,0:T(8,128)} %get-tuple-element.93.table_all), custom_call_target="tpu_custom_call" | custom-call | tf_op jit(solution)/shard_map/adapter_sums/pallas_call | solution.py:1558
  381.3 1.9 reshape.766
  383.3 1.3 copy.208
  384.5 1.0 copy-done.1
  385.5 1.3 copy.209
  (161 shorter events, 27.4 us)
Async XLA Ops:
  31.9 1.6 copy-start.16
  31.9 2.0 copy-start.17
  32.0 7.3 %copy-start.4 = (bf16[96,1152]{1,0:T(8,128)(2,1)}, bf16[96,1152]{1,0:T(8,128)(2,1)S(1)}, u32[]{:S(2)}) copy-start(bf16[96,1152]{1,0:T(8,128)(2,1)S(1)} %constant_dynamic-update-slice_fusion.b_qkv2) | copy-start | bytes 663556
  46.7 22.0 %copy-start.7 = (bf16[32,768]{1,0:T(8,128)(2,1)}, bf16[32,768]{1,0:T(8,128)(2,1)S(1)}, u32[]{:S(2)}) copy-start(bf16[32,768]{1,0:T(8,128)(2,1)S(1)} %constant_dynamic-update-slice_fusion.2.b_o2) | copy-start | bytes 147460
  49.3 20.4 %copy-start.3 = (bf16[768,32]{1,0:T(8,128)(2,1)}, bf16[768,32]{1,0:T(8,128)(2,1)S(1)}, u32[]{:S(2)}) copy-start(bf16[768,32]{1,0:T(8,128)(2,1)S(1)} %reshape.775.a_gu) | copy-start | bytes 147460
  49.3 19.3 %copy-start.5 = (bf16[192,2,1024]{2,1,0:T(2,128)(2,1)S(1)}, bf16[192,2,1024]{2,1,0:T(2,128)(2,1)}, u32[]{:S(2)}) copy-start(bf16[192,2,1024]{2,1,0:T(2,128)(2,1)} %param.31) | copy-start | bytes 2359300
  67.7 2.1 copy-start.6
  70.5 104.0 %copy-start.8 = (f32[4,8,640]{2,1,0:T(8,128)S(1)}, f32[4,8,640]{2,1,0:T(8,128)}, u32[]{:S(2)}) copy-start(f32[4,8,640]{2,1,0:T(8,128)} %get-tuple-element.93.table_all) | copy-start | bytes 245764
  190.6 46.3 %copy-start = (bf16[768,48]{1,0:T(8,128)(2,1)S(1)}, bf16[768,48]{1,0:T(8,128)(2,1)}, u32[]{:S(2)}) copy-start(bf16[768,48]{1,0:T(8,128)(2,1)} %reshape.773.a_qkv) | copy-start | bytes 221188
  336.2 1.6 copy-start.11
  336.2 1.8 copy-start.15
  337.7 0.8 copy-start.14
  337.7 0.9 copy-start.10
  338.1 0.9 copy-start.9
  338.6 0.9 copy-start.12
  339.8 0.8 copy-start.13
  349.5 33.7 %copy-start.2 = (f32[640,768]{1,0:T(8,128)S(1)}, f32[640,768]{1,0:T(8,128)}, u32[]{:S(2)}) copy-start(f32[640,768]{1,0:T(8,128)} %get-tuple-element.113) | copy-start | bytes 5898244
  383.3 2.3 copy-start.1
